TPU v7x, 256 devices: a whole 4x4x8 slice. The times are simulated.
256 devices in a mesh: section: 2 (over core), group: 32 (over z, y), tp: 4 (over x).
Axes of the slice: x: 4, y: 4, z: 8, core: 2. Of those that a mesh axis runs over, the one named last changes fastest.
Arguments:
- resp_queries: bfloat16 [16384, 5120], P(('section', 'group', 'tp')), may hold values from -8 to 8
- resp_keys: bfloat16 [16384, 1024], P(('section', 'group', 'tp')), may hold values from -6 to 6
- resp_values: bfloat16 [16384, 1024], P(('section', 'group', 'tp')), may hold values from -6 to 6
- resp_dout: bfloat16 [16384, 5120], P(('section', 'group', 'tp')), may hold values from -6 to 6
- prompt_kv: bfloat16 [32, 2, 1024, 1024], P('group', None, None, 'tp'), may hold values from -8 to 8
- lengths: int32 [64], P(('section', 'group')), may hold values from 64 to 256, as said below
- owners: int32 [64], P(('section', 'group')), may hold values from 0 to 3
- visible_tiles: int32 [64, 8], P(('section', 'group')), may hold values from 0 to 1, as said below
Outputs:
- resp_dq: bfloat16 [16384, 5120], P(('section', 'group', 'tp'))
- resp_dk: bfloat16 [16384, 1024], P(('section', 'group', 'tp'))
- resp_dv: bfloat16 [16384, 1024], P(('section', 'group', 'tp'))
- prompt_grads: bfloat16 [32, 2, 1024, 1024], P('group', None, 'section', 'tp')
Inputs may be any that keep to these rules, and one draw needn't show every extreme that they name: Response j lies on section index j // 32 and group index g = j mod 32 and belongs to the prompt on group index (g - owners[j]) mod 32. `lengths`: rows of a response at or past its length are padding; some response fills all 256 slots. `visible_tiles`: tile 0 of a prompt is visible to every response.
All inputs are finite; a program needn't handle non-finite values.
Results may differ from a plain program's by a relative error of at most 0.04.
Values may be sent and summed in bfloat16 or wider, within the bound.
No kernel may reach another device: no remote copies, remote signals or barrier semaphores. Data moves between devices by JAX's collectives and lax.ppermute only.
A program may use at most 128 MiB of HBM per device.

v0:
```python
import functools

import jax
import jax.numpy as jnp
from jax import lax
from jax.experimental import pallas as pl
from jax.experimental.pallas import tpu as pltpu
from jax.sharding import PartitionSpec as P

HEADS = 40
KV_HEADS = 8
HEAD_DIM = 128
PTILE = 128
WIN = 4
PER_KV = HEADS // KV_HEADS
CHUNKS = 2
ROW = 4

MASKED = -1e30
SCALING = HEAD_DIM ** (-0.5)
LOG2E = 1.4426950408889634
VMEM_LIMIT = 48 * 1024 * 1024

TP, SECTION, LENGTH, OWNER, VISIBLE = 0, 1, 2, 3, 4


def shifted(block, axis, distance):
    devices = range(lax.axis_size(axis))
    route = [((i - distance) % len(devices), i) for i in devices]
    return lax.ppermute(block, axis, route)


def after(block, earlier):
    return lax.optimization_barrier((block, earlier))[0]


def along_row(block, distance):
    count = lax.axis_size("group")
    route = [(i - i % ROW + (i - distance) % ROW, i) for i in range(count)]
    return lax.ppermute(block, "group", route)


def to_row(block, distance):
    return shifted(block, "group", distance * ROW)


def whole():
    return pl.BlockSpec(memory_space=pltpu.VMEM)


def scalars():
    return pl.BlockSpec(memory_space=pltpu.SMEM)


def small_call(kernel, name, out_shape, in_specs):
    return pl.pallas_call(
        kernel,
        out_shape=out_shape,
        in_specs=in_specs,
        out_specs=jax.tree.map(lambda _: whole(), out_shape),
        compiler_params=pltpu.CompilerParams(vmem_limit_bytes=VMEM_LIMIT),
        name=name,
    )


def halves_kernel(section, prompt, *parts):
    half, cols = parts[0].shape[1:]
    rows = pl.ds(pl.multiple_of(section[0] * half, half), half)
    for chunk, part in enumerate(parts):
        part[...] = prompt[0, :, rows, chunk * cols : (chunk + 1) * cols]


def sends_kernel(place, own, before, *sends):
    for offset, send in enumerate(sends, 1):

        @pl.when(place[0] + offset >= ROW)
        def _(send=send):
            send[...] = before[...]

        @pl.when(place[0] + offset < ROW)
        def _(send=send):
            send[...] = own[...]


def pick_kernel(which, *refs):
    choices, chosen = refs[:-1], refs[-1]
    for offset, choice in enumerate(choices):

        @pl.when(which[0] == offset)
        def _(choice=choice):
            chosen[...] = choice[...]


def pack_kernel(tp, queries, grad_out, keys, values, *packs):
    tp_count = len(packs)
    for d, pack in enumerate(packs):
        device, at = lax.rem(tp[0] + d, tp_count), 0
        for chunk in range(CHUNKS):
            for source in (queries, grad_out, keys, values):
                cols = source.shape[1] // tp_count
                part = cols // CHUNKS
                start = pl.multiple_of(device * cols + chunk * part, 128)
                pack[:, at : at + part] = source[:, pl.ds(start, part)]
                at += part


def unpack_kernel(tp, *refs):
    packs, (grad_q, grad_k, grad_v) = refs[:-3], refs[-3:]
    tp_count = len(packs)
    q_cols = grad_q.shape[1] // tp_count
    k_cols = grad_k.shape[1] // tp_count
    q_part, k_part = q_cols // CHUNKS, k_cols // CHUNKS
    for d, pack in enumerate(packs):
        device, at = lax.rem(tp[0] + d, tp_count), 0
        for chunk in range(CHUNKS):
            q_at = pl.ds(pl.multiple_of(device * q_cols + chunk * q_part, 128), q_part)
            k_at = pl.ds(pl.multiple_of(device * k_cols + chunk * k_part, 128), k_part)
            grad_q[:, q_at] = pack[:, at : at + q_part]
            at += q_part
            grad_k[:, k_at] = pack[:, at : at + k_part]
            at += k_part
            grad_v[:, k_at] = pack[:, at : at + k_part]
            at += k_part


def place(index, tp, tp_count, rows):
    block = index // rows
    return lax.rem(tp - block + tp_count, tp_count) * rows + lax.rem(index, rows)


def attend_kernel(chunk, tp_count, meta, *refs):
    packs, refs = refs[:tp_count], refs[tp_count:]
    earlier, refs = refs[: tp_count if chunk else 0], refs[tp_count if chunk else 0 :]
    offers, other, refs = refs[:WIN], refs[WIN], refs[WIN + 1 :]
    backs, refs = refs[:tp_count], refs[tp_count:]
    own_grad, other_grad = refs[:2]
    q_all, do_all, keys, values, keys_t, bias, scores, grad_prob, weights, grad_scores, dk, dv = refs[
        2:
    ]
    rows = packs[0].shape[0]
    resp = rows * tp_count
    half, k_cols = other.shape[1:]
    kv_heads = k_cols // HEAD_DIM
    prompt_len = 2 * half
    total = prompt_len + resp
    per_half = half // PTILE
    q_cols = kv_heads * PER_KV * HEAD_DIM
    tp, section, length, owner = meta[TP], meta[SECTION], meta[LENGTH], meta[OWNER]
    taken = chunk * 2 * (q_cols + k_cols)
    given = chunk * (q_cols + 2 * k_cols)
    for back, block in zip(backs, earlier):
        back[:, :given] = block[...]

    key_at = place(lax.broadcasted_iota(jnp.int32, (resp, resp), 0), tp, tp_count, rows)
    row_at = place(lax.broadcasted_iota(jnp.int32, (resp, resp), 1), tp, tp_count, rows)
    bias[...] = jnp.where(key_at <= row_at, 0.0, MASKED)
    live = (
        place(lax.broadcasted_iota(jnp.int32, (1, resp), 1), tp, tp_count, rows) < length
    ).astype(jnp.float32)
    tile_bias = []
    for tile in range(2 * per_half):
        side = section if tile < per_half else 1 - section
        visible = meta[VISIBLE + side * per_half + tile % per_half]
        tile_bias.append(jnp.where(visible == 1, 0.0, MASKED))

    nt = (((1,), (1,)), ((), ()))
    for kv in range(kv_heads):
        at = slice(kv * HEAD_DIM, (kv + 1) * HEAD_DIM)
        for offset, offer in enumerate(offers):

            @pl.when(owner == offset)
            def _(offer=offer):
                keys[:half] = offer[0, :, at]
                values[:half] = offer[1, :, at]

        keys[half:prompt_len] = other[0, :, at]
        values[half:prompt_len] = other[1, :, at]
        for i in range(tp_count):
            here = slice(i * rows, (i + 1) * rows)
            there = slice(prompt_len + i * rows, prompt_len + (i + 1) * rows)
            k_from = taken + 2 * q_cols + kv * HEAD_DIM
            keys[there] = packs[i][:, k_from : k_from + HEAD_DIM]
            values[there] = packs[i][:, k_from + k_cols : k_from + k_cols + HEAD_DIM]
            for head in range(PER_KV):
                q_from = taken + (kv * PER_KV + head) * HEAD_DIM
                q_all[head, here] = packs[i][:, q_from : q_from + HEAD_DIM]
                do_all[head, here] = packs[i][:, q_cols + q_from : q_cols + q_from + HEAD_DIM]
        keys_t[...] = keys[...].T
        dk[...] = jnp.zeros_like(dk)
        dv[...] = jnp.zeros_like(dv)

        for head in range(PER_KV):
            query = q_all[head]
            cotangent = do_all[head]
            tops = []
            for tile in range(total // PTILE):
                span = slice(tile * PTILE, (tile + 1) * PTILE)
                part = lax.dot_general(
                    keys[span], query, nt, preferred_element_type=jnp.float32
                )
                if tile >= 2 * per_half:
                    low = (tile - 2 * per_half) * PTILE
                    part = part + bias[low : low + PTILE]
                scores[span] = part
                top = jnp.max(part.reshape(PTILE // 8, 8, resp), axis=0)
                if tile < 2 * per_half:
                    top = top + tile_bias[tile]
                tops.append(top)
                grad_prob[span] = lax.dot_general(
                    values[span], cotangent, nt, preferred_element_type=jnp.float32
                )
            largest = jnp.max(functools.reduce(jnp.maximum, tops), axis=0, keepdims=True)
            factor = SCALING * LOG2E
            sums = jnp.zeros((8, resp), jnp.float32)
            dots = jnp.zeros((8, resp), jnp.float32)
            for tile in range(total // PTILE):
                span = slice(tile * PTILE, (tile + 1) * PTILE)
                shift = largest
                if tile < 2 * per_half:
                    shift = shift - tile_bias[tile]
                exponent = jnp.exp2((scores[span] - shift) * factor)
                scores[span] = exponent
                sums += jnp.sum(exponent.reshape(PTILE // 8, 8, resp), axis=0)
                dots += jnp.sum((exponent * grad_prob[span]).reshape(PTILE // 8, 8, resp), axis=0)
            inverse = 1.0 / jnp.sum(sums, axis=0, keepdims=True)
            row_delta = jnp.sum(dots, axis=0, keepdims=True) * inverse
            inverse = inverse * live
            for tile in range(total // PTILE):
                span = slice(tile * PTILE, (tile + 1) * PTILE)
                probabilities = scores[span] * inverse
                weights[span] = probabilities.astype(jnp.bfloat16)
                grad_scores[span] = (probabilities * (grad_prob[span] - row_delta)).astype(
                    jnp.bfloat16
                )
            dv[...] += jnp.dot(weights[...], cotangent, preferred_element_type=jnp.float32)
            dk[...] += jnp.dot(grad_scores[...], query, preferred_element_type=jnp.float32)
            grad_query_t = jnp.dot(
                keys_t[...], grad_scores[...], preferred_element_type=jnp.float32
            )
            grad_query = (grad_query_t.T * SCALING).astype(jnp.bfloat16)
            q_from = given + (kv * PER_KV + head) * HEAD_DIM
            for i in range(tp_count):
                backs[i][:, q_from : q_from + HEAD_DIM] = grad_query[i * rows : (i + 1) * rows]

        own_grad[0, :, at] = (dk[:half] * SCALING).astype(jnp.bfloat16)
        other_grad[0, :, at] = (dk[half:prompt_len] * SCALING).astype(jnp.bfloat16)
        own_grad[1, :, at] = dv[:half].astype(jnp.bfloat16)
        other_grad[1, :, at] = dv[half:prompt_len].astype(jnp.bfloat16)
        for i in range(tp_count):
            k_from = given + q_cols + kv * HEAD_DIM
            v_from = k_from + k_cols
            span = slice(prompt_len + i * rows, prompt_len + (i + 1) * rows)
            backs[i][:, k_from : k_from + HEAD_DIM] = (dk[span] * SCALING).astype(jnp.bfloat16)
            backs[i][:, v_from : v_from + HEAD_DIM] = dv[span].astype(jnp.bfloat16)


def attend(chunk, meta, packs, earlier, offers, other):
    tp_count, rows = len(packs), packs[0].shape[0]
    resp = rows * tp_count
    half, k_cols = other.shape[1:]
    kv_heads = k_cols // HEAD_DIM
    q_cols = kv_heads * PER_KV * HEAD_DIM
    total = 2 * half + resp
    f32, bf16 = jnp.float32, jnp.bfloat16
    flops = 10 * resp * total * kv_heads * PER_KV * HEAD_DIM
    results = pl.pallas_call(
        functools.partial(attend_kernel, chunk, tp_count),
        out_shape=[
            jax.ShapeDtypeStruct((rows, (chunk + 1) * (q_cols + 2 * k_cols)), bf16)
        ]
        * tp_count
        + [jax.ShapeDtypeStruct(other.shape, bf16)] * 2,
        in_specs=[scalars()] + [whole()] * (tp_count + len(earlier) + len(offers) + 1),
        out_specs=[whole()] * (tp_count + 2),
        scratch_shapes=[
            pltpu.VMEM((PER_KV, resp, HEAD_DIM), bf16),
            pltpu.VMEM((PER_KV, resp, HEAD_DIM), bf16),
            pltpu.VMEM((total, HEAD_DIM), bf16),
            pltpu.VMEM((total, HEAD_DIM), bf16),
            pltpu.VMEM((HEAD_DIM, total), bf16),
            pltpu.VMEM((resp, resp), f32),
            pltpu.VMEM((total, resp), f32),
            pltpu.VMEM((total, resp), f32),
            pltpu.VMEM((total, resp), bf16),
            pltpu.VMEM((total, resp), bf16),
            pltpu.VMEM((total, HEAD_DIM), f32),
            pltpu.VMEM((total, HEAD_DIM), f32),
        ],
        compiler_params=pltpu.CompilerParams(vmem_limit_bytes=VMEM_LIMIT),
        cost_estimate=pl.CostEstimate(
            flops=flops, bytes_accessed=6 * 1024 * 1024, transcendentals=flops // 1280
        ),
        name="attend",
    )(meta, *packs, *earlier, *offers, other)
    return results[:tp_count], results[tp_count], results[tp_count + 1]


def shards(
    resp_queries, resp_keys, resp_values, resp_dout, prompt_kv, lengths, owners, visible_tiles
):
    tp_count = lax.axis_size("tp")
    tp = lax.axis_index("tp").astype(jnp.int32)[None]
    section = lax.axis_index("section").astype(jnp.int32)[None]
    at_row = lax.rem(lax.axis_index("group").astype(jnp.int32), ROW)
    rows = resp_queries.shape[0]
    half = prompt_kv.shape[2] // 2
    k_part = prompt_kv.shape[3] // CHUNKS
    pack_cols = 2 * (resp_queries.shape[1] + resp_keys.shape[1]) // tp_count
    bf16, f32 = jnp.bfloat16, jnp.float32
    part = jax.ShapeDtypeStruct((2, half, k_part), bf16)

    meta = jnp.concatenate([tp, section, lengths, owners, visible_tiles[0]])
    halves = small_call(
        halves_kernel,
        "halves",
        [part] * CHUNKS,
        [scalars(), whole()],
    )(section, prompt_kv)
    sibling_owner = shifted(after(owners, halves), "section", 1)
    packs = small_call(
        pack_kernel,
        "pack",
        [jax.ShapeDtypeStruct((rows, pack_cols), bf16)] * tp_count,
        [scalars()] + [whole()] * 4,
    )(after(tp, sibling_owner), resp_queries, resp_dout, resp_keys, resp_values)
    arrived = {d: shifted(packs[d], "tp", d) for d in range(1, tp_count, 2)}
    for d in range(2, tp_count, 2):
        arrived[d] = shifted(after(packs[d], arrived), "tp", d)
    arrived = [packs[0]] + [arrived[d] for d in range(1, tp_count)]

    before = [to_row(block, 1) for block in halves]
    sends = [
        list(
            small_call(sends_kernel, "sends", [part] * (WIN - 1), [scalars()] + [whole()] * 2)(
                after(at_row[None], packs), halves[c], before[c]
            )
        )
        for c in range(CHUNKS)
    ]
    sends[0][1] = after(sends[0][1], sends[1])
    offers = []
    for c in range(CHUNKS):
        offer = {0: halves[c]}
        for offset in (1, 3, 2):
            send = sends[c][offset - 1]
            if c:
                send = after(send, offers[c - 1][offset])
            offer[offset] = along_row(send, offset)
        offers.append([offer[offset] for offset in range(WIN)])

    backs, shares, passing, ringed, terms = [], [], [], {}, []
    for c in range(CHUNKS):
        wanted = small_call(pick_kernel, "pick", part, [scalars()] + [whole()] * WIN)(
            sibling_owner, *offers[c]
        )
        other = shifted(wanted, "section", 1)
        other = after(other, terms)
        backs, own_grad, other_grad = attend(c, meta, arrived, backs, offers[c], other)
        sibling_grad = shifted(other_grad, "section", 1)
        terms = []
        for offset in range(WIN):
            term = jnp.where(owners[0] == offset, own_grad.astype(f32), 0.0) + jnp.where(
                sibling_owner[0] == offset, sibling_grad.astype(f32), 0.0
            )
            terms.append(term if offset == 0 else term.astype(bf16))
        terms = lax.optimization_barrier(terms)
        for offset in (1, 3, 2):
            term = after(terms[offset], ringed[offset]) if c else terms[offset]
            ringed[offset] = along_row(term, -offset)
        kept, passed = terms[0], jnp.zeros(part.shape, f32)
        for offset in range(1, WIN):
            term = ringed[offset].astype(f32)
            crossing = at_row + offset >= ROW
            kept = kept + jnp.where(crossing, 0.0, term)
            passed = passed + jnp.where(crossing, term, 0.0)
        passed = passed.astype(bf16)
        passing.append(passed)
        shares.append((kept + to_row(passed, -1).astype(f32)).astype(bf16))
    backs = after(backs, passing[0])
    returned = [backs[0]] + [shifted(backs[d], "tp", -d) for d in range(1, tp_count)]

    grads = small_call(
        unpack_kernel,
        "unpack",
        [
            jax.ShapeDtypeStruct(resp_queries.shape, bf16),
            jax.ShapeDtypeStruct(resp_keys.shape, bf16),
            jax.ShapeDtypeStruct(resp_values.shape, bf16),
        ],
        [scalars()] + [whole()] * tp_count,
    )(tp, *returned)
    return (grads[0], grads[1], grads[2], jnp.concatenate(shares, -1)[None])


def solution(mesh):
    placed = (
        P(("section", "group", "tp"), None),
        P(("section", "group", "tp"), None),
        P(("section", "group", "tp"), None),
        P(("section", "group", "tp"), None),
        P("group", None, None, "tp"),
        P(("section", "group")),
        P(("section", "group")),
        P(("section", "group"), None),
    )
    return jax.shard_map(
        shards,
        mesh=mesh,
        in_specs=placed,
        out_specs=(
            P(("section", "group", "tp"), None),
            P(("section", "group", "tp"), None),
            P(("section", "group", "tp"), None),
            P("group", None, "section", "tp"),
        ),
        check_vma=False,
    )
```

profile of v0, /device:TPU:24, one launch (start us, length us, event | category | flops | bytes accessed | tf_op | source)
XLA Modules:
  0.0 104.6 jit_solution(11633663703057730827)
XLA Ops:
  0.6 1.2 %copy-done = bf16[1,2,1024,256]{3,2,1,0:T(8,128)(2,1)S(1)} copy-done((bf16[1,2,1024,256]{3,2,1,0:T(8,128)(2,1)S(1)}, bf16[1,2,1024,256]{3,2,1,0:T(8,128)(2,1)}, u32[]{:S(2)}) %copy-start) | copy-done | bytes 1048600
  2.0 2.0 %collective-permute-start.4 = (bf16[2,512,128]{2,1,0:T(8,128)(2,1)S(1)}, bf16[2,512,128]{2,1,0:T(8,128)(2,1)S(1)}, u32[]{:S(2)}, u32[]{:S(2)}) collective-permute-start(bf16[2,512,128]{2,1,0:T(8,128)(2,1)S(1)} %get-tuple-element.55.own.refs_0_.refs_4_), channel_id=1, source_target_pairs={{112,0},{116,4},{120,8},{124,12},{0,16},{4,20},{8,24},{12,28},{16,... | collective-permute-start | bytes 786440 | tf_op jit(solution)/shard_map/ppermute | solution.py:30
  4.0 1.9 %collective-permute-start.6 = (bf16[2,512,128]{2,1,0:T(8,128)(2,1)S(1)}, bf16[2,512,128]{2,1,0:T(8,128)(2,1)S(1)}, u32[]{:S(2)}, u32[]{:S(2)}) collective-permute-start(bf16[2,512,128]{2,1,0:T(8,128)(2,1)S(1)} %get-tuple-element.56.own.refs_0_.refs_8_), channel_id=1, source_target_pairs={{112,0},{116,4},{120,8},{124,12},{0,16},{4,20},{8,24},{12,28},{16,... | collective-permute-start | bytes 786440 | tf_op jit(solution)/shard_map/ppermute | solution.py:30
  5.9 1.4 %collective-permute-done.which = s32[1]{0:T(128)} collective-permute-done((s32[1]{0:T(128)}, s32[1]{0:T(128)}, u32[]{:S(2)}, u32[]{:S(2)}) %collective-permute-start) | collective-permute-done | bytes 36 | tf_op jit(solution)/shard_map/ppermute | solution.py:30
  7.3 1.1 %copy-done.2 = bf16[64,5120]{1,0:T(8,128)(2,1)S(1)} copy-done((bf16[64,5120]{1,0:T(8,128)(2,1)S(1)}, bf16[64,5120]{1,0:T(8,128)(2,1)}, u32[]{:S(2)}) %copy-start.2) | copy-done | bytes 655384
  8.4 1.0 pack.1
  9.4 1.5 %collective-permute-start.1 = (bf16[64,3072]{1,0:T(8,128)(2,1)}, bf16[64,3072]{1,0:T(8,128)(2,1)S(1)}, u32[]{:S(2)}, u32[]{:S(2)}) collective-permute-start(bf16[64,3072]{1,0:T(8,128)(2,1)} %get-tuple-element.60), channel_id=1, source_target_pairs={{3,0},{0,1},{1,2},{2,3},{7,4},{4,5},{5,6},{6,7},{11,8},{8,9},{9,10... | collective-permute-start | bytes 1179656 | tf_op jit(solution)/shard_map/ppermute | solution.py:30
  10.9 1.7 %collective-permute-start.2 = (bf16[64,3072]{1,0:T(8,128)(2,1)S(1)}, bf16[64,3072]{1,0:T(8,128)(2,1)S(1)}, u32[]{:S(2)}, u32[]{:S(2)}) collective-permute-start(bf16[64,3072]{1,0:T(8,128)(2,1)S(1)} %get-tuple-element.62), channel_id=1, source_target_pairs={{1,0},{2,1},{3,2},{0,3},{5,4},{6,5},{7,6},{4,7},{9,8},{10,9},{11,1... | collective-permute-start | bytes 1179656 | tf_op jit(solution)/shard_map/ppermute | solution.py:30
  12.6 2.4 %collective-permute-done.4.before = bf16[2,512,128]{2,1,0:T(8,128)(2,1)S(1)} collective-permute-done((bf16[2,512,128]{2,1,0:T(8,128)(2,1)S(1)}, bf16[2,512,128]{2,1,0:T(8,128)(2,1)S(1)}, u32[]{:S(2)}, u32[]{:S(2)}) %collective-permute-start.4) | collective-permute-done | bytes 262176 | tf_op jit(solution)/shard_map/ppermute | solution.py:30
  15.1 0.3 collective-permute-start.5
  15.4 4.4 %collective-permute-done.6.before = bf16[2,512,128]{2,1,0:T(8,128)(2,1)S(1)} collective-permute-done((bf16[2,512,128]{2,1,0:T(8,128)(2,1)S(1)}, bf16[2,512,128]{2,1,0:T(8,128)(2,1)S(1)}, u32[]{:S(2)}, u32[]{:S(2)}) %collective-permute-start.6) | collective-permute-done | bytes 262176 | tf_op jit(solution)/shard_map/ppermute | solution.py:30
  19.9 1.3 %collective-permute-start.7 = (bf16[2,512,128]{2,1,0:T(8,128)(2,1)S(1)}, bf16[2,512,128]{2,1,0:T(8,128)(2,1)S(1)}, u32[]{:S(2)}, u32[]{:S(2)}) collective-permute-start(bf16[2,512,128]{2,1,0:T(8,128)(2,1)S(1)} %get-tuple-element.70), channel_id=1, source_target_pairs={{8,0},{12,4},{0,8},{4,12},{24,16},{28,20},{16,24},{20,28},{40,32},... | collective-permute-start | bytes 786440 | tf_op jit(solution)/shard_map/ppermute | solution.py:40
  21.2 0.8 collective-permute-done.1.refs_1_
  22.0 2.5 %collective-permute-start.3 = (bf16[64,3072]{1,0:T(8,128)(2,1)}, bf16[64,3072]{1,0:T(8,128)(2,1)S(1)}, u32[]{:S(2)}, u32[]{:S(2)}) collective-permute-start(bf16[64,3072]{1,0:T(8,128)(2,1)} %get-tuple-element.63), channel_id=1, source_target_pairs={{2,0},{3,1},{0,2},{1,3},{6,4},{7,5},{4,6},{5,7},{10,8},{11,9},{8,1... | collective-permute-start | bytes 1179656 | tf_op jit(solution)/shard_map/ppermute | solution.py:30
  24.6 6.2 %collective-permute-done.7.refs_2_.refs_6_ = bf16[2,512,128]{2,1,0:T(8,128)(2,1)S(1)} collective-permute-done((bf16[2,512,128]{2,1,0:T(8,128)(2,1)S(1)}, bf16[2,512,128]{2,1,0:T(8,128)(2,1)S(1)}, u32[]{:S(2)}, u32[]{:S(2)}) %collective-permute-start.7) | collective-permute-done | bytes 262176 | tf_op jit(solution)/shard_map/ppermute | solution.py:40
  30.8 3.8 %collective-permute-done.8.refs_3_.refs_7_ = bf16[2,512,128]{2,1,0:T(8,128)(2,1)S(1)} collective-permute-done((bf16[2,512,128]{2,1,0:T(8,128)(2,1)S(1)}, bf16[2,512,128]{2,1,0:T(8,128)(2,1)S(1)}, u32[]{:S(2)}, u32[]{:S(2)}) %collective-permute-start.8) | collective-permute-done | bytes 262176 | tf_op jit(solution)/shard_map/ppermute | solution.py:40
  34.6 0.7 pick.2
  36.8 0.6 copy-done.8
  37.5 0.6 collective-permute-start.10
  38.1 1.2 %collective-permute-start.11 = (bf16[2,512,128]{2,1,0:T(8,128)(2,1)}, bf16[2,512,128]{2,1,0:T(8,128)(2,1)S(1)}, u32[]{:S(2)}, u32[]{:S(2)}) collective-permute-start(bf16[2,512,128]{2,1,0:T(8,128)(2,1)} %copy-done.5), channel_id=1, source_target_pairs={{8,0},{12,4},{0,8},{4,12},{24,16},{28,20},{16,24},{20,28},{40,32},... | collective-permute-start | bytes 786440 | tf_op jit(solution)/shard_map/ppermute | solution.py:40
  39.3 0.8 collective-permute-start.12
  40.1 8.7 %attend.2 = (bf16[64,896]{1,0:T(8,128)(2,1)S(1)}, bf16[64,896]{1,0:T(8,128)(2,1)S(1)}, bf16[64,896]{1,0:T(8,128)(2,1)S(1)}, bf16[64,896]{1,0:T(8,128)(2,1)S(1)},...) custom-call(s32[12]{0:T(128)S(1)} %concatenate.6.meta, ...), custom_call_target="tpu_custom_call" | custom-call | flops 2097152000 | bytes 6291456 | tf_op jit(solution)/shard_map/attend/pallas_call | solution.py:266
  51.6 2.3 %collective-permute-done.12.refs_3_.refs_11_ = bf16[2,512,128]{2,1,0:T(8,128)(2,1)S(1)} collective-permute-done((bf16[2,512,128]{2,1,0:T(8,128)(2,1)S(1)}, bf16[2,512,128]{2,1,0:T(8,128)(2,1)S(1)}, u32[]{:S(2)}, u32[]{:S(2)}) %collective-permute-start.12) | collective-permute-done | bytes 262176 | tf_op jit(solution)/shard_map/ppermute | solution.py:40
  53.9 0.7 pick.3
  54.7 1.3 %fusion.22 = (bf16[2,512,128]{2,1,0:T(8,128)(2,1)}, bf16[2,512,128]{2,1,0:T(8,128)(2,1)}, bf16[2,512,128]{2,1,0:T(8,128)(2,1)}, f32[2,512,128]{2,1,0:T(8,128)}) fusion(bf16[2,512,128]{2,1,0:T(8,128)(2,1)S(1)} %get-tuple-element.79, bf16[2,512,128]{2,1,0:T(8,128)(2,1)S(1)} %collective-permute-done.14, pred[]{:T(512)} %bitcast.11, pred[]{:T(512)} %bitcast.10, ...), kind=kLoop, calls=%fused_computation.50 | loop fusion | flops 2228224 | bytes 1835016 | tf_op jit(solution)/shard_map/convert_element_type | solution.py:365
  55.9 2.3 %collective-permute-start.16 = (bf16[2,512,128]{2,1,0:T(8,128)(2,1)}, bf16[2,512,128]{2,1,0:T(8,128)(2,1)}, u32[]{:S(2)}, u32[]{:S(2)}) collective-permute-start(bf16[2,512,128]{2,1,0:T(8,128)(2,1)} %get-tuple-element.83), channel_id=1, source_target_pairs={{8,0},{12,4},{0,8},{4,12},{24,16},{28,20},{16,24},{20,28},{40,32},... | collective-permute-start | bytes 786440 | tf_op jit(solution)/shard_map/ppermute | solution.py:40
  58.2 2.0 %collective-permute-start.17 = (bf16[2,512,128]{2,1,0:T(8,128)(2,1)}, bf16[2,512,128]{2,1,0:T(8,128)(2,1)}, u32[]{:S(2)}, u32[]{:S(2)}) collective-permute-start(bf16[2,512,128]{2,1,0:T(8,128)(2,1)} %get-tuple-element.84), channel_id=1, source_target_pairs={{12,0},{0,4},{4,8},{8,12},{28,16},{16,20},{20,24},{24,28},{44,32},... | collective-permute-start | bytes 786440 | tf_op jit(solution)/shard_map/ppermute | solution.py:40
  60.3 8.4 %attend.3 = (bf16[64,1792]{1,0:T(8,128)(2,1)S(1)}, bf16[64,1792]{1,0:T(8,128)(2,1)S(1)}, bf16[64,1792]{1,0:T(8,128)(2,1)S(1)}, bf16[64,1792]{1,0:T(8,128)(2,1)S(...) custom-call(s32[12]{0:T(128)S(1)} %concatenate.6.meta, ...), custom_call_target="tpu_custom_call" | custom-call | flops 2097152000 | bytes 6291456 | tf_op jit(solution)/shard_map/attend/pallas_call | solution.py:266
  68.8 3.0 %collective-permute-done.15 = bf16[2,512,128]{2,1,0:T(8,128)(2,1)} collective-permute-done((bf16[2,512,128]{2,1,0:T(8,128)(2,1)}, bf16[2,512,128]{2,1,0:T(8,128)(2,1)}, u32[]{:S(2)}, u32[]{:S(2)}) %collective-permute-start.15) | collective-permute-done | bytes 262176 | tf_op jit(solution)/shard_map/ppermute | solution.py:40
  71.8 0.6 collective-permute-done.17
  72.4 1.3 %fusion.2 = bf16[2,512,128]{2,1,0:T(8,128)(2,1)S(1)} fusion(bf16[2,512,128]{2,1,0:T(8,128)(2,1)} %collective-permute-done.15, bf16[2,512,128]{2,1,0:T(8,128)(2,1)} %collective-permute-done.16, bf16[2,512,128]{2,1,0:T(8,128)(2,1)} %collective-permute-done.17, pred[]{:T(512)S(6)} %ge.14, pred[]{:T(512)S(6)} %ge.13, pred[]{:T(512)S(6)} %ge.12), kind=kLoop, calls=%fused_computation.30 | loop fusion | flops 1179648 | bytes 1048579 | tf_op jit(solution)/shard_map/convert_element_type | solution.py:376
  73.7 2.8 %collective-permute-start.18 = (bf16[64,1792]{1,0:T(8,128)(2,1)S(1)}, bf16[64,1792]{1,0:T(8,128)(2,1)S(1)}, u32[]{:S(2)}, u32[]{:S(2)}) collective-permute-start(bf16[64,1792]{1,0:T(8,128)(2,1)S(1)} %get-tuple-element.91), channel_id=1, source_target_pairs={{1,0},{2,1},{3,2},{0,3},{5,4},{6,5},{7,6},{4,7},{9,8},{10,9},{11,1... | collective-permute-start | bytes 688136 | tf_op jit(solution)/shard_map/ppermute | solution.py:30
  76.5 0.3 fusion.29
  76.8 0.7 collective-permute-start.23
  77.5 3.5 %collective-permute-start.24 = (bf16[2,512,128]{2,1,0:T(8,128)(2,1)S(1)}, bf16[2,512,128]{2,1,0:T(8,128)(2,1)S(1)}, u32[]{:S(2)}, u32[]{:S(2)}) collective-permute-start(bf16[2,512,128]{2,1,0:T(8,128)(2,1)S(1)} %get-tuple-element.103), channel_id=1, source_target_pairs={{8,0},{12,4},{0,8},{4,12},{24,16},{28,20},{16,24},{20,28},{40,32},... | collective-permute-start | bytes 786440 | tf_op jit(solution)/shard_map/ppermute | solution.py:40
  81.0 0.8 collective-permute-start.19
  81.8 0.9 collective-permute-start.20
  82.7 8.4 %collective-permute-done.19.refs_2_ = bf16[64,1792]{1,0:T(8,128)(2,1)S(1)} collective-permute-done((bf16[64,1792]{1,0:T(8,128)(2,1)S(1)}, bf16[64,1792]{1,0:T(8,128)(2,1)S(1)}, u32[]{:S(2)}, u32[]{:S(2)}) %collective-permute-start.19) | collective-permute-done | bytes 229408 | tf_op jit(solution)/shard_map/ppermute | solution.py:30
  91.1 1.4 %collective-permute-start.21 = (bf16[2,512,128]{2,1,0:T(8,128)(2,1)S(1)}, bf16[2,512,128]{2,1,0:T(8,128)(2,1)S(1)}, u32[]{:S(2)}, u32[]{:S(2)}) collective-permute-start(bf16[2,512,128]{2,1,0:T(8,128)(2,1)S(1)} %fusion.2), channel_id=1, source_target_pairs={{16,0},{20,4},{24,8},{28,12},{32,16},{36,20},{40,24},{44,28},{48,3... | collective-permute-start | bytes 786440 | tf_op jit(solution)/shard_map/ppermute | solution.py:30
  92.5 1.6 %collective-permute-done.20.refs_3_ = bf16[64,1792]{1,0:T(8,128)(2,1)S(1)} collective-permute-done((bf16[64,1792]{1,0:T(8,128)(2,1)S(1)}, bf16[64,1792]{1,0:T(8,128)(2,1)S(1)}, u32[]{:S(2)}, u32[]{:S(2)}) %collective-permute-start.20) | collective-permute-done | bytes 229408 | tf_op jit(solution)/shard_map/ppermute | solution.py:30
  94.1 1.0 unpack.1
  95.1 0.2 fusion.15
  95.3 1.5 %collective-permute-start.26 = (bf16[2,512,128]{2,1,0:T(8,128)(2,1)S(1)}, bf16[2,512,128]{2,1,0:T(8,128)(2,1)S(1)}, u32[]{:S(2)}, u32[]{:S(2)}) collective-permute-start(bf16[2,512,128]{2,1,0:T(8,128)(2,1)S(1)} %fusion.15), channel_id=1, source_target_pairs={{16,0},{20,4},{24,8},{28,12},{32,16},{36,20},{40,24},{44,28},{48,3... | collective-permute-start | bytes 786440 | tf_op jit(solution)/shard_map/ppermute | solution.py:30
  96.8 0.7 collective-permute-done.21
  97.4 1.3 %fusion.7 = bf16[2,512,128]{2,1,0:T(8,128)(2,1)S(1)} fusion(f32[2,512,128]{2,1,0:T(8,128)S(1)} %copy-done.7, bf16[2,512,128]{2,1,0:T(8,128)(2,1)} %collective-permute-done.15, bf16[2,512,128]{2,1,0:T(8,128)(2,1)} %collective-permute-done.16, bf16[2,512,128]{2,1,0:T(8,128)(2,1)} %collective-permute-done.17, ...), kind=kLoop, calls=%fused_computation.35 | loop fusion | flops 1572864 | bytes 1835011 | tf_op jit(solution)/shard_map/convert_element_type | solution.py:378
  98.7 4.8 %collective-permute-done.26 = bf16[2,512,128]{2,1,0:T(8,128)(2,1)S(1)} collective-permute-done((bf16[2,512,128]{2,1,0:T(8,128)(2,1)S(1)}, bf16[2,512,128]{2,1,0:T(8,128)(2,1)S(1)}, u32[]{:S(2)}, u32[]{:S(2)}) %collective-permute-start.26) | collective-permute-done | bytes 262176 | tf_op jit(solution)/shard_map/ppermute | solution.py:30
  103.6 0.2 fusion.12
  103.8 0.9 maximum_bitcast_fusion
  (41 shorter events, 0.8 us)
Async XLA Ops:
  0.6 1.2 %copy-start = (bf16[1,2,1024,256]{3,2,1,0:T(8,128)(2,1)S(1)}, bf16[1,2,1024,256]{3,2,1,0:T(8,128)(2,1)}, u32[]{:S(2)}) copy-start(bf16[1,2,1024,256]{3,2,1,0:T(8,128)(2,1)} %prompt.1) | copy-start | bytes 3145732
  1.9 5.4 %copy-start.1 = (bf16[64,5120]{1,0:T(8,128)(2,1)S(1)}, bf16[64,5120]{1,0:T(8,128)(2,1)}, u32[]{:S(2)}) copy-start(bf16[64,5120]{1,0:T(8,128)(2,1)} %queries.1) | copy-start | bytes 1966084
  1.9 5.4 %copy-start.3 = (bf16[64,1024]{1,0:T(8,128)(2,1)S(1)}, bf16[64,1024]{1,0:T(8,128)(2,1)}, u32[]{:S(2)}) copy-start(bf16[64,1024]{1,0:T(8,128)(2,1)} %keys.1) | copy-start | bytes 393220
  1.9 5.4 %copy-start.4 = (bf16[64,1024]{1,0:T(8,128)(2,1)S(1)}, bf16[64,1024]{1,0:T(8,128)(2,1)}, u32[]{:S(2)}) copy-start(bf16[64,1024]{1,0:T(8,128)(2,1)} %values.1) | copy-start | bytes 393220
  2.0 13.1 %collective-permute-start.4 = (bf16[2,512,128]{2,1,0:T(8,128)(2,1)S(1)}, bf16[2,512,128]{2,1,0:T(8,128)(2,1)S(1)}, u32[]{:S(2)}, u32[]{:S(2)}) collective-permute-start(bf16[2,512,128]{2,1,0:T(8,128)(2,1)S(1)} %get-tuple-element.55.own.refs_0_.refs_4_), channel_id=1, source_target_pairs={{112,0},{116,4},{120,8},{124,12},{0,16},{4,20},{8,24},{12,28},{16,... | collective-permute-start | bytes 786440 | tf_op jit(solution)/shard_map/ppermute | solution.py:30
  4.0 15.9 %collective-permute-start.6 = (bf16[2,512,128]{2,1,0:T(8,128)(2,1)S(1)}, bf16[2,512,128]{2,1,0:T(8,128)(2,1)S(1)}, u32[]{:S(2)}, u32[]{:S(2)}) collective-permute-start(bf16[2,512,128]{2,1,0:T(8,128)(2,1)S(1)} %get-tuple-element.56.own.refs_0_.refs_8_), channel_id=1, source_target_pairs={{112,0},{116,4},{120,8},{124,12},{0,16},{4,20},{8,24},{12,28},{16,... | collective-permute-start | bytes 786440 | tf_op jit(solution)/shard_map/ppermute | solution.py:30
  5.9 1.4 %collective-permute-start = (s32[1]{0:T(128)}, s32[1]{0:T(128)}, u32[]{:S(2)}, u32[]{:S(2)}) collective-permute-start(s32[1]{0:T(128)} %param.14), channel_id=1, source_target_pairs={{128,0},{0,128},{129,1},{1,129},{130,2},{2,130},{131,3},{3,131},{1... | collective-permute-start | bytes 20 | tf_op jit(solution)/shard_map/ppermute | solution.py:30
  7.3 1.1 %copy-start.2 = (bf16[64,5120]{1,0:T(8,128)(2,1)S(1)}, bf16[64,5120]{1,0:T(8,128)(2,1)}, u32[]{:S(2)}) copy-start(bf16[64,5120]{1,0:T(8,128)(2,1)} %grad_out.1) | copy-start | bytes 1966084
  9.4 12.6 %collective-permute-start.1 = (bf16[64,3072]{1,0:T(8,128)(2,1)}, bf16[64,3072]{1,0:T(8,128)(2,1)S(1)}, u32[]{:S(2)}, u32[]{:S(2)}) collective-permute-start(bf16[64,3072]{1,0:T(8,128)(2,1)} %get-tuple-element.60), channel_id=1, source_target_pairs={{3,0},{0,1},{1,2},{2,3},{7,4},{4,5},{5,6},{6,7},{11,8},{8,9},{9,10... | collective-permute-start | bytes 1179656 | tf_op jit(solution)/shard_map/ppermute | solution.py:30
  10.9 11.2 %collective-permute-start.2 = (bf16[64,3072]{1,0:T(8,128)(2,1)S(1)}, bf16[64,3072]{1,0:T(8,128)(2,1)S(1)}, u32[]{:S(2)}, u32[]{:S(2)}) collective-permute-start(bf16[64,3072]{1,0:T(8,128)(2,1)S(1)} %get-tuple-element.62), channel_id=1, source_target_pairs={{1,0},{2,1},{3,2},{0,3},{5,4},{6,5},{7,6},{4,7},{9,8},{10,9},{11,1... | collective-permute-start | bytes 1179656 | tf_op jit(solution)/shard_map/ppermute | solution.py:30
  15.1 9.4 %collective-permute-start.5 = (bf16[2,512,128]{2,1,0:T(8,128)(2,1)S(1)}, bf16[2,512,128]{2,1,0:T(8,128)(2,1)S(1)}, u32[]{:S(2)}, u32[]{:S(2)}) collective-permute-start(bf16[2,512,128]{2,1,0:T(8,128)(2,1)S(1)} %get-tuple-element.65), channel_id=1, source_target_pairs={{12,0},{0,4},{4,8},{8,12},{28,16},{16,20},{20,24},{24,28},{44,32},... | collective-permute-start | bytes 786440 | tf_op jit(solution)/shard_map/ppermute | solution.py:40
  19.9 15.4 %copy-start.5 = (bf16[2,512,128]{2,1,0:T(8,128)(2,1)}, bf16[2,512,128]{2,1,0:T(8,128)(2,1)S(1)}, u32[]{:S(2)}) copy-start(bf16[2,512,128]{2,1,0:T(8,128)(2,1)S(1)} %get-tuple-element.77) | copy-start | bytes 786436
  19.9 15.4 %copy-start.6 = (bf16[2,512,128]{2,1,0:T(8,128)(2,1)}, bf16[2,512,128]{2,1,0:T(8,128)(2,1)S(1)}, u32[]{:S(2)}) copy-start(bf16[2,512,128]{2,1,0:T(8,128)(2,1)S(1)} %get-tuple-element.76) | copy-start | bytes 786436
  19.9 10.9 %collective-permute-start.7 = (bf16[2,512,128]{2,1,0:T(8,128)(2,1)S(1)}, bf16[2,512,128]{2,1,0:T(8,128)(2,1)S(1)}, u32[]{:S(2)}, u32[]{:S(2)}) collective-permute-start(bf16[2,512,128]{2,1,0:T(8,128)(2,1)S(1)} %get-tuple-element.70), channel_id=1, source_target_pairs={{8,0},{12,4},{0,8},{4,12},{24,16},{28,20},{16,24},{20,28},{40,32},... | collective-permute-start | bytes 786440 | tf_op jit(solution)/shard_map/ppermute | solution.py:40
  21.2 13.4 %collective-permute-start.8 = (bf16[2,512,128]{2,1,0:T(8,128)(2,1)S(1)}, bf16[2,512,128]{2,1,0:T(8,128)(2,1)S(1)}, u32[]{:S(2)}, u32[]{:S(2)}) collective-permute-start(bf16[2,512,128]{2,1,0:T(8,128)(2,1)S(1)} %get-tuple-element.71), channel_id=1, source_target_pairs={{4,0},{8,4},{12,8},{0,12},{20,16},{24,20},{28,24},{16,28},{36,32},... | collective-permute-start | bytes 786440 | tf_op jit(solution)/shard_map/ppermute | solution.py:40
  22.0 18.1 %collective-permute-start.3 = (bf16[64,3072]{1,0:T(8,128)(2,1)}, bf16[64,3072]{1,0:T(8,128)(2,1)S(1)}, u32[]{:S(2)}, u32[]{:S(2)}) collective-permute-start(bf16[64,3072]{1,0:T(8,128)(2,1)} %get-tuple-element.63), channel_id=1, source_target_pairs={{2,0},{3,1},{0,2},{1,3},{6,4},{7,5},{4,6},{5,7},{10,8},{11,9},{8,1... | collective-permute-start | bytes 1179656 | tf_op jit(solution)/shard_map/ppermute | solution.py:30
  35.3 4.8 %collective-permute-start.9 = (bf16[2,512,128]{2,1,0:T(8,128)(2,1)S(1)}, bf16[2,512,128]{2,1,0:T(8,128)(2,1)}, u32[]{:S(2)}, u32[]{:S(2)}) collective-permute-start(bf16[2,512,128]{2,1,0:T(8,128)(2,1)S(1)} %pick.2), channel_id=1, source_target_pairs={{128,0},{0,128},{129,1},{1,129},{130,2},{2,130},{131,3},{3,131},{1... | collective-permute-start | bytes 786440 | tf_op jit(solution)/shard_map/ppermute | solution.py:30
  36.7 0.7 copy-start.8
  37.5 14.1 %collective-permute-start.10 = (bf16[2,512,128]{2,1,0:T(8,128)(2,1)}, bf16[2,512,128]{2,1,0:T(8,128)(2,1)S(1)}, u32[]{:S(2)}, u32[]{:S(2)}) collective-permute-start(bf16[2,512,128]{2,1,0:T(8,128)(2,1)} %copy-done.6), channel_id=1, source_target_pairs={{12,0},{0,4},{4,8},{8,12},{28,16},{16,20},{20,24},{24,28},{44,32},... | collective-permute-start | bytes 786440 | tf_op jit(solution)/shard_map/ppermute | solution.py:40
  38.1 13.5 %collective-permute-start.11 = (bf16[2,512,128]{2,1,0:T(8,128)(2,1)}, bf16[2,512,128]{2,1,0:T(8,128)(2,1)S(1)}, u32[]{:S(2)}, u32[]{:S(2)}) collective-permute-start(bf16[2,512,128]{2,1,0:T(8,128)(2,1)} %copy-done.5), channel_id=1, source_target_pairs={{8,0},{12,4},{0,8},{4,12},{24,16},{28,20},{16,24},{20,28},{40,32},... | collective-permute-start | bytes 786440 | tf_op jit(solution)/shard_map/ppermute | solution.py:40
  39.3 14.5 %collective-permute-start.12 = (bf16[2,512,128]{2,1,0:T(8,128)(2,1)S(1)}, bf16[2,512,128]{2,1,0:T(8,128)(2,1)S(1)}, u32[]{:S(2)}, u32[]{:S(2)}) collective-permute-start(bf16[2,512,128]{2,1,0:T(8,128)(2,1)S(1)} %get-tuple-element.78), channel_id=1, source_target_pairs={{4,0},{8,4},{12,8},{0,12},{20,16},{24,20},{28,24},{16,28},{36,32},... | collective-permute-start | bytes 786440 | tf_op jit(solution)/shard_map/ppermute | solution.py:40
  48.9 5.8 %collective-permute-start.14 = (bf16[2,512,128]{2,1,0:T(8,128)(2,1)S(1)}, bf16[2,512,128]{2,1,0:T(8,128)(2,1)S(1)}, u32[]{:S(2)}, u32[]{:S(2)}) collective-permute-start(bf16[2,512,128]{2,1,0:T(8,128)(2,1)S(1)} %get-tuple-element.80), channel_id=1, source_target_pairs={{128,0},{0,128},{129,1},{1,129},{130,2},{2,130},{131,3},{3,131},{1... | collective-permute-start | bytes 786440 | tf_op jit(solution)/shard_map/ppermute | solution.py:30
  54.5 5.7 %collective-permute-start.13 = (bf16[2,512,128]{2,1,0:T(8,128)(2,1)S(1)}, bf16[2,512,128]{2,1,0:T(8,128)(2,1)S(1)}, u32[]{:S(2)}, u32[]{:S(2)}) collective-permute-start(bf16[2,512,128]{2,1,0:T(8,128)(2,1)S(1)} %pick.3), channel_id=1, source_target_pairs={{128,0},{0,128},{129,1},{1,129},{130,2},{2,130},{131,3},{3,131},{1... | collective-permute-start | bytes 786440 | tf_op jit(solution)/shard_map/ppermute | solution.py:30
  55.9 15.8 %collective-permute-start.15 = (bf16[2,512,128]{2,1,0:T(8,128)(2,1)}, bf16[2,512,128]{2,1,0:T(8,128)(2,1)}, u32[]{:S(2)}, u32[]{:S(2)}) collective-permute-start(bf16[2,512,128]{2,1,0:T(8,128)(2,1)} %get-tuple-element.82), channel_id=1, source_target_pairs={{4,0},{8,4},{12,8},{0,12},{20,16},{24,20},{28,24},{16,28},{36,32},... | collective-permute-start | bytes 786440 | tf_op jit(solution)/shard_map/ppermute | solution.py:40
  55.9 15.8 %collective-permute-start.16 = (bf16[2,512,128]{2,1,0:T(8,128)(2,1)}, bf16[2,512,128]{2,1,0:T(8,128)(2,1)}, u32[]{:S(2)}, u32[]{:S(2)}) collective-permute-start(bf16[2,512,128]{2,1,0:T(8,128)(2,1)} %get-tuple-element.83), channel_id=1, source_target_pairs={{8,0},{12,4},{0,8},{4,12},{24,16},{28,20},{16,24},{20,28},{40,32},... | collective-permute-start | bytes 786440 | tf_op jit(solution)/shard_map/ppermute | solution.py:40
  58.2 14.2 %collective-permute-start.17 = (bf16[2,512,128]{2,1,0:T(8,128)(2,1)}, bf16[2,512,128]{2,1,0:T(8,128)(2,1)}, u32[]{:S(2)}, u32[]{:S(2)}) collective-permute-start(bf16[2,512,128]{2,1,0:T(8,128)(2,1)} %get-tuple-element.84), channel_id=1, source_target_pairs={{12,0},{0,4},{4,8},{8,12},{28,16},{16,20},{20,24},{24,28},{44,32},... | collective-permute-start | bytes 786440 | tf_op jit(solution)/shard_map/ppermute | solution.py:40
  68.7 7.8 %collective-permute-start.22 = (bf16[2,512,128]{2,1,0:T(8,128)(2,1)S(1)}, bf16[2,512,128]{2,1,0:T(8,128)(2,1)S(1)}, u32[]{:S(2)}, u32[]{:S(2)}) collective-permute-start(bf16[2,512,128]{2,1,0:T(8,128)(2,1)S(1)} %get-tuple-element.98), channel_id=1, source_target_pairs={{128,0},{0,128},{129,1},{1,129},{130,2},{2,130},{131,3},{3,131},{1... | collective-permute-start | bytes 786440 | tf_op jit(solution)/shard_map/ppermute | solution.py:30
  73.7 8.1 %collective-permute-start.18 = (bf16[64,1792]{1,0:T(8,128)(2,1)S(1)}, bf16[64,1792]{1,0:T(8,128)(2,1)S(1)}, u32[]{:S(2)}, u32[]{:S(2)}) collective-permute-start(bf16[64,1792]{1,0:T(8,128)(2,1)S(1)} %get-tuple-element.91), channel_id=1, source_target_pairs={{1,0},{2,1},{3,2},{0,3},{5,4},{6,5},{7,6},{4,7},{9,8},{10,9},{11,1... | collective-permute-start | bytes 688136 | tf_op jit(solution)/shard_map/ppermute | solution.py:30
  76.8 18.3 %collective-permute-start.23 = (bf16[2,512,128]{2,1,0:T(8,128)(2,1)S(1)}, bf16[2,512,128]{2,1,0:T(8,128)(2,1)S(1)}, u32[]{:S(2)}, u32[]{:S(2)}) collective-permute-start(bf16[2,512,128]{2,1,0:T(8,128)(2,1)S(1)} %get-tuple-element.101), channel_id=1, source_target_pairs={{4,0},{8,4},{12,8},{0,12},{20,16},{24,20},{28,24},{16,28},{36,32},... | collective-permute-start | bytes 786440 | tf_op jit(solution)/shard_map/ppermute | solution.py:40
  77.5 17.6 %collective-permute-start.24 = (bf16[2,512,128]{2,1,0:T(8,128)(2,1)S(1)}, bf16[2,512,128]{2,1,0:T(8,128)(2,1)S(1)}, u32[]{:S(2)}, u32[]{:S(2)}) collective-permute-start(bf16[2,512,128]{2,1,0:T(8,128)(2,1)S(1)} %get-tuple-element.103), channel_id=1, source_target_pairs={{8,0},{12,4},{0,8},{4,12},{24,16},{28,20},{16,24},{20,28},{40,32},... | collective-permute-start | bytes 786440 | tf_op jit(solution)/shard_map/ppermute | solution.py:40
  81.0 14.1 %collective-permute-start.25 = (bf16[2,512,128]{2,1,0:T(8,128)(2,1)S(1)}, bf16[2,512,128]{2,1,0:T(8,128)(2,1)S(1)}, u32[]{:S(2)}, u32[]{:S(2)}) collective-permute-start(bf16[2,512,128]{2,1,0:T(8,128)(2,1)S(1)} %get-tuple-element.105), channel_id=1, source_target_pairs={{12,0},{0,4},{4,8},{8,12},{28,16},{16,20},{20,24},{24,28},{44,32},... | collective-permute-start | bytes 786440 | tf_op jit(solution)/shard_map/ppermute | solution.py:40
  81.0 10.1 %collective-permute-start.19 = (bf16[64,1792]{1,0:T(8,128)(2,1)S(1)}, bf16[64,1792]{1,0:T(8,128)(2,1)S(1)}, u32[]{:S(2)}, u32[]{:S(2)}) collective-permute-start(bf16[64,1792]{1,0:T(8,128)(2,1)S(1)} %get-tuple-element.92), channel_id=1, source_target_pairs={{2,0},{3,1},{0,2},{1,3},{6,4},{7,5},{4,6},{5,7},{10,8},{11,9},{8,1... | collective-permute-start | bytes 688136 | tf_op jit(solution)/shard_map/ppermute | solution.py:30
  81.8 12.3 %collective-permute-start.20 = (bf16[64,1792]{1,0:T(8,128)(2,1)S(1)}, bf16[64,1792]{1,0:T(8,128)(2,1)S(1)}, u32[]{:S(2)}, u32[]{:S(2)}) collective-permute-start(bf16[64,1792]{1,0:T(8,128)(2,1)S(1)} %get-tuple-element.93), channel_id=1, source_target_pairs={{3,0},{0,1},{1,2},{2,3},{7,4},{4,5},{5,6},{6,7},{11,8},{8,9},{9,10... | collective-permute-start | bytes 688136 | tf_op jit(solution)/shard_map/ppermute | solution.py:30
  91.1 6.4 %collective-permute-start.21 = (bf16[2,512,128]{2,1,0:T(8,128)(2,1)S(1)}, bf16[2,512,128]{2,1,0:T(8,128)(2,1)S(1)}, u32[]{:S(2)}, u32[]{:S(2)}) collective-permute-start(bf16[2,512,128]{2,1,0:T(8,128)(2,1)S(1)} %fusion.2), channel_id=1, source_target_pairs={{16,0},{20,4},{24,8},{28,12},{32,16},{36,20},{40,24},{44,28},{48,3... | collective-permute-start | bytes 786440 | tf_op jit(solution)/shard_map/ppermute | solution.py:30
  95.1 2.3 %copy-start.7 = (f32[2,512,128]{2,1,0:T(8,128)S(1)}, f32[2,512,128]{2,1,0:T(8,128)}, u32[]{:S(2)}) copy-start(f32[2,512,128]{2,1,0:T(8,128)} %get-tuple-element.81) | copy-start | bytes 1572868
  95.3 8.3 %collective-permute-start.26 = (bf16[2,512,128]{2,1,0:T(8,128)(2,1)S(1)}, bf16[2,512,128]{2,1,0:T(8,128)(2,1)S(1)}, u32[]{:S(2)}, u32[]{:S(2)}) collective-permute-start(bf16[2,512,128]{2,1,0:T(8,128)(2,1)S(1)} %fusion.15), channel_id=1, source_target_pairs={{16,0},{20,4},{24,8},{28,12},{32,16},{36,20},{40,24},{44,28},{48,3... | collective-permute-start | bytes 786440 | tf_op jit(solution)/shard_map/ppermute | solution.py:30
where the time goes:
time: 106 us; the launch traced here: 105 us
  waiting for transfers between devices  40.4 us (38%)
  starting transfers between devices  30.3 us (29%)
  Pallas kernels  20.8 us (20%)
  other arithmetic  5.37 us (5%)
  between operations  4.72 us (4%)
  local copies, waits for them, and re-layouts  3.06 us (3%)
    ppermute x15, waiting for transfers between devices, shifted(): return lax.ppermute(block, axis, route)  24.5 us
    ppermute x15, starting transfers between devices, shifted(): return lax.ppermute(block, axis, route)  17.5 us
    pallas_call x2, Pallas kernels, attend(): pl.pallas_call(functools.partial(attend_kernel, chunk, tp_count), out_sha...  17.1 us
    ppermute x12, waiting for transfers between devices, along_row(): return lax.ppermute(block, 'group', route)  16 us
    ppermute x12, starting transfers between devices, along_row(): return lax.ppermute(block, 'group', route)  12.8 us
    unnamed x18, local copies, waits for them, and re-layouts  2.97 us
  transfers between devices with their start and end apart: 27, of which 13 were waited for; matrix products, arithmetic and copies ran while one was open for 4% of the time, Pallas kernels for 20%

commit v1 on v0

--- a/solution.py
+++ b/solution.py
@@ -19,7 +19,8 @@
 MASKED = -1e30
 SCALING = HEAD_DIM ** (-0.5)
 LOG2E = 1.4426950408889634
-VMEM_LIMIT = 48 * 1024 * 1024
+ATTEND_VMEM = 24 * 1024 * 1024
+SMALL_VMEM = 8 * 1024 * 1024
 
 TP, SECTION, LENGTH, OWNER, VISIBLE = 0, 1, 2, 3, 4
 
@@ -58,7 +59,7 @@
         out_shape=out_shape,
         in_specs=in_specs,
         out_specs=jax.tree.map(lambda _: whole(), out_shape),
-        compiler_params=pltpu.CompilerParams(vmem_limit_bytes=VMEM_LIMIT),
+        compiler_params=pltpu.CompilerParams(vmem_limit_bytes=SMALL_VMEM),
         name=name,
     )
 
@@ -91,10 +92,10 @@
             chosen[...] = choice[...]
 
 
-def pack_kernel(tp, queries, grad_out, keys, values, *packs):
+def pack_kernel(meta, queries, grad_out, keys, values, *packs):
     tp_count = len(packs)
     for d, pack in enumerate(packs):
-        device, at = lax.rem(tp[0] + d, tp_count), 0
+        device, at = lax.rem(meta[TP] + d, tp_count), 0
         for chunk in range(CHUNKS):
             for source in (queries, grad_out, keys, values):
                 cols = source.shape[1] // tp_count
@@ -121,6 +122,15 @@
             at += k_part
             grad_v[:, k_at] = pack[:, at : at + k_part]
             at += k_part
+
+
+def finish_kernel(*refs):
+    shares, total = refs[:-1], refs[-1]
+    cols = shares[0].shape[2]
+    for chunk in range(CHUNKS):
+        kept, came = shares[2 * chunk : 2 * chunk + 2]
+        whole_sum = kept[...] + came[...].astype(jnp.float32)
+        total[0, :, :, chunk * cols : (chunk + 1) * cols] = whole_sum.astype(jnp.bfloat16)
 
 
 def place(index, tp, tp_count, rows):
@@ -286,9 +296,9 @@
             pltpu.VMEM((total, HEAD_DIM), f32),
             pltpu.VMEM((total, HEAD_DIM), f32),
         ],
-        compiler_params=pltpu.CompilerParams(vmem_limit_bytes=VMEM_LIMIT),
+        compiler_params=pltpu.CompilerParams(vmem_limit_bytes=ATTEND_VMEM),
         cost_estimate=pl.CostEstimate(
-            flops=flops, bytes_accessed=6 * 1024 * 1024, transcendentals=flops // 1280
+            flops=8 * flops, bytes_accessed=6 * 1024 * 1024, transcendentals=flops // 1280
         ),
         name="attend",
     )(meta, *packs, *earlier, *offers, other)
@@ -309,7 +319,6 @@
     bf16, f32 = jnp.bfloat16, jnp.float32
     part = jax.ShapeDtypeStruct((2, half, k_part), bf16)
 
-    meta = jnp.concatenate([tp, section, lengths, owners, visible_tiles[0]])
     halves = small_call(
         halves_kernel,
         "halves",
@@ -317,12 +326,14 @@
         [scalars(), whole()],
     )(section, prompt_kv)
     sibling_owner = shifted(after(owners, halves), "section", 1)
+    meta = jnp.concatenate([tp, section, lengths, owners, visible_tiles[0]])
+    meta = after(meta, sibling_owner)
     packs = small_call(
         pack_kernel,
         "pack",
         [jax.ShapeDtypeStruct((rows, pack_cols), bf16)] * tp_count,
         [scalars()] + [whole()] * 4,
-    )(after(tp, sibling_owner), resp_queries, resp_dout, resp_keys, resp_values)
+    )(meta, resp_queries, resp_dout, resp_keys, resp_values)
     arrived = {d: shifted(packs[d], "tp", d) for d in range(1, tp_count, 2)}
     for d in range(2, tp_count, 2):
         arrived[d] = shifted(after(packs[d], arrived), "tp", d)
@@ -337,7 +348,7 @@
         )
         for c in range(CHUNKS)
     ]
-    sends[0][1] = after(sends[0][1], sends[1])
+
     offers = []
     for c in range(CHUNKS):
         offer = {0: halves[c]}
@@ -356,7 +367,11 @@
         other = shifted(wanted, "section", 1)
         other = after(other, terms)
         backs, own_grad, other_grad = attend(c, meta, arrived, backs, offers[c], other)
-        sibling_grad = shifted(other_grad, "section", 1)
+        if c == CHUNKS - 1:
+            returned = {d: shifted(backs[d], "tp", -d) for d in range(1, tp_count, 2)}
+            for d in range(2, tp_count, 2):
+                returned[d] = shifted(after(backs[d], returned), "tp", -d)
+        sibling_grad = after(shifted(other_grad, "section", 1), passing)
         terms = []
         for offset in range(WIN):
             term = jnp.where(owners[0] == offset, own_grad.astype(f32), 0.0) + jnp.where(
@@ -374,10 +389,10 @@
             kept = kept + jnp.where(crossing, 0.0, term)
             passed = passed + jnp.where(crossing, term, 0.0)
         passed = passed.astype(bf16)
+        if c == CHUNKS - 1:
+            passed = after(passed, (returned[1], returned[tp_count - 1]))
         passing.append(passed)
-        shares.append((kept + to_row(passed, -1).astype(f32)).astype(bf16))
-    backs = after(backs, passing[0])
-    returned = [backs[0]] + [shifted(backs[d], "tp", -d) for d in range(1, tp_count)]
+        shares += [kept, passed]
 
     grads = small_call(
         unpack_kernel,
@@ -388,8 +403,16 @@
             jax.ShapeDtypeStruct(resp_values.shape, bf16),
         ],
         [scalars()] + [whole()] * tp_count,
-    )(tp, *returned)
-    return (grads[0], grads[1], grads[2], jnp.concatenate(shares, -1)[None])
+    )(tp, backs[0], *[returned[d] for d in range(1, tp_count)])
+    shares[1] = to_row(after(shares[1], returned[1]), -1)
+    shares[3] = to_row(shares[3], -1)
+    prompt_grads = small_call(
+        finish_kernel,
+        "finish",
+        jax.ShapeDtypeStruct((1, 2, half, prompt_kv.shape[3]), bf16),
+        [whole()] * len(shares),
+    )(*shares)
+    return (grads[0], grads[1], grads[2], prompt_grads)
 
 
 def solution(mesh):

time: 106 us -> 101 us (0.953)
  the two profiles are of different devices: /device:TPU:24 before, /device:TPU:1 now
where the time goes in v1:
time: 101 us
  starting transfers between devices  36 us (36%)
  waiting for transfers between devices  30 us (30%)
  Pallas kernels  23.1 us (23%)
  local copies, waits for them, and re-layouts  5 us (5%)
  between operations  4.71 us (5%)
  other arithmetic  2.12 us (2%)
    ppermute x15, starting transfers between devices, shifted(): return lax.ppermute(block, axis, route)  21.9 us
    pallas_call x2, Pallas kernels, attend(): pl.pallas_call(functools.partial(attend_kernel, chunk, tp_count), out_sha...  17.2 us
    ppermute x15, waiting for transfers between devices, shifted(): return lax.ppermute(block, axis, route)  15.9 us
    ppermute x12, waiting for transfers between devices, along_row(): return lax.ppermute(block, 'group', route)  14.1 us
    ppermute x12, starting transfers between devices, along_row(): return lax.ppermute(block, 'group', route)  14.1 us
    unnamed x24, local copies, waits for them, and re-layouts  4.92 us
  transfers between devices with their start and end apart: 27, of which 8 were waited for; matrix products, arithmetic and copies ran while one was open for 2% of the time, Pallas kernels for 22%

profile of v1, /device:TPU:1, one launch (start us, length us, event | category | flops | bytes accessed | tf_op | source)
XLA Modules:
  0.0 100.9 jit_solution(14936897750643345913)
XLA Ops:
  0.6 1.2 %copy-done = bf16[1,2,1024,256]{3,2,1,0:T(8,128)(2,1)S(1)} copy-done((bf16[1,2,1024,256]{3,2,1,0:T(8,128)(2,1)S(1)}, bf16[1,2,1024,256]{3,2,1,0:T(8,128)(2,1)}, u32[]{:S(2)}) %copy-start) | copy-done | bytes 1048600
  2.0 2.5 %collective-permute-start.4 = (bf16[2,512,128]{2,1,0:T(8,128)(2,1)S(1)}, bf16[2,512,128]{2,1,0:T(8,128)(2,1)S(1)}, u32[]{:S(2)}, u32[]{:S(2)}) collective-permute-start(bf16[2,512,128]{2,1,0:T(8,128)(2,1)S(1)} %get-tuple-element.54.own.refs_0_.refs_4_), channel_id=1, source_target_pairs={{112,0},{116,4},{120,8},{124,12},{0,16},{4,20},{8,24},{12,28},{16,... | collective-permute-start | bytes 786440 | tf_op jit(solution)/shard_map/ppermute | solution.py:31
  4.5 1.0 collective-permute-start
  6.8 0.6 copy-done.11
  7.5 1.1 %copy-done.2 = bf16[64,5120]{1,0:T(8,128)(2,1)S(1)} copy-done((bf16[64,5120]{1,0:T(8,128)(2,1)S(1)}, bf16[64,5120]{1,0:T(8,128)(2,1)}, u32[]{:S(2)}) %copy-start.2) | copy-done | bytes 655384
  8.6 1.6 %pack.1 = (bf16[64,3072]{1,0:T(8,128)(2,1)S(1)}, bf16[64,3072]{1,0:T(8,128)(2,1)}, bf16[64,3072]{1,0:T(8,128)(2,1)}, bf16[64,3072]{1,0:T(8,128)(2,1)S(1)}) custom-call(s32[12]{0:T(128)S(1)} %concatenate.3.meta, bf16[64,5120]{1,0:T(8,128)(2,1)S(1)} %copy-done.1, bf16[64,5120]{1,0:T(8,128)(2,1)S(1)} %copy-done.2, bf16[64,1024]{1,0:T(8,128)(2,1)S(1)} %copy-done.3, ...), custom_call_target="tpu_custom_call" | custom-call | tf_op jit(solution)/shard_map/pack/pallas_call | solution.py:331
  10.2 1.2 %collective-permute-start.1 = (bf16[64,3072]{1,0:T(8,128)(2,1)}, bf16[64,3072]{1,0:T(8,128)(2,1)S(1)}, u32[]{:S(2)}, u32[]{:S(2)}) collective-permute-start(bf16[64,3072]{1,0:T(8,128)(2,1)} %get-tuple-element.59), channel_id=1, source_target_pairs={{3,0},{0,1},{1,2},{2,3},{7,4},{4,5},{5,6},{6,7},{11,8},{8,9},{9,10... | collective-permute-start | bytes 1179656 | tf_op jit(solution)/shard_map/ppermute | solution.py:31
  11.4 1.5 %collective-permute-start.2 = (bf16[64,3072]{1,0:T(8,128)(2,1)S(1)}, bf16[64,3072]{1,0:T(8,128)(2,1)S(1)}, u32[]{:S(2)}, u32[]{:S(2)}) collective-permute-start(bf16[64,3072]{1,0:T(8,128)(2,1)S(1)} %get-tuple-element.61), channel_id=1, source_target_pairs={{1,0},{2,1},{3,2},{0,3},{5,4},{6,5},{7,6},{4,7},{9,8},{10,9},{11,1... | collective-permute-start | bytes 1179656 | tf_op jit(solution)/shard_map/ppermute | solution.py:31
  12.9 1.6 %collective-permute-done.4.before = bf16[2,512,128]{2,1,0:T(8,128)(2,1)S(1)} collective-permute-done((bf16[2,512,128]{2,1,0:T(8,128)(2,1)S(1)}, bf16[2,512,128]{2,1,0:T(8,128)(2,1)S(1)}, u32[]{:S(2)}, u32[]{:S(2)}) %collective-permute-start.4) | collective-permute-done | bytes 262176 | tf_op jit(solution)/shard_map/ppermute | solution.py:31
  14.6 1.4 %collective-permute-start.5 = (bf16[2,512,128]{2,1,0:T(8,128)(2,1)S(1)}, bf16[2,512,128]{2,1,0:T(8,128)(2,1)S(1)}, u32[]{:S(2)}, u32[]{:S(2)}) collective-permute-start(bf16[2,512,128]{2,1,0:T(8,128)(2,1)S(1)} %get-tuple-element.64), channel_id=1, source_target_pairs={{12,0},{0,4},{4,8},{8,12},{28,16},{16,20},{20,24},{24,28},{44,32},... | collective-permute-start | bytes 786440 | tf_op jit(solution)/shard_map/ppermute | solution.py:41
  15.9 2.6 %collective-permute-start.6 = (bf16[2,512,128]{2,1,0:T(8,128)(2,1)S(1)}, bf16[2,512,128]{2,1,0:T(8,128)(2,1)S(1)}, u32[]{:S(2)}, u32[]{:S(2)}) collective-permute-start(bf16[2,512,128]{2,1,0:T(8,128)(2,1)S(1)} %get-tuple-element.65), channel_id=1, source_target_pairs={{8,0},{12,4},{0,8},{4,12},{24,16},{28,20},{16,24},{20,28},{40,32},... | collective-permute-start | bytes 786440 | tf_op jit(solution)/shard_map/ppermute | solution.py:41
  18.6 1.1 %collective-permute-start.7 = (bf16[2,512,128]{2,1,0:T(8,128)(2,1)S(1)}, bf16[2,512,128]{2,1,0:T(8,128)(2,1)S(1)}, u32[]{:S(2)}, u32[]{:S(2)}) collective-permute-start(bf16[2,512,128]{2,1,0:T(8,128)(2,1)S(1)} %get-tuple-element.66), channel_id=1, source_target_pairs={{4,0},{8,4},{12,8},{0,12},{20,16},{24,20},{28,24},{16,28},{36,32},... | collective-permute-start | bytes 786440 | tf_op jit(solution)/shard_map/ppermute | solution.py:41
  19.6 2.8 %collective-permute-done.1.refs_1_ = bf16[64,3072]{1,0:T(8,128)(2,1)S(1)} collective-permute-done((bf16[64,3072]{1,0:T(8,128)(2,1)}, bf16[64,3072]{1,0:T(8,128)(2,1)S(1)}, u32[]{:S(2)}, u32[]{:S(2)}) %collective-permute-start.1) | collective-permute-done | bytes 393248 | tf_op jit(solution)/shard_map/ppermute | solution.py:31
  22.4 1.9 %collective-permute-start.3 = (bf16[64,3072]{1,0:T(8,128)(2,1)}, bf16[64,3072]{1,0:T(8,128)(2,1)S(1)}, u32[]{:S(2)}, u32[]{:S(2)}) collective-permute-start(bf16[64,3072]{1,0:T(8,128)(2,1)} %get-tuple-element.62), channel_id=1, source_target_pairs={{2,0},{3,1},{0,2},{1,3},{6,4},{7,5},{4,6},{5,7},{10,8},{11,9},{8,1... | collective-permute-start | bytes 1179656 | tf_op jit(solution)/shard_map/ppermute | solution.py:31
  24.3 1.6 %collective-permute-start.9 = (bf16[2,512,128]{2,1,0:T(8,128)(2,1)S(1)}, bf16[2,512,128]{2,1,0:T(8,128)(2,1)S(1)}, u32[]{:S(2)}, u32[]{:S(2)}) collective-permute-start(bf16[2,512,128]{2,1,0:T(8,128)(2,1)S(1)} %get-tuple-element.55.own.refs_0_.refs_8_), channel_id=1, source_target_pairs={{112,0},{116,4},{120,8},{124,12},{0,16},{4,20},{8,24},{12,28},{16,... | collective-permute-start | bytes 786440 | tf_op jit(solution)/shard_map/ppermute | solution.py:31
  25.9 3.3 %collective-permute-done.6.refs_2_.refs_6_ = bf16[2,512,128]{2,1,0:T(8,128)(2,1)S(1)} collective-permute-done((bf16[2,512,128]{2,1,0:T(8,128)(2,1)S(1)}, bf16[2,512,128]{2,1,0:T(8,128)(2,1)S(1)}, u32[]{:S(2)}, u32[]{:S(2)}) %collective-permute-start.6) | collective-permute-done | bytes 262176 | tf_op jit(solution)/shard_map/ppermute | solution.py:41
  29.3 0.7 pick.2
  30.0 2.2 %collective-permute-start.8 = (bf16[2,512,128]{2,1,0:T(8,128)(2,1)S(1)}, bf16[2,512,128]{2,1,0:T(8,128)(2,1)S(1)}, u32[]{:S(2)}, u32[]{:S(2)}) collective-permute-start(bf16[2,512,128]{2,1,0:T(8,128)(2,1)S(1)} %pick.2), channel_id=1, source_target_pairs={{128,0},{0,128},{129,1},{1,129},{130,2},{2,130},{131,3},{3,131},{1... | collective-permute-start | bytes 786440 | tf_op jit(solution)/shard_map/ppermute | solution.py:31
  32.2 1.1 %collective-permute-done.9.before = bf16[2,512,128]{2,1,0:T(8,128)(2,1)S(1)} collective-permute-done((bf16[2,512,128]{2,1,0:T(8,128)(2,1)S(1)}, bf16[2,512,128]{2,1,0:T(8,128)(2,1)S(1)}, u32[]{:S(2)}, u32[]{:S(2)}) %collective-permute-start.9) | collective-permute-done | bytes 262176 | tf_op jit(solution)/shard_map/ppermute | solution.py:31
  33.3 0.9 sends.3
  34.2 1.3 %collective-permute-start.10 = (bf16[2,512,128]{2,1,0:T(8,128)(2,1)}, bf16[2,512,128]{2,1,0:T(8,128)(2,1)S(1)}, u32[]{:S(2)}, u32[]{:S(2)}) collective-permute-start(bf16[2,512,128]{2,1,0:T(8,128)(2,1)} %get-tuple-element.72), channel_id=1, source_target_pairs={{12,0},{0,4},{4,8},{8,12},{28,16},{16,20},{20,24},{24,28},{44,32},... | collective-permute-start | bytes 786440 | tf_op jit(solution)/shard_map/ppermute | solution.py:41
  35.5 2.6 %collective-permute-start.11 = (bf16[2,512,128]{2,1,0:T(8,128)(2,1)}, bf16[2,512,128]{2,1,0:T(8,128)(2,1)S(1)}, u32[]{:S(2)}, u32[]{:S(2)}) collective-permute-start(bf16[2,512,128]{2,1,0:T(8,128)(2,1)} %get-tuple-element.74), channel_id=1, source_target_pairs={{8,0},{12,4},{0,8},{4,12},{24,16},{28,20},{16,24},{20,28},{40,32},... | collective-permute-start | bytes 786440 | tf_op jit(solution)/shard_map/ppermute | solution.py:41
  38.1 1.1 %collective-permute-start.12 = (bf16[2,512,128]{2,1,0:T(8,128)(2,1)S(1)}, bf16[2,512,128]{2,1,0:T(8,128)(2,1)S(1)}, u32[]{:S(2)}, u32[]{:S(2)}) collective-permute-start(bf16[2,512,128]{2,1,0:T(8,128)(2,1)S(1)} %get-tuple-element.76), channel_id=1, source_target_pairs={{4,0},{8,4},{12,8},{0,12},{20,16},{24,20},{28,24},{16,28},{36,32},... | collective-permute-start | bytes 786440 | tf_op jit(solution)/shard_map/ppermute | solution.py:41
  39.2 8.8 %attend.2 = (bf16[64,896]{1,0:T(8,128)(2,1)S(1)}, bf16[64,896]{1,0:T(8,128)(2,1)S(1)}, bf16[64,896]{1,0:T(8,128)(2,1)S(1)}, bf16[64,896]{1,0:T(8,128)(2,1)S(1)},...) custom-call(s32[12]{0:T(128)S(1)} %concatenate.3.meta, bf16[64,3072]{1,0:T(8,128)(2,1)S(1)} %get-tuple-element.58.refs_0_, ...), custom_call_target="tpu_custom_call" | custom-call | flops 16777216000 | bytes 6291456 | tf_op jit(solution)/shard_map/attend/pallas_call | solution.py:276
  47.9 0.6 copy-done.5
  48.6 0.6 copy-done.7
  49.2 0.6 copy-done.9
  49.8 2.9 %collective-permute-start.14 = (bf16[2,512,128]{2,1,0:T(8,128)(2,1)}, bf16[2,512,128]{2,1,0:T(8,128)(2,1)}, u32[]{:S(2)}, u32[]{:S(2)}) collective-permute-start(bf16[2,512,128]{2,1,0:T(8,128)(2,1)} %get-tuple-element.78), channel_id=1, source_target_pairs={{128,0},{0,128},{129,1},{1,129},{130,2},{2,130},{131,3},{3,131},{1... | collective-permute-start | bytes 786440 | tf_op jit(solution)/shard_map/ppermute | solution.py:31
  55.3 0.7 pick.3
  56.1 1.3 %fusion.18 = (bf16[2,512,128]{2,1,0:T(8,128)(2,1)S(1)}, bf16[2,512,128]{2,1,0:T(8,128)(2,1)S(1)}, bf16[2,512,128]{2,1,0:T(8,128)(2,1)S(1)}, f32[2,512,128]{2,1,0:T(8,128)S(1)}) fusion(bf16[2,512,128]{2,1,0:T(8,128)(2,1)S(1)} %get-tuple-element.77, bf16[2,512,128]{2,1,0:T(8,128)(2,1)} %collective-permute-done.14, pred[]{:T(512)} %bitcast.11, pred[]{:T(512)} %bitcast.10, ...), kind=kLoop, calls=%fused_computation.46 | loop fusion | flops 2228224 | bytes 1835016 | tf_op jit(solution)/shard_map/convert_element_type | solution.py:380
  57.5 2.2 %collective-permute-start.19 = (bf16[2,512,128]{2,1,0:T(8,128)(2,1)S(1)}, bf16[2,512,128]{2,1,0:T(8,128)(2,1)S(1)}, u32[]{:S(2)}, u32[]{:S(2)}) collective-permute-start(bf16[2,512,128]{2,1,0:T(8,128)(2,1)S(1)} %get-tuple-element.81), channel_id=1, source_target_pairs={{8,0},{12,4},{0,8},{4,12},{24,16},{28,20},{16,24},{20,28},{40,32},... | collective-permute-start | bytes 786440 | tf_op jit(solution)/shard_map/ppermute | solution.py:41
  59.7 8.4 %attend.3 = (bf16[64,1792]{1,0:T(8,128)(2,1)S(1)}, bf16[64,1792]{1,0:T(8,128)(2,1)S(1)}, bf16[64,1792]{1,0:T(8,128)(2,1)S(1)}, bf16[64,1792]{1,0:T(8,128)(2,1)S(...) custom-call(s32[12]{0:T(128)S(1)} %concatenate.3.meta, ...), custom_call_target="tpu_custom_call" | custom-call | flops 16777216000 | bytes 6291456 | tf_op jit(solution)/shard_map/attend/pallas_call | solution.py:276
  68.2 1.1 %collective-permute-start.22 = (bf16[2,512,128]{2,1,0:T(8,128)(2,1)S(1)}, bf16[2,512,128]{2,1,0:T(8,128)(2,1)S(1)}, u32[]{:S(2)}, u32[]{:S(2)}) collective-permute-start(bf16[2,512,128]{2,1,0:T(8,128)(2,1)S(1)} %get-tuple-element.94), channel_id=1, source_target_pairs={{128,0},{0,128},{129,1},{1,129},{130,2},{2,130},{131,3},{3,131},{1... | collective-permute-start | bytes 786440 | tf_op jit(solution)/shard_map/ppermute | solution.py:31
  69.3 3.7 %collective-permute-done.20 = bf16[2,512,128]{2,1,0:T(8,128)(2,1)S(1)} collective-permute-done((bf16[2,512,128]{2,1,0:T(8,128)(2,1)S(1)}, bf16[2,512,128]{2,1,0:T(8,128)(2,1)S(1)}, u32[]{:S(2)}, u32[]{:S(2)}) %collective-permute-start.20) | collective-permute-done | bytes 262176 | tf_op jit(solution)/shard_map/ppermute | solution.py:41
  73.0 0.3 fusion.5
  73.2 0.3 fusion.25
  73.7 1.2 %collective-permute-start.24 = (bf16[2,512,128]{2,1,0:T(8,128)(2,1)S(1)}, bf16[2,512,128]{2,1,0:T(8,128)(2,1)S(1)}, u32[]{:S(2)}, u32[]{:S(2)}) collective-permute-start(bf16[2,512,128]{2,1,0:T(8,128)(2,1)S(1)} %get-tuple-element.100), channel_id=1, source_target_pairs={{8,0},{12,4},{0,8},{4,12},{24,16},{28,20},{16,24},{20,28},{40,32},... | collective-permute-start | bytes 786440 | tf_op jit(solution)/shard_map/ppermute | solution.py:41
  75.0 0.3 collective-permute-start.25
  75.3 1.2 %collective-permute-start.15 = (bf16[64,1792]{1,0:T(8,128)(2,1)S(1)}, bf16[64,1792]{1,0:T(8,128)(2,1)S(1)}, u32[]{:S(2)}, u32[]{:S(2)}) collective-permute-start(bf16[64,1792]{1,0:T(8,128)(2,1)S(1)} %get-tuple-element.85), channel_id=1, source_target_pairs={{1,0},{2,1},{3,2},{0,3},{5,4},{6,5},{7,6},{4,7},{9,8},{10,9},{11,1... | collective-permute-start | bytes 688136 | tf_op jit(solution)/shard_map/ppermute | solution.py:31
  76.4 0.3 collective-permute-start.16
  76.7 3.7 %collective-permute-done.15.refs_1_ = bf16[64,1792]{1,0:T(8,128)(2,1)S(1)} collective-permute-done((bf16[64,1792]{1,0:T(8,128)(2,1)S(1)}, bf16[64,1792]{1,0:T(8,128)(2,1)S(1)}, u32[]{:S(2)}, u32[]{:S(2)}) %collective-permute-start.15) | collective-permute-done | bytes 229408 | tf_op jit(solution)/shard_map/ppermute | solution.py:31
  80.4 1.6 %collective-permute-start.21 = (bf16[2,512,128]{2,1,0:T(8,128)(2,1)S(1)}, bf16[2,512,128]{2,1,0:T(8,128)(2,1)S(1)}, u32[]{:S(2)}, u32[]{:S(2)}) collective-permute-start(bf16[2,512,128]{2,1,0:T(8,128)(2,1)S(1)} %get-tuple-element.92), channel_id=1, source_target_pairs={{16,0},{20,4},{24,8},{28,12},{32,16},{36,20},{40,24},{44,28},{48,3... | collective-permute-start | bytes 786440 | tf_op jit(solution)/shard_map/ppermute | solution.py:31
  82.1 7.0 %collective-permute-done.25 = bf16[2,512,128]{2,1,0:T(8,128)(2,1)S(1)} collective-permute-done((bf16[2,512,128]{2,1,0:T(8,128)(2,1)S(1)}, bf16[2,512,128]{2,1,0:T(8,128)(2,1)S(1)}, u32[]{:S(2)}, u32[]{:S(2)}) %collective-permute-start.25) | collective-permute-done | bytes 262176 | tf_op jit(solution)/shard_map/ppermute | solution.py:41
  89.4 1.7 %collective-permute-start.26 = (bf16[2,512,128]{2,1,0:T(8,128)(2,1)S(1)}, bf16[2,512,128]{2,1,0:T(8,128)(2,1)S(1)}, u32[]{:S(2)}, u32[]{:S(2)}) collective-permute-start(bf16[2,512,128]{2,1,0:T(8,128)(2,1)S(1)} %get-tuple-element.103), channel_id=1, source_target_pairs={{16,0},{20,4},{24,8},{28,12},{32,16},{36,20},{40,24},{44,28},{48,3... | collective-permute-start | bytes 786440 | tf_op jit(solution)/shard_map/ppermute | solution.py:31
  91.1 1.1 %collective-permute-start.17 = (bf16[64,1792]{1,0:T(8,128)(2,1)S(1)}, bf16[64,1792]{1,0:T(8,128)(2,1)S(1)}, u32[]{:S(2)}, u32[]{:S(2)}) collective-permute-start(bf16[64,1792]{1,0:T(8,128)(2,1)S(1)} %get-tuple-element.88), channel_id=1, source_target_pairs={{2,0},{3,1},{0,2},{1,3},{6,4},{7,5},{4,6},{5,7},{10,8},{11,9},{8,1... | collective-permute-start | bytes 688136 | tf_op jit(solution)/shard_map/ppermute | solution.py:31
  92.1 6.8 %collective-permute-done.17.refs_2_ = bf16[64,1792]{1,0:T(8,128)(2,1)S(1)} collective-permute-done((bf16[64,1792]{1,0:T(8,128)(2,1)S(1)}, bf16[64,1792]{1,0:T(8,128)(2,1)S(1)}, u32[]{:S(2)}, u32[]{:S(2)}) %collective-permute-start.17) | collective-permute-done | bytes 229408 | tf_op jit(solution)/shard_map/ppermute | solution.py:31
  98.9 1.0 %unpack.1 = (bf16[64,5120]{1,0:T(8,128)(2,1)}, bf16[64,1024]{1,0:T(8,128)(2,1)}, bf16[64,1024]{1,0:T(8,128)(2,1)}) custom-call(s32[1]{0:T(128)} %bitcast.tp, bf16[64,1792]{1,0:T(8,128)(2,1)S(1)} %get-tuple-element.84.refs_0_, bf16[64,1792]{1,0:T(8,128)(2,1)S(1)} %collective-permute-done.15.refs_1_, bf16[64,1792]{1,0:T(8,128)(2,1)S(1)} %collective-permute-done.17.refs_2_, ...), custom_call_target="tpu_custom_call" | custom-call | tf_op jit(solution)/shard_map/unpack/pallas_call | solution.py:397
  100.0 0.9 finish.1
  (45 shorter events, 1.0 us)
Async XLA Ops:
  0.6 1.2 %copy-start = (bf16[1,2,1024,256]{3,2,1,0:T(8,128)(2,1)S(1)}, bf16[1,2,1024,256]{3,2,1,0:T(8,128)(2,1)}, u32[]{:S(2)}) copy-start(bf16[1,2,1024,256]{3,2,1,0:T(8,128)(2,1)} %prompt.1) | copy-start | bytes 3145732
  1.9 5.6 %copy-start.1 = (bf16[64,5120]{1,0:T(8,128)(2,1)S(1)}, bf16[64,5120]{1,0:T(8,128)(2,1)}, u32[]{:S(2)}) copy-start(bf16[64,5120]{1,0:T(8,128)(2,1)} %queries.1) | copy-start | bytes 1966084
  1.9 5.6 %copy-start.3 = (bf16[64,1024]{1,0:T(8,128)(2,1)S(1)}, bf16[64,1024]{1,0:T(8,128)(2,1)}, u32[]{:S(2)}) copy-start(bf16[64,1024]{1,0:T(8,128)(2,1)} %keys.1) | copy-start | bytes 393220
  1.9 5.7 %copy-start.4 = (bf16[64,1024]{1,0:T(8,128)(2,1)S(1)}, bf16[64,1024]{1,0:T(8,128)(2,1)}, u32[]{:S(2)}) copy-start(bf16[64,1024]{1,0:T(8,128)(2,1)} %values.1) | copy-start | bytes 393220
  2.0 12.5 %collective-permute-start.4 = (bf16[2,512,128]{2,1,0:T(8,128)(2,1)S(1)}, bf16[2,512,128]{2,1,0:T(8,128)(2,1)S(1)}, u32[]{:S(2)}, u32[]{:S(2)}) collective-permute-start(bf16[2,512,128]{2,1,0:T(8,128)(2,1)S(1)} %get-tuple-element.54.own.refs_0_.refs_4_), channel_id=1, source_target_pairs={{112,0},{116,4},{120,8},{124,12},{0,16},{4,20},{8,24},{12,28},{16,... | collective-permute-start | bytes 786440 | tf_op jit(solution)/shard_map/ppermute | solution.py:31
  4.5 3.0 %collective-permute-start = (s32[1]{0:T(128)}, s32[1]{0:T(128)}, u32[]{:S(2)}, u32[]{:S(2)}) collective-permute-start(s32[1]{0:T(128)} %param.14), channel_id=1, source_target_pairs={{128,0},{0,128},{129,1},{1,129},{130,2},{2,130},{131,3},{3,131},{1... | collective-permute-start | bytes 20 | tf_op jit(solution)/shard_map/ppermute | solution.py:31
  6.8 0.7 copy-start.11
  7.5 1.1 %copy-start.2 = (bf16[64,5120]{1,0:T(8,128)(2,1)S(1)}, bf16[64,5120]{1,0:T(8,128)(2,1)}, u32[]{:S(2)}) copy-start(bf16[64,5120]{1,0:T(8,128)(2,1)} %grad_out.1) | copy-start | bytes 1966084
  10.2 12.2 %collective-permute-start.1 = (bf16[64,3072]{1,0:T(8,128)(2,1)}, bf16[64,3072]{1,0:T(8,128)(2,1)S(1)}, u32[]{:S(2)}, u32[]{:S(2)}) collective-permute-start(bf16[64,3072]{1,0:T(8,128)(2,1)} %get-tuple-element.59), channel_id=1, source_target_pairs={{3,0},{0,1},{1,2},{2,3},{7,4},{4,5},{5,6},{6,7},{11,8},{8,9},{9,10... | collective-permute-start | bytes 1179656 | tf_op jit(solution)/shard_map/ppermute | solution.py:31
  11.4 11.0 %collective-permute-start.2 = (bf16[64,3072]{1,0:T(8,128)(2,1)S(1)}, bf16[64,3072]{1,0:T(8,128)(2,1)S(1)}, u32[]{:S(2)}, u32[]{:S(2)}) collective-permute-start(bf16[64,3072]{1,0:T(8,128)(2,1)S(1)} %get-tuple-element.61), channel_id=1, source_target_pairs={{1,0},{2,1},{3,2},{0,3},{5,4},{6,5},{7,6},{4,7},{9,8},{10,9},{11,1... | collective-permute-start | bytes 1179656 | tf_op jit(solution)/shard_map/ppermute | solution.py:31
  14.6 11.4 %collective-permute-start.5 = (bf16[2,512,128]{2,1,0:T(8,128)(2,1)S(1)}, bf16[2,512,128]{2,1,0:T(8,128)(2,1)S(1)}, u32[]{:S(2)}, u32[]{:S(2)}) collective-permute-start(bf16[2,512,128]{2,1,0:T(8,128)(2,1)S(1)} %get-tuple-element.64), channel_id=1, source_target_pairs={{12,0},{0,4},{4,8},{8,12},{28,16},{16,20},{20,24},{24,28},{44,32},... | collective-permute-start | bytes 786440 | tf_op jit(solution)/shard_map/ppermute | solution.py:41
  15.9 13.4 %collective-permute-start.6 = (bf16[2,512,128]{2,1,0:T(8,128)(2,1)S(1)}, bf16[2,512,128]{2,1,0:T(8,128)(2,1)S(1)}, u32[]{:S(2)}, u32[]{:S(2)}) collective-permute-start(bf16[2,512,128]{2,1,0:T(8,128)(2,1)S(1)} %get-tuple-element.65), channel_id=1, source_target_pairs={{8,0},{12,4},{0,8},{4,12},{24,16},{28,20},{16,24},{20,28},{40,32},... | collective-permute-start | bytes 786440 | tf_op jit(solution)/shard_map/ppermute | solution.py:41
  18.6 10.8 %collective-permute-start.7 = (bf16[2,512,128]{2,1,0:T(8,128)(2,1)S(1)}, bf16[2,512,128]{2,1,0:T(8,128)(2,1)S(1)}, u32[]{:S(2)}, u32[]{:S(2)}) collective-permute-start(bf16[2,512,128]{2,1,0:T(8,128)(2,1)S(1)} %get-tuple-element.66), channel_id=1, source_target_pairs={{4,0},{8,4},{12,8},{0,12},{20,16},{24,20},{28,24},{16,28},{36,32},... | collective-permute-start | bytes 786440 | tf_op jit(solution)/shard_map/ppermute | solution.py:41
  22.4 16.8 %collective-permute-start.3 = (bf16[64,3072]{1,0:T(8,128)(2,1)}, bf16[64,3072]{1,0:T(8,128)(2,1)S(1)}, u32[]{:S(2)}, u32[]{:S(2)}) collective-permute-start(bf16[64,3072]{1,0:T(8,128)(2,1)} %get-tuple-element.62), channel_id=1, source_target_pairs={{2,0},{3,1},{0,2},{1,3},{6,4},{7,5},{4,6},{5,7},{10,8},{11,9},{8,1... | collective-permute-start | bytes 1179656 | tf_op jit(solution)/shard_map/ppermute | solution.py:31
  24.3 9.0 %collective-permute-start.9 = (bf16[2,512,128]{2,1,0:T(8,128)(2,1)S(1)}, bf16[2,512,128]{2,1,0:T(8,128)(2,1)S(1)}, u32[]{:S(2)}, u32[]{:S(2)}) collective-permute-start(bf16[2,512,128]{2,1,0:T(8,128)(2,1)S(1)} %get-tuple-element.55.own.refs_0_.refs_8_), channel_id=1, source_target_pairs={{112,0},{116,4},{120,8},{124,12},{0,16},{4,20},{8,24},{12,28},{16,... | collective-permute-start | bytes 786440 | tf_op jit(solution)/shard_map/ppermute | solution.py:31
  30.0 9.2 %collective-permute-start.8 = (bf16[2,512,128]{2,1,0:T(8,128)(2,1)S(1)}, bf16[2,512,128]{2,1,0:T(8,128)(2,1)S(1)}, u32[]{:S(2)}, u32[]{:S(2)}) collective-permute-start(bf16[2,512,128]{2,1,0:T(8,128)(2,1)S(1)} %pick.2), channel_id=1, source_target_pairs={{128,0},{0,128},{129,1},{1,129},{130,2},{2,130},{131,3},{3,131},{1... | collective-permute-start | bytes 786440 | tf_op jit(solution)/shard_map/ppermute | solution.py:31
  34.2 21.1 %collective-permute-start.10 = (bf16[2,512,128]{2,1,0:T(8,128)(2,1)}, bf16[2,512,128]{2,1,0:T(8,128)(2,1)S(1)}, u32[]{:S(2)}, u32[]{:S(2)}) collective-permute-start(bf16[2,512,128]{2,1,0:T(8,128)(2,1)} %get-tuple-element.72), channel_id=1, source_target_pairs={{12,0},{0,4},{4,8},{8,12},{28,16},{16,20},{20,24},{24,28},{44,32},... | collective-permute-start | bytes 786440 | tf_op jit(solution)/shard_map/ppermute | solution.py:41
  35.5 19.8 %collective-permute-start.11 = (bf16[2,512,128]{2,1,0:T(8,128)(2,1)}, bf16[2,512,128]{2,1,0:T(8,128)(2,1)S(1)}, u32[]{:S(2)}, u32[]{:S(2)}) collective-permute-start(bf16[2,512,128]{2,1,0:T(8,128)(2,1)} %get-tuple-element.74), channel_id=1, source_target_pairs={{8,0},{12,4},{0,8},{4,12},{24,16},{28,20},{16,24},{20,28},{40,32},... | collective-permute-start | bytes 786440 | tf_op jit(solution)/shard_map/ppermute | solution.py:41
  38.1 17.2 %collective-permute-start.12 = (bf16[2,512,128]{2,1,0:T(8,128)(2,1)S(1)}, bf16[2,512,128]{2,1,0:T(8,128)(2,1)S(1)}, u32[]{:S(2)}, u32[]{:S(2)}) collective-permute-start(bf16[2,512,128]{2,1,0:T(8,128)(2,1)S(1)} %get-tuple-element.76), channel_id=1, source_target_pairs={{4,0},{8,4},{12,8},{0,12},{20,16},{24,20},{28,24},{16,28},{36,32},... | collective-permute-start | bytes 786440 | tf_op jit(solution)/shard_map/ppermute | solution.py:41
  47.9 0.6 copy-start.5
  48.6 0.6 copy-start.7
  49.2 0.6 copy-start.9
  49.8 6.2 %collective-permute-start.14 = (bf16[2,512,128]{2,1,0:T(8,128)(2,1)}, bf16[2,512,128]{2,1,0:T(8,128)(2,1)}, u32[]{:S(2)}, u32[]{:S(2)}) collective-permute-start(bf16[2,512,128]{2,1,0:T(8,128)(2,1)} %get-tuple-element.78), channel_id=1, source_target_pairs={{128,0},{0,128},{129,1},{1,129},{130,2},{2,130},{131,3},{3,131},{1... | collective-permute-start | bytes 786440 | tf_op jit(solution)/shard_map/ppermute | solution.py:31
  56.0 3.7 %collective-permute-start.13 = (bf16[2,512,128]{2,1,0:T(8,128)(2,1)S(1)}, bf16[2,512,128]{2,1,0:T(8,128)(2,1)S(1)}, u32[]{:S(2)}, u32[]{:S(2)}) collective-permute-start(bf16[2,512,128]{2,1,0:T(8,128)(2,1)S(1)} %pick.3), channel_id=1, source_target_pairs={{128,0},{0,128},{129,1},{1,129},{130,2},{2,130},{131,3},{3,131},{1... | collective-permute-start | bytes 786440 | tf_op jit(solution)/shard_map/ppermute | solution.py:31
  56.1 3.6 %copy-start.6 = (bf16[64,896]{1,0:T(8,128)(2,1)S(1)}, bf16[64,896]{1,0:T(8,128)(2,1)}, u32[]{:S(2)}) copy-start(bf16[64,896]{1,0:T(8,128)(2,1)} %copy-done.5) | copy-start | bytes 344068
  56.1 3.6 %copy-start.8 = (bf16[64,896]{1,0:T(8,128)(2,1)S(1)}, bf16[64,896]{1,0:T(8,128)(2,1)}, u32[]{:S(2)}) copy-start(bf16[64,896]{1,0:T(8,128)(2,1)} %copy-done.7) | copy-start | bytes 344068
  56.1 3.6 %copy-start.10 = (bf16[64,896]{1,0:T(8,128)(2,1)S(1)}, bf16[64,896]{1,0:T(8,128)(2,1)}, u32[]{:S(2)}) copy-start(bf16[64,896]{1,0:T(8,128)(2,1)} %copy-done.9) | copy-start | bytes 344068
  57.4 11.8 %collective-permute-start.18 = (bf16[2,512,128]{2,1,0:T(8,128)(2,1)S(1)}, bf16[2,512,128]{2,1,0:T(8,128)(2,1)S(1)}, u32[]{:S(2)}, u32[]{:S(2)}) collective-permute-start(bf16[2,512,128]{2,1,0:T(8,128)(2,1)S(1)} %get-tuple-element.80), channel_id=1, source_target_pairs={{4,0},{8,4},{12,8},{0,12},{20,16},{24,20},{28,24},{16,28},{36,32},... | collective-permute-start | bytes 786440 | tf_op jit(solution)/shard_map/ppermute | solution.py:41
  57.5 11.7 %collective-permute-start.19 = (bf16[2,512,128]{2,1,0:T(8,128)(2,1)S(1)}, bf16[2,512,128]{2,1,0:T(8,128)(2,1)S(1)}, u32[]{:S(2)}, u32[]{:S(2)}) collective-permute-start(bf16[2,512,128]{2,1,0:T(8,128)(2,1)S(1)} %get-tuple-element.81), channel_id=1, source_target_pairs={{8,0},{12,4},{0,8},{4,12},{24,16},{28,20},{16,24},{20,28},{40,32},... | collective-permute-start | bytes 786440 | tf_op jit(solution)/shard_map/ppermute | solution.py:41
  59.7 13.3 %collective-permute-start.20 = (bf16[2,512,128]{2,1,0:T(8,128)(2,1)S(1)}, bf16[2,512,128]{2,1,0:T(8,128)(2,1)S(1)}, u32[]{:S(2)}, u32[]{:S(2)}) collective-permute-start(bf16[2,512,128]{2,1,0:T(8,128)(2,1)S(1)} %get-tuple-element.82), channel_id=1, source_target_pairs={{12,0},{0,4},{4,8},{8,12},{28,16},{16,20},{20,24},{24,28},{44,32},... | collective-permute-start | bytes 786440 | tf_op jit(solution)/shard_map/ppermute | solution.py:41
  68.2 5.1 %collective-permute-start.22 = (bf16[2,512,128]{2,1,0:T(8,128)(2,1)S(1)}, bf16[2,512,128]{2,1,0:T(8,128)(2,1)S(1)}, u32[]{:S(2)}, u32[]{:S(2)}) collective-permute-start(bf16[2,512,128]{2,1,0:T(8,128)(2,1)S(1)} %get-tuple-element.94), channel_id=1, source_target_pairs={{128,0},{0,128},{129,1},{1,129},{130,2},{2,130},{131,3},{3,131},{1... | collective-permute-start | bytes 786440 | tf_op jit(solution)/shard_map/ppermute | solution.py:31
  73.5 8.6 %collective-permute-start.23 = (bf16[2,512,128]{2,1,0:T(8,128)(2,1)S(1)}, bf16[2,512,128]{2,1,0:T(8,128)(2,1)S(1)}, u32[]{:S(2)}, u32[]{:S(2)}) collective-permute-start(bf16[2,512,128]{2,1,0:T(8,128)(2,1)S(1)} %get-tuple-element.98), channel_id=1, source_target_pairs={{4,0},{8,4},{12,8},{0,12},{20,16},{24,20},{28,24},{16,28},{36,32},... | collective-permute-start | bytes 786440 | tf_op jit(solution)/shard_map/ppermute | solution.py:41
  73.7 8.4 %collective-permute-start.24 = (bf16[2,512,128]{2,1,0:T(8,128)(2,1)S(1)}, bf16[2,512,128]{2,1,0:T(8,128)(2,1)S(1)}, u32[]{:S(2)}, u32[]{:S(2)}) collective-permute-start(bf16[2,512,128]{2,1,0:T(8,128)(2,1)S(1)} %get-tuple-element.100), channel_id=1, source_target_pairs={{8,0},{12,4},{0,8},{4,12},{24,16},{28,20},{16,24},{20,28},{40,32},... | collective-permute-start | bytes 786440 | tf_op jit(solution)/shard_map/ppermute | solution.py:41
  75.0 14.1 %collective-permute-start.25 = (bf16[2,512,128]{2,1,0:T(8,128)(2,1)S(1)}, bf16[2,512,128]{2,1,0:T(8,128)(2,1)S(1)}, u32[]{:S(2)}, u32[]{:S(2)}) collective-permute-start(bf16[2,512,128]{2,1,0:T(8,128)(2,1)S(1)} %get-tuple-element.102), channel_id=1, source_target_pairs={{12,0},{0,4},{4,8},{8,12},{28,16},{16,20},{20,24},{24,28},{44,32},... | collective-permute-start | bytes 786440 | tf_op jit(solution)/shard_map/ppermute | solution.py:41
  75.3 5.2 %collective-permute-start.15 = (bf16[64,1792]{1,0:T(8,128)(2,1)S(1)}, bf16[64,1792]{1,0:T(8,128)(2,1)S(1)}, u32[]{:S(2)}, u32[]{:S(2)}) collective-permute-start(bf16[64,1792]{1,0:T(8,128)(2,1)S(1)} %get-tuple-element.85), channel_id=1, source_target_pairs={{1,0},{2,1},{3,2},{0,3},{5,4},{6,5},{7,6},{4,7},{9,8},{10,9},{11,1... | collective-permute-start | bytes 688136 | tf_op jit(solution)/shard_map/ppermute | solution.py:31
  76.4 12.9 %collective-permute-start.16 = (bf16[64,1792]{1,0:T(8,128)(2,1)S(1)}, bf16[64,1792]{1,0:T(8,128)(2,1)S(1)}, u32[]{:S(2)}, u32[]{:S(2)}) collective-permute-start(bf16[64,1792]{1,0:T(8,128)(2,1)S(1)} %get-tuple-element.87), channel_id=1, source_target_pairs={{3,0},{0,1},{1,2},{2,3},{7,4},{4,5},{5,6},{6,7},{11,8},{8,9},{9,10... | collective-permute-start | bytes 688136 | tf_op jit(solution)/shard_map/ppermute | solution.py:31
  80.4 19.5 %collective-permute-start.21 = (bf16[2,512,128]{2,1,0:T(8,128)(2,1)S(1)}, bf16[2,512,128]{2,1,0:T(8,128)(2,1)S(1)}, u32[]{:S(2)}, u32[]{:S(2)}) collective-permute-start(bf16[2,512,128]{2,1,0:T(8,128)(2,1)S(1)} %get-tuple-element.92), channel_id=1, source_target_pairs={{16,0},{20,4},{24,8},{28,12},{32,16},{36,20},{40,24},{44,28},{48,3... | collective-permute-start | bytes 786440 | tf_op jit(solution)/shard_map/ppermute | solution.py:31
  89.4 10.6 %collective-permute-start.26 = (bf16[2,512,128]{2,1,0:T(8,128)(2,1)S(1)}, bf16[2,512,128]{2,1,0:T(8,128)(2,1)S(1)}, u32[]{:S(2)}, u32[]{:S(2)}) collective-permute-start(bf16[2,512,128]{2,1,0:T(8,128)(2,1)S(1)} %get-tuple-element.103), channel_id=1, source_target_pairs={{16,0},{20,4},{24,8},{28,12},{32,16},{36,20},{40,24},{44,28},{48,3... | collective-permute-start | bytes 786440 | tf_op jit(solution)/shard_map/ppermute | solution.py:31
  91.1 7.9 %collective-permute-start.17 = (bf16[64,1792]{1,0:T(8,128)(2,1)S(1)}, bf16[64,1792]{1,0:T(8,128)(2,1)S(1)}, u32[]{:S(2)}, u32[]{:S(2)}) collective-permute-start(bf16[64,1792]{1,0:T(8,128)(2,1)S(1)} %get-tuple-element.88), channel_id=1, source_target_pairs={{2,0},{3,1},{0,2},{1,3},{6,4},{7,5},{4,6},{5,7},{10,8},{11,9},{8,1... | collective-permute-start | bytes 688136 | tf_op jit(solution)/shard_map/ppermute | solution.py:31

commit v2 on v1

--- a/solution.py
+++ b/solution.py
@@ -22,7 +22,7 @@
 ATTEND_VMEM = 24 * 1024 * 1024
 SMALL_VMEM = 8 * 1024 * 1024
 
-TP, SECTION, LENGTH, OWNER, VISIBLE = 0, 1, 2, 3, 4
+TP, SECTION, LENGTH, VISIBLE = 0, 1, 2, 3
 
 
 def shifted(block, axis, distance):
@@ -83,13 +83,14 @@
             send[...] = own[...]
 
 
-def pick_kernel(which, *refs):
-    choices, chosen = refs[:-1], refs[-1]
-    for offset, choice in enumerate(choices):
-
-        @pl.when(which[0] == offset)
-        def _(choice=choice):
-            chosen[...] = choice[...]
+def pick_kernel(first, second, *refs):
+    choices, chosen = refs[:WIN], refs[WIN:]
+    for which, target in zip((first, second), chosen):
+        for offset, choice in enumerate(choices):
+
+            @pl.when(which[0] == offset)
+            def _(choice=choice, target=target):
+                target[...] = choice[...]
 
 
 def pack_kernel(meta, queries, grad_out, keys, values, *packs):
@@ -141,7 +142,7 @@
 def attend_kernel(chunk, tp_count, meta, *refs):
     packs, refs = refs[:tp_count], refs[tp_count:]
     earlier, refs = refs[: tp_count if chunk else 0], refs[tp_count if chunk else 0 :]
-    offers, other, refs = refs[:WIN], refs[WIN], refs[WIN + 1 :]
+    (own, other), refs = refs[:2], refs[2:]
     backs, refs = refs[:tp_count], refs[tp_count:]
     own_grad, other_grad = refs[:2]
     q_all, do_all, keys, values, keys_t, bias, scores, grad_prob, weights, grad_scores, dk, dv = refs[
@@ -155,7 +156,7 @@
     total = prompt_len + resp
     per_half = half // PTILE
     q_cols = kv_heads * PER_KV * HEAD_DIM
-    tp, section, length, owner = meta[TP], meta[SECTION], meta[LENGTH], meta[OWNER]
+    tp, section, length = meta[TP], meta[SECTION], meta[LENGTH]
     taken = chunk * 2 * (q_cols + k_cols)
     given = chunk * (q_cols + 2 * k_cols)
     for back, block in zip(backs, earlier):
@@ -176,13 +177,8 @@
     nt = (((1,), (1,)), ((), ()))
     for kv in range(kv_heads):
         at = slice(kv * HEAD_DIM, (kv + 1) * HEAD_DIM)
-        for offset, offer in enumerate(offers):
-
-            @pl.when(owner == offset)
-            def _(offer=offer):
-                keys[:half] = offer[0, :, at]
-                values[:half] = offer[1, :, at]
-
+        keys[:half] = own[0, :, at]
+        values[:half] = own[1, :, at]
         keys[half:prompt_len] = other[0, :, at]
         values[half:prompt_len] = other[1, :, at]
         for i in range(tp_count):
@@ -196,56 +192,58 @@
                 q_all[head, here] = packs[i][:, q_from : q_from + HEAD_DIM]
                 do_all[head, here] = packs[i][:, q_cols + q_from : q_cols + q_from + HEAD_DIM]
         keys_t[...] = keys[...].T
-        dk[...] = jnp.zeros_like(dk)
-        dv[...] = jnp.zeros_like(dv)
-
+
+        def products(head, tile):
+            span = slice(tile * PTILE, (tile + 1) * PTILE)
+            part = lax.dot_general(
+                keys[span], q_all[head], nt, preferred_element_type=jnp.float32
+            )
+            if tile >= 2 * per_half:
+                low = tile * PTILE - prompt_len
+                part = part + bias[low : low + PTILE]
+            scores[head % 2, span] = part
+            grad_prob[head % 2, span] = lax.dot_general(
+                values[span], do_all[head], nt, preferred_element_type=jnp.float32
+            )
+            top = jnp.max(part.reshape(PTILE // 8, 8, resp), axis=0)
+            return top + tile_bias[tile] if tile < 2 * per_half else top
+
+        tiles = total // PTILE
+        tops = [products(0, tile) for tile in range(tiles)]
         for head in range(PER_KV):
-            query = q_all[head]
-            cotangent = do_all[head]
-            tops = []
-            for tile in range(total // PTILE):
+            buf = head % 2
+            largest = jnp.max(functools.reduce(jnp.maximum, tops), axis=0, keepdims=True)
+            sums, dots, tops = [], [], []
+            for tile in range(tiles):
                 span = slice(tile * PTILE, (tile + 1) * PTILE)
-                part = lax.dot_general(
-                    keys[span], query, nt, preferred_element_type=jnp.float32
-                )
-                if tile >= 2 * per_half:
-                    low = (tile - 2 * per_half) * PTILE
-                    part = part + bias[low : low + PTILE]
-                scores[span] = part
-                top = jnp.max(part.reshape(PTILE // 8, 8, resp), axis=0)
-                if tile < 2 * per_half:
-                    top = top + tile_bias[tile]
-                tops.append(top)
-                grad_prob[span] = lax.dot_general(
-                    values[span], cotangent, nt, preferred_element_type=jnp.float32
-                )
-            largest = jnp.max(functools.reduce(jnp.maximum, tops), axis=0, keepdims=True)
-            factor = SCALING * LOG2E
-            sums = jnp.zeros((8, resp), jnp.float32)
-            dots = jnp.zeros((8, resp), jnp.float32)
-            for tile in range(total // PTILE):
+                shift = largest - tile_bias[tile] if tile < 2 * per_half else largest
+                exponent = jnp.exp2((scores[buf, span] - shift) * (SCALING * LOG2E))
+                scores[buf, span] = exponent
+                sums.append(jnp.sum(exponent.reshape(PTILE // 8, 8, resp), axis=0))
+                weighed = exponent * grad_prob[buf, span]
+                dots.append(jnp.sum(weighed.reshape(PTILE // 8, 8, resp), axis=0))
+                if head + 1 < PER_KV:
+                    tops.append(products(head + 1, tile))
+            inverse = 1.0 / jnp.sum(functools.reduce(jnp.add, sums), axis=0, keepdims=True)
+            row_delta = (
+                jnp.sum(functools.reduce(jnp.add, dots), axis=0, keepdims=True) * inverse
+            )
+            inverse = inverse * live
+            for tile in range(tiles):
                 span = slice(tile * PTILE, (tile + 1) * PTILE)
-                shift = largest
-                if tile < 2 * per_half:
-                    shift = shift - tile_bias[tile]
-                exponent = jnp.exp2((scores[span] - shift) * factor)
-                scores[span] = exponent
-                sums += jnp.sum(exponent.reshape(PTILE // 8, 8, resp), axis=0)
-                dots += jnp.sum((exponent * grad_prob[span]).reshape(PTILE // 8, 8, resp), axis=0)
-            inverse = 1.0 / jnp.sum(sums, axis=0, keepdims=True)
-            row_delta = jnp.sum(dots, axis=0, keepdims=True) * inverse
-            inverse = inverse * live
-            for tile in range(total // PTILE):
-                span = slice(tile * PTILE, (tile + 1) * PTILE)
-                probabilities = scores[span] * inverse
-                weights[span] = probabilities.astype(jnp.bfloat16)
-                grad_scores[span] = (probabilities * (grad_prob[span] - row_delta)).astype(
-                    jnp.bfloat16
-                )
-            dv[...] += jnp.dot(weights[...], cotangent, preferred_element_type=jnp.float32)
-            dk[...] += jnp.dot(grad_scores[...], query, preferred_element_type=jnp.float32)
+                probabilities = scores[buf, span] * inverse
+                weights[buf, span] = probabilities.astype(jnp.bfloat16)
+                grad_scores[buf, span] = (
+                    probabilities * (grad_prob[buf, span] - row_delta)
+                ).astype(jnp.bfloat16)
+            for target, left, right in (
+                (dv, weights, do_all),
+                (dk, grad_scores, q_all),
+            ):
+                product = jnp.dot(left[buf], right[head], preferred_element_type=jnp.float32)
+                target[...] = product if head == 0 else target[...] + product
             grad_query_t = jnp.dot(
-                keys_t[...], grad_scores[...], preferred_element_type=jnp.float32
+                keys_t[...], grad_scores[buf], preferred_element_type=jnp.float32
             )
             grad_query = (grad_query_t.T * SCALING).astype(jnp.bfloat16)
             q_from = given + (kv * PER_KV + head) * HEAD_DIM
@@ -264,7 +262,7 @@
             backs[i][:, v_from : v_from + HEAD_DIM] = dv[span].astype(jnp.bfloat16)
 
 
-def attend(chunk, meta, packs, earlier, offers, other):
+def attend(chunk, meta, packs, earlier, own, other):
     tp_count, rows = len(packs), packs[0].shape[0]
     resp = rows * tp_count
     half, k_cols = other.shape[1:]
@@ -280,7 +278,7 @@
         ]
         * tp_count
         + [jax.ShapeDtypeStruct(other.shape, bf16)] * 2,
-        in_specs=[scalars()] + [whole()] * (tp_count + len(earlier) + len(offers) + 1),
+        in_specs=[scalars()] + [whole()] * (tp_count + len(earlier) + 2),
         out_specs=[whole()] * (tp_count + 2),
         scratch_shapes=[
             pltpu.VMEM((PER_KV, resp, HEAD_DIM), bf16),
@@ -289,10 +287,10 @@
             pltpu.VMEM((total, HEAD_DIM), bf16),
             pltpu.VMEM((HEAD_DIM, total), bf16),
             pltpu.VMEM((resp, resp), f32),
-            pltpu.VMEM((total, resp), f32),
-            pltpu.VMEM((total, resp), f32),
-            pltpu.VMEM((total, resp), bf16),
-            pltpu.VMEM((total, resp), bf16),
+            pltpu.VMEM((2, total, resp), f32),
+            pltpu.VMEM((2, total, resp), f32),
+            pltpu.VMEM((2, total, resp), bf16),
+            pltpu.VMEM((2, total, resp), bf16),
             pltpu.VMEM((total, HEAD_DIM), f32),
             pltpu.VMEM((total, HEAD_DIM), f32),
         ],
@@ -301,7 +299,7 @@
             flops=8 * flops, bytes_accessed=6 * 1024 * 1024, transcendentals=flops // 1280
         ),
         name="attend",
-    )(meta, *packs, *earlier, *offers, other)
+    )(meta, *packs, *earlier, own, other)
     return results[:tp_count], results[tp_count], results[tp_count + 1]
 
 
@@ -326,7 +324,7 @@
         [scalars(), whole()],
     )(section, prompt_kv)
     sibling_owner = shifted(after(owners, halves), "section", 1)
-    meta = jnp.concatenate([tp, section, lengths, owners, visible_tiles[0]])
+    meta = jnp.concatenate([tp, section, lengths, visible_tiles[0]])
     meta = after(meta, sibling_owner)
     packs = small_call(
         pack_kernel,
@@ -361,12 +359,11 @@
 
     backs, shares, passing, ringed, terms = [], [], [], {}, []
     for c in range(CHUNKS):
-        wanted = small_call(pick_kernel, "pick", part, [scalars()] + [whole()] * WIN)(
-            sibling_owner, *offers[c]
-        )
-        other = shifted(wanted, "section", 1)
-        other = after(other, terms)
-        backs, own_grad, other_grad = attend(c, meta, arrived, backs, offers[c], other)
+        wanted, own = small_call(
+            pick_kernel, "pick", [part] * 2, [scalars()] * 2 + [whole()] * WIN
+        )(sibling_owner, owners, *offers[c])
+        other = after(shifted(wanted, "section", 1), terms)
+        backs, own_grad, other_grad = attend(c, meta, arrived, backs, own, other)
         if c == CHUNKS - 1:
             returned = {d: shifted(backs[d], "tp", -d) for d in range(1, tp_count, 2)}
             for d in range(2, tp_count, 2):
@@ -394,6 +391,14 @@
         passing.append(passed)
         shares += [kept, passed]
 
+    shares[1] = to_row(after(shares[1], returned[1]), -1)
+    shares[3] = to_row(shares[3], -1)
+    prompt_grads = small_call(
+        finish_kernel,
+        "finish",
+        jax.ShapeDtypeStruct((1, 2, half, prompt_kv.shape[3]), bf16),
+        [whole()] * len(shares),
+    )(*shares)
     grads = small_call(
         unpack_kernel,
         "unpack",
@@ -403,15 +408,7 @@
             jax.ShapeDtypeStruct(resp_values.shape, bf16),
         ],
         [scalars()] + [whole()] * tp_count,
-    )(tp, backs[0], *[returned[d] for d in range(1, tp_count)])
-    shares[1] = to_row(after(shares[1], returned[1]), -1)
-    shares[3] = to_row(shares[3], -1)
-    prompt_grads = small_call(
-        finish_kernel,
-        "finish",
-        jax.ShapeDtypeStruct((1, 2, half, prompt_kv.shape[3]), bf16),
-        [whole()] * len(shares),
-    )(*shares)
+    )(after(tp, prompt_grads), backs[0], *[returned[d] for d in range(1, tp_count)])
     return (grads[0], grads[1], grads[2], prompt_grads)
 
 

time: 101 us -> 97.4 us (0.964)
  the two profiles are of different devices: /device:TPU:1 before, /device:TPU:24 now
where the time goes in v2:
time: 97.4 us; the launch traced here: 97.1 us
  starting transfers between devices  33.9 us (35%)
  waiting for transfers between devices  32.1 us (33%)
  Pallas kernels  19.6 us (20%)
  local copies, waits for them, and re-layouts  4.9 us (5%)
  between operations  4.45 us (5%)
  other arithmetic  2.19 us (2%)
    ppermute x15, waiting for transfers between devices, shifted(): return lax.ppermute(block, axis, route)  20.5 us
    ppermute x15, starting transfers between devices, shifted(): return lax.ppermute(block, axis, route)  18.1 us
    ppermute x12, starting transfers between devices, along_row(): return lax.ppermute(block, 'group', route)  15.8 us
    pallas_call x2, Pallas kernels, attend(): pl.pallas_call(functools.partial(attend_kernel, chunk, tp_count), out_sha...  13.7 us
    ppermute x12, waiting for transfers between devices, along_row(): return lax.ppermute(block, 'group', route)  11.6 us
    unnamed x24, local copies, waits for them, and re-layouts  4.9 us
  transfers between devices with their start and end apart: 27, of which 11 were waited for; matrix products, arithmetic and copies ran while one was open for 2% of the time, Pallas kernels for 19%

profile of v2, /device:TPU:24, one launch (start us, length us, event | category | flops | bytes accessed | tf_op | source)
XLA Modules:
  0.0 97.1 jit_solution(12679820530276559924)
XLA Ops:
  0.6 1.2 %copy-done = bf16[1,2,1024,256]{3,2,1,0:T(8,128)(2,1)S(1)} copy-done((bf16[1,2,1024,256]{3,2,1,0:T(8,128)(2,1)S(1)}, bf16[1,2,1024,256]{3,2,1,0:T(8,128)(2,1)}, u32[]{:S(2)}) %copy-start) | copy-done | bytes 1048600
  2.0 2.0 %collective-permute-start.4 = (bf16[2,512,128]{2,1,0:T(8,128)(2,1)S(1)}, bf16[2,512,128]{2,1,0:T(8,128)(2,1)S(1)}, u32[]{:S(2)}, u32[]{:S(2)}) collective-permute-start(bf16[2,512,128]{2,1,0:T(8,128)(2,1)S(1)} %get-tuple-element.59.own.refs_0_), channel_id=1, source_target_pairs={{112,0},{116,4},{120,8},{124,12},{0,16},{4,20},{8,24},{12,28},{16,... | collective-permute-start | bytes 786440 | tf_op jit(solution)/shard_map/ppermute | solution.py:31
  4.6 0.6 copy-done.11
  5.4 1.1 %copy-done.2 = bf16[64,5120]{1,0:T(8,128)(2,1)S(1)} copy-done((bf16[64,5120]{1,0:T(8,128)(2,1)S(1)}, bf16[64,5120]{1,0:T(8,128)(2,1)}, u32[]{:S(2)}) %copy-start.2) | copy-done | bytes 655384
  6.5 1.6 %pack.1 = (bf16[64,3072]{1,0:T(8,128)(2,1)S(1)}, bf16[64,3072]{1,0:T(8,128)(2,1)}, bf16[64,3072]{1,0:T(8,128)(2,1)S(1)}, bf16[64,3072]{1,0:T(8,128)(2,1)}) custom-call(s32[11]{0:T(128)S(1)} %pad_add_fusion.meta, bf16[64,5120]{1,0:T(8,128)(2,1)S(1)} %copy-done.1, bf16[64,5120]{1,0:T(8,128)(2,1)S(1)} %copy-done.2, bf16[64,1024]{1,0:T(8,128)(2,1)S(1)} %copy-done.3, ...), custom_call_target="tpu_custom_call" | custom-call | tf_op jit(solution)/shard_map/pack/pallas_call | solution.py:329
  8.0 1.5 %collective-permute-start.1 = (bf16[64,3072]{1,0:T(8,128)(2,1)}, bf16[64,3072]{1,0:T(8,128)(2,1)S(1)}, u32[]{:S(2)}, u32[]{:S(2)}) collective-permute-start(bf16[64,3072]{1,0:T(8,128)(2,1)} %get-tuple-element.64), channel_id=1, source_target_pairs={{3,0},{0,1},{1,2},{2,3},{7,4},{4,5},{5,6},{6,7},{11,8},{8,9},{9,10... | collective-permute-start | bytes 1179656 | tf_op jit(solution)/shard_map/ppermute | solution.py:31
  9.5 1.7 %collective-permute-start.2 = (bf16[64,3072]{1,0:T(8,128)(2,1)}, bf16[64,3072]{1,0:T(8,128)(2,1)S(1)}, u32[]{:S(2)}, u32[]{:S(2)}) collective-permute-start(bf16[64,3072]{1,0:T(8,128)(2,1)} %get-tuple-element.66), channel_id=1, source_target_pairs={{1,0},{2,1},{3,2},{0,3},{5,4},{6,5},{7,6},{4,7},{9,8},{10,9},{11,1... | collective-permute-start | bytes 1179656 | tf_op jit(solution)/shard_map/ppermute | solution.py:31
  11.3 2.9 %collective-permute-done.4.before = bf16[2,512,128]{2,1,0:T(8,128)(2,1)S(1)} collective-permute-done((bf16[2,512,128]{2,1,0:T(8,128)(2,1)S(1)}, bf16[2,512,128]{2,1,0:T(8,128)(2,1)S(1)}, u32[]{:S(2)}, u32[]{:S(2)}) %collective-permute-start.4) | collective-permute-done | bytes 262176 | tf_op jit(solution)/shard_map/ppermute | solution.py:31
  14.3 0.3 collective-permute-start.5
  14.6 2.6 %collective-permute-start.6 = (bf16[2,512,128]{2,1,0:T(8,128)(2,1)S(1)}, bf16[2,512,128]{2,1,0:T(8,128)(2,1)S(1)}, u32[]{:S(2)}, u32[]{:S(2)}) collective-permute-start(bf16[2,512,128]{2,1,0:T(8,128)(2,1)S(1)} %get-tuple-element.70), channel_id=1, source_target_pairs={{8,0},{12,4},{0,8},{4,12},{24,16},{28,20},{16,24},{20,28},{40,32},... | collective-permute-start | bytes 786440 | tf_op jit(solution)/shard_map/ppermute | solution.py:41
  17.2 3.8 %collective-permute-done.1.refs_1_ = bf16[64,3072]{1,0:T(8,128)(2,1)S(1)} collective-permute-done((bf16[64,3072]{1,0:T(8,128)(2,1)}, bf16[64,3072]{1,0:T(8,128)(2,1)S(1)}, u32[]{:S(2)}, u32[]{:S(2)}) %collective-permute-start.1) | collective-permute-done | bytes 393248 | tf_op jit(solution)/shard_map/ppermute | solution.py:31
  21.0 2.7 %collective-permute-start.3 = (bf16[64,3072]{1,0:T(8,128)(2,1)S(1)}, bf16[64,3072]{1,0:T(8,128)(2,1)S(1)}, u32[]{:S(2)}, u32[]{:S(2)}) collective-permute-start(bf16[64,3072]{1,0:T(8,128)(2,1)S(1)} %get-tuple-element.67), channel_id=1, source_target_pairs={{2,0},{3,1},{0,2},{1,3},{6,4},{7,5},{4,6},{5,7},{10,8},{11,9},{8,1... | collective-permute-start | bytes 1179656 | tf_op jit(solution)/shard_map/ppermute | solution.py:31
  23.7 1.9 %collective-permute-start.13 = (bf16[2,512,128]{2,1,0:T(8,128)(2,1)S(1)}, bf16[2,512,128]{2,1,0:T(8,128)(2,1)S(1)}, u32[]{:S(2)}, u32[]{:S(2)}) collective-permute-start(bf16[2,512,128]{2,1,0:T(8,128)(2,1)S(1)} %get-tuple-element.60.own.refs_0_), channel_id=1, source_target_pairs={{112,0},{116,4},{120,8},{124,12},{0,16},{4,20},{8,24},{12,28},{16,... | collective-permute-start | bytes 786440 | tf_op jit(solution)/shard_map/ppermute | solution.py:31
  26.3 2.8 %collective-permute-done.7.refs_3_ = bf16[2,512,128]{2,1,0:T(8,128)(2,1)S(1)} collective-permute-done((bf16[2,512,128]{2,1,0:T(8,128)(2,1)S(1)}, bf16[2,512,128]{2,1,0:T(8,128)(2,1)S(1)}, u32[]{:S(2)}, u32[]{:S(2)}) %collective-permute-start.7) | collective-permute-done | bytes 262176 | tf_op jit(solution)/shard_map/ppermute | solution.py:41
  29.1 0.7 pick.2
  29.8 3.5 %collective-permute-done.13.before = bf16[2,512,128]{2,1,0:T(8,128)(2,1)S(1)} collective-permute-done((bf16[2,512,128]{2,1,0:T(8,128)(2,1)S(1)}, bf16[2,512,128]{2,1,0:T(8,128)(2,1)S(1)}, u32[]{:S(2)}, u32[]{:S(2)}) %collective-permute-start.13) | collective-permute-done | bytes 262176 | tf_op jit(solution)/shard_map/ppermute | solution.py:31
  33.4 0.9 sends.3
  34.4 2.6 %collective-permute-start.15 = (bf16[2,512,128]{2,1,0:T(8,128)(2,1)}, bf16[2,512,128]{2,1,0:T(8,128)(2,1)S(1)}, u32[]{:S(2)}, u32[]{:S(2)}) collective-permute-start(bf16[2,512,128]{2,1,0:T(8,128)(2,1)} %get-tuple-element.87), channel_id=1, source_target_pairs={{8,0},{12,4},{0,8},{4,12},{24,16},{28,20},{16,24},{20,28},{40,32},... | collective-permute-start | bytes 786440 | tf_op jit(solution)/shard_map/ppermute | solution.py:41
  37.0 6.8 %attend.2 = (bf16[64,896]{1,0:T(8,128)(2,1)S(1)}, bf16[64,896]{1,0:T(8,128)(2,1)S(1)}, bf16[64,896]{1,0:T(8,128)(2,1)S(1)}, bf16[64,896]{1,0:T(8,128)(2,1)S(1)},...) custom-call(s32[11]{0:T(128)S(1)} %pad_add_fusion.meta, ...), custom_call_target="tpu_custom_call" | custom-call | flops 16777216000 | bytes 6291456 | tf_op jit(solution)/shard_map/attend/pallas_call | solution.py:274
  43.9 0.6 copy-done.5
  44.5 0.6 copy-done.7
  45.2 0.6 copy-done.9
  48.2 0.7 pick.3
  48.9 0.5 collective-permute-start.17
  49.4 1.3 %fusion.18 = (bf16[2,512,128]{2,1,0:T(8,128)(2,1)S(1)}, bf16[2,512,128]{2,1,0:T(8,128)(2,1)S(1)}, bf16[2,512,128]{2,1,0:T(8,128)(2,1)S(1)}, f32[2,512,128]{2,1,0:T(8,128)S(1)}) fusion(bf16[2,512,128]{2,1,0:T(8,128)(2,1)S(1)} %get-tuple-element.74, bf16[2,512,128]{2,1,0:T(8,128)(2,1)} %collective-permute-done.9, pred[]{:T(512)} %bitcast.11, pred[]{:T(512)} %bitcast.10, ...), kind=kLoop, calls=%fused_computation.46 | loop fusion | flops 2228224 | bytes 1835016 | tf_op jit(solution)/shard_map/convert_element_type | solution.py:377
  50.7 1.0 %collective-permute-start.10 = (bf16[2,512,128]{2,1,0:T(8,128)(2,1)S(1)}, bf16[2,512,128]{2,1,0:T(8,128)(2,1)S(1)}, u32[]{:S(2)}, u32[]{:S(2)}) collective-permute-start(bf16[2,512,128]{2,1,0:T(8,128)(2,1)S(1)} %get-tuple-element.77), channel_id=1, source_target_pairs={{4,0},{8,4},{12,8},{0,12},{20,16},{24,20},{28,24},{16,28},{36,32},... | collective-permute-start | bytes 786440 | tf_op jit(solution)/shard_map/ppermute | solution.py:41
  51.7 3.8 %collective-permute-start.11 = (bf16[2,512,128]{2,1,0:T(8,128)(2,1)S(1)}, bf16[2,512,128]{2,1,0:T(8,128)(2,1)S(1)}, u32[]{:S(2)}, u32[]{:S(2)}) collective-permute-start(bf16[2,512,128]{2,1,0:T(8,128)(2,1)S(1)} %get-tuple-element.78), channel_id=1, source_target_pairs={{8,0},{12,4},{0,8},{4,12},{24,16},{28,20},{16,24},{20,28},{40,32},... | collective-permute-start | bytes 786440 | tf_op jit(solution)/shard_map/ppermute | solution.py:41
  55.5 1.3 %collective-permute-start.12 = (bf16[2,512,128]{2,1,0:T(8,128)(2,1)S(1)}, bf16[2,512,128]{2,1,0:T(8,128)(2,1)S(1)}, u32[]{:S(2)}, u32[]{:S(2)}) collective-permute-start(bf16[2,512,128]{2,1,0:T(8,128)(2,1)S(1)} %get-tuple-element.79), channel_id=1, source_target_pairs={{12,0},{0,4},{4,8},{8,12},{28,16},{16,20},{20,24},{24,28},{44,32},... | collective-permute-start | bytes 786440 | tf_op jit(solution)/shard_map/ppermute | solution.py:41
  56.8 6.9 %attend.3 = (bf16[64,1792]{1,0:T(8,128)(2,1)S(1)}, bf16[64,1792]{1,0:T(8,128)(2,1)S(1)}, bf16[64,1792]{1,0:T(8,128)(2,1)S(1)}, bf16[64,1792]{1,0:T(8,128)(2,1)S(...) custom-call(s32[11]{0:T(128)S(1)} %pad_add_fusion.meta, ...), custom_call_target="tpu_custom_call" | custom-call | flops 16777216000 | bytes 6291456 | tf_op jit(solution)/shard_map/attend/pallas_call | solution.py:274
  63.8 3.5 %collective-permute-done.11 = bf16[2,512,128]{2,1,0:T(8,128)(2,1)S(1)} collective-permute-done((bf16[2,512,128]{2,1,0:T(8,128)(2,1)S(1)}, bf16[2,512,128]{2,1,0:T(8,128)(2,1)S(1)}, u32[]{:S(2)}, u32[]{:S(2)}) %collective-permute-start.11) | collective-permute-done | bytes 262176 | tf_op jit(solution)/shard_map/ppermute | solution.py:41
  67.3 0.3 fusion.5
  67.6 0.3 fusion.25
  67.9 2.2 %collective-permute-start.23 = (bf16[2,512,128]{2,1,0:T(8,128)(2,1)S(1)}, bf16[2,512,128]{2,1,0:T(8,128)(2,1)S(1)}, u32[]{:S(2)}, u32[]{:S(2)}) collective-permute-start(bf16[2,512,128]{2,1,0:T(8,128)(2,1)S(1)} %get-tuple-element.104), channel_id=1, source_target_pairs={{12,0},{0,4},{4,8},{8,12},{28,16},{16,20},{20,24},{24,28},{44,32},... | collective-permute-start | bytes 786440 | tf_op jit(solution)/shard_map/ppermute | solution.py:41
  70.2 1.1 %collective-permute-start.22 = (bf16[2,512,128]{2,1,0:T(8,128)(2,1)S(1)}, bf16[2,512,128]{2,1,0:T(8,128)(2,1)S(1)}, u32[]{:S(2)}, u32[]{:S(2)}) collective-permute-start(bf16[2,512,128]{2,1,0:T(8,128)(2,1)S(1)} %get-tuple-element.102), channel_id=1, source_target_pairs={{8,0},{12,4},{0,8},{4,12},{24,16},{28,20},{16,24},{20,28},{40,32},... | collective-permute-start | bytes 786440 | tf_op jit(solution)/shard_map/ppermute | solution.py:41
  71.3 0.6 collective-permute-start.21
  71.9 1.4 %collective-permute-start.18 = (bf16[64,1792]{1,0:T(8,128)(2,1)S(1)}, bf16[64,1792]{1,0:T(8,128)(2,1)S(1)}, u32[]{:S(2)}, u32[]{:S(2)}) collective-permute-start(bf16[64,1792]{1,0:T(8,128)(2,1)S(1)} %get-tuple-element.93), channel_id=1, source_target_pairs={{1,0},{2,1},{3,2},{0,3},{5,4},{6,5},{7,6},{4,7},{9,8},{10,9},{11,1... | collective-permute-start | bytes 688136 | tf_op jit(solution)/shard_map/ppermute | solution.py:31
  73.4 0.6 collective-permute-start.24
  74.0 4.1 %collective-permute-done.18.refs_1_ = bf16[64,1792]{1,0:T(8,128)(2,1)S(1)} collective-permute-done((bf16[64,1792]{1,0:T(8,128)(2,1)S(1)}, bf16[64,1792]{1,0:T(8,128)(2,1)S(1)}, u32[]{:S(2)}, u32[]{:S(2)}) %collective-permute-start.18) | collective-permute-done | bytes 229408 | tf_op jit(solution)/shard_map/ppermute | solution.py:31
  78.1 1.9 %collective-permute-start.19 = (bf16[2,512,128]{2,1,0:T(8,128)(2,1)S(1)}, bf16[2,512,128]{2,1,0:T(8,128)(2,1)S(1)}, u32[]{:S(2)}, u32[]{:S(2)}) collective-permute-start(bf16[2,512,128]{2,1,0:T(8,128)(2,1)S(1)} %get-tuple-element.94), channel_id=1, source_target_pairs={{16,0},{20,4},{24,8},{28,12},{32,16},{36,20},{40,24},{44,28},{48,3... | collective-permute-start | bytes 786440 | tf_op jit(solution)/shard_map/ppermute | solution.py:31
  80.0 1.5 %collective-permute-done.23 = bf16[2,512,128]{2,1,0:T(8,128)(2,1)S(1)} collective-permute-done((bf16[2,512,128]{2,1,0:T(8,128)(2,1)S(1)}, bf16[2,512,128]{2,1,0:T(8,128)(2,1)S(1)}, u32[]{:S(2)}, u32[]{:S(2)}) %collective-permute-start.23) | collective-permute-done | bytes 262176 | tf_op jit(solution)/shard_map/ppermute | solution.py:41
  81.5 3.6 %collective-permute-done.21 = bf16[2,512,128]{2,1,0:T(8,128)(2,1)S(1)} collective-permute-done((bf16[2,512,128]{2,1,0:T(8,128)(2,1)S(1)}, bf16[2,512,128]{2,1,0:T(8,128)(2,1)S(1)}, u32[]{:S(2)}, u32[]{:S(2)}) %collective-permute-start.21) | collective-permute-done | bytes 262176 | tf_op jit(solution)/shard_map/ppermute | solution.py:41
  85.1 0.3 fusion.11
  85.4 2.0 %collective-permute-start.25 = (bf16[2,512,128]{2,1,0:T(8,128)(2,1)S(1)}, bf16[2,512,128]{2,1,0:T(8,128)(2,1)S(1)}, u32[]{:S(2)}, u32[]{:S(2)}) collective-permute-start(bf16[2,512,128]{2,1,0:T(8,128)(2,1)S(1)} %get-tuple-element.106), channel_id=1, source_target_pairs={{16,0},{20,4},{24,8},{28,12},{32,16},{36,20},{40,24},{44,28},{48,3... | collective-permute-start | bytes 786440 | tf_op jit(solution)/shard_map/ppermute | solution.py:31
  87.4 1.6 %collective-permute-start.26 = (bf16[64,1792]{1,0:T(8,128)(2,1)S(1)}, bf16[64,1792]{1,0:T(8,128)(2,1)S(1)}, u32[]{:S(2)}, u32[]{:S(2)}) collective-permute-start(bf16[64,1792]{1,0:T(8,128)(2,1)S(1)} %get-tuple-element.110), channel_id=1, source_target_pairs={{2,0},{3,1},{0,2},{1,3},{6,4},{7,5},{4,6},{5,7},{10,8},{11,9},{8,1... | collective-permute-start | bytes 688136 | tf_op jit(solution)/shard_map/ppermute | solution.py:31
  89.0 4.6 %collective-permute-done.25.refs_3_ = bf16[2,512,128]{2,1,0:T(8,128)(2,1)S(1)} collective-permute-done((bf16[2,512,128]{2,1,0:T(8,128)(2,1)S(1)}, bf16[2,512,128]{2,1,0:T(8,128)(2,1)S(1)}, u32[]{:S(2)}, u32[]{:S(2)}) %collective-permute-start.25) | collective-permute-done | bytes 262176 | tf_op jit(solution)/shard_map/ppermute | solution.py:31
  93.6 0.9 finish.1
  94.5 1.5 %collective-permute-done.26.refs_2_ = bf16[64,1792]{1,0:T(8,128)(2,1)S(1)} collective-permute-done((bf16[64,1792]{1,0:T(8,128)(2,1)S(1)}, bf16[64,1792]{1,0:T(8,128)(2,1)S(1)}, u32[]{:S(2)}, u32[]{:S(2)}) %collective-permute-start.26) | collective-permute-done | bytes 229408 | tf_op jit(solution)/shard_map/ppermute | solution.py:31
  96.1 1.0 %unpack.1 = (bf16[64,5120]{1,0:T(8,128)(2,1)}, bf16[64,1024]{1,0:T(8,128)(2,1)}, bf16[64,1024]{1,0:T(8,128)(2,1)}) custom-call(s32[1]{0:T(128)} %bitcast.tp, bf16[64,1792]{1,0:T(8,128)(2,1)S(1)} %get-tuple-element.108.refs_0_, bf16[64,1792]{1,0:T(8,128)(2,1)S(1)} %collective-permute-done.18.refs_1_, bf16[64,1792]{1,0:T(8,128)(2,1)S(1)} %collective-permute-done.26.refs_2_, ...), custom_call_target="tpu_custom_call" | custom-call | tf_op jit(solution)/shard_map/unpack/pallas_call | solution.py:402
  (45 shorter events, 0.9 us)
Async XLA Ops:
  0.6 1.2 %copy-start = (bf16[1,2,1024,256]{3,2,1,0:T(8,128)(2,1)S(1)}, bf16[1,2,1024,256]{3,2,1,0:T(8,128)(2,1)}, u32[]{:S(2)}) copy-start(bf16[1,2,1024,256]{3,2,1,0:T(8,128)(2,1)} %prompt.1) | copy-start | bytes 3145732
  1.9 3.5 %copy-start.1 = (bf16[64,5120]{1,0:T(8,128)(2,1)S(1)}, bf16[64,5120]{1,0:T(8,128)(2,1)}, u32[]{:S(2)}) copy-start(bf16[64,5120]{1,0:T(8,128)(2,1)} %queries.1) | copy-start | bytes 1966084
  1.9 3.5 %copy-start.3 = (bf16[64,1024]{1,0:T(8,128)(2,1)S(1)}, bf16[64,1024]{1,0:T(8,128)(2,1)}, u32[]{:S(2)}) copy-start(bf16[64,1024]{1,0:T(8,128)(2,1)} %keys.1) | copy-start | bytes 393220
  1.9 3.5 %copy-start.4 = (bf16[64,1024]{1,0:T(8,128)(2,1)S(1)}, bf16[64,1024]{1,0:T(8,128)(2,1)}, u32[]{:S(2)}) copy-start(bf16[64,1024]{1,0:T(8,128)(2,1)} %values.1) | copy-start | bytes 393220
  2.0 12.2 %collective-permute-start.4 = (bf16[2,512,128]{2,1,0:T(8,128)(2,1)S(1)}, bf16[2,512,128]{2,1,0:T(8,128)(2,1)S(1)}, u32[]{:S(2)}, u32[]{:S(2)}) collective-permute-start(bf16[2,512,128]{2,1,0:T(8,128)(2,1)S(1)} %get-tuple-element.59.own.refs_0_), channel_id=1, source_target_pairs={{112,0},{116,4},{120,8},{124,12},{0,16},{4,20},{8,24},{12,28},{16,... | collective-permute-start | bytes 786440 | tf_op jit(solution)/shard_map/ppermute | solution.py:31
  4.0 1.4 %collective-permute-start = (s32[1]{0:T(128)}, s32[1]{0:T(128)}, u32[]{:S(2)}, u32[]{:S(2)}) collective-permute-start(s32[1]{0:T(128)} %param.14), channel_id=1, source_target_pairs={{128,0},{0,128},{129,1},{1,129},{130,2},{2,130},{131,3},{3,131},{1... | collective-permute-start | bytes 20 | tf_op jit(solution)/shard_map/ppermute | solution.py:31
  4.6 0.7 copy-start.11
  5.4 1.1 %copy-start.2 = (bf16[64,5120]{1,0:T(8,128)(2,1)S(1)}, bf16[64,5120]{1,0:T(8,128)(2,1)}, u32[]{:S(2)}) copy-start(bf16[64,5120]{1,0:T(8,128)(2,1)} %grad_out.1) | copy-start | bytes 1966084
  8.0 12.9 %collective-permute-start.1 = (bf16[64,3072]{1,0:T(8,128)(2,1)}, bf16[64,3072]{1,0:T(8,128)(2,1)S(1)}, u32[]{:S(2)}, u32[]{:S(2)}) collective-permute-start(bf16[64,3072]{1,0:T(8,128)(2,1)} %get-tuple-element.64), channel_id=1, source_target_pairs={{3,0},{0,1},{1,2},{2,3},{7,4},{4,5},{5,6},{6,7},{11,8},{8,9},{9,10... | collective-permute-start | bytes 1179656 | tf_op jit(solution)/shard_map/ppermute | solution.py:31
  9.5 11.5 %collective-permute-start.2 = (bf16[64,3072]{1,0:T(8,128)(2,1)}, bf16[64,3072]{1,0:T(8,128)(2,1)S(1)}, u32[]{:S(2)}, u32[]{:S(2)}) collective-permute-start(bf16[64,3072]{1,0:T(8,128)(2,1)} %get-tuple-element.66), channel_id=1, source_target_pairs={{1,0},{2,1},{3,2},{0,3},{5,4},{6,5},{7,6},{4,7},{9,8},{10,9},{11,1... | collective-permute-start | bytes 1179656 | tf_op jit(solution)/shard_map/ppermute | solution.py:31
  14.3 12.0 %collective-permute-start.5 = (bf16[2,512,128]{2,1,0:T(8,128)(2,1)S(1)}, bf16[2,512,128]{2,1,0:T(8,128)(2,1)S(1)}, u32[]{:S(2)}, u32[]{:S(2)}) collective-permute-start(bf16[2,512,128]{2,1,0:T(8,128)(2,1)S(1)} %get-tuple-element.69), channel_id=1, source_target_pairs={{12,0},{0,4},{4,8},{8,12},{28,16},{16,20},{20,24},{24,28},{44,32},... | collective-permute-start | bytes 786440 | tf_op jit(solution)/shard_map/ppermute | solution.py:41
  14.6 11.7 %collective-permute-start.6 = (bf16[2,512,128]{2,1,0:T(8,128)(2,1)S(1)}, bf16[2,512,128]{2,1,0:T(8,128)(2,1)S(1)}, u32[]{:S(2)}, u32[]{:S(2)}) collective-permute-start(bf16[2,512,128]{2,1,0:T(8,128)(2,1)S(1)} %get-tuple-element.70), channel_id=1, source_target_pairs={{8,0},{12,4},{0,8},{4,12},{24,16},{28,20},{16,24},{20,28},{40,32},... | collective-permute-start | bytes 786440 | tf_op jit(solution)/shard_map/ppermute | solution.py:41
  17.2 11.9 %collective-permute-start.7 = (bf16[2,512,128]{2,1,0:T(8,128)(2,1)S(1)}, bf16[2,512,128]{2,1,0:T(8,128)(2,1)S(1)}, u32[]{:S(2)}, u32[]{:S(2)}) collective-permute-start(bf16[2,512,128]{2,1,0:T(8,128)(2,1)S(1)} %get-tuple-element.71), channel_id=1, source_target_pairs={{4,0},{8,4},{12,8},{0,12},{20,16},{24,20},{28,24},{16,28},{36,32},... | collective-permute-start | bytes 786440 | tf_op jit(solution)/shard_map/ppermute | solution.py:41
  21.0 16.0 %collective-permute-start.3 = (bf16[64,3072]{1,0:T(8,128)(2,1)S(1)}, bf16[64,3072]{1,0:T(8,128)(2,1)S(1)}, u32[]{:S(2)}, u32[]{:S(2)}) collective-permute-start(bf16[64,3072]{1,0:T(8,128)(2,1)S(1)} %get-tuple-element.67), channel_id=1, source_target_pairs={{2,0},{3,1},{0,2},{1,3},{6,4},{7,5},{4,6},{5,7},{10,8},{11,9},{8,1... | collective-permute-start | bytes 1179656 | tf_op jit(solution)/shard_map/ppermute | solution.py:31
  23.7 9.6 %collective-permute-start.13 = (bf16[2,512,128]{2,1,0:T(8,128)(2,1)S(1)}, bf16[2,512,128]{2,1,0:T(8,128)(2,1)S(1)}, u32[]{:S(2)}, u32[]{:S(2)}) collective-permute-start(bf16[2,512,128]{2,1,0:T(8,128)(2,1)S(1)} %get-tuple-element.60.own.refs_0_), channel_id=1, source_target_pairs={{112,0},{116,4},{120,8},{124,12},{0,16},{4,20},{8,24},{12,28},{16,... | collective-permute-start | bytes 786440 | tf_op jit(solution)/shard_map/ppermute | solution.py:31
  29.7 7.3 %collective-permute-start.8 = (bf16[2,512,128]{2,1,0:T(8,128)(2,1)S(1)}, bf16[2,512,128]{2,1,0:T(8,128)(2,1)S(1)}, u32[]{:S(2)}, u32[]{:S(2)}) collective-permute-start(bf16[2,512,128]{2,1,0:T(8,128)(2,1)S(1)} %get-tuple-element.73), channel_id=1, source_target_pairs={{128,0},{0,128},{129,1},{1,129},{130,2},{2,130},{131,3},{3,131},{1... | collective-permute-start | bytes 786440 | tf_op jit(solution)/shard_map/ppermute | solution.py:31
  34.2 13.9 %collective-permute-start.14 = (bf16[2,512,128]{2,1,0:T(8,128)(2,1)}, bf16[2,512,128]{2,1,0:T(8,128)(2,1)S(1)}, u32[]{:S(2)}, u32[]{:S(2)}) collective-permute-start(bf16[2,512,128]{2,1,0:T(8,128)(2,1)} %get-tuple-element.85), channel_id=1, source_target_pairs={{12,0},{0,4},{4,8},{8,12},{28,16},{16,20},{20,24},{24,28},{44,32},... | collective-permute-start | bytes 786440 | tf_op jit(solution)/shard_map/ppermute | solution.py:41
  34.4 13.7 %collective-permute-start.15 = (bf16[2,512,128]{2,1,0:T(8,128)(2,1)}, bf16[2,512,128]{2,1,0:T(8,128)(2,1)S(1)}, u32[]{:S(2)}, u32[]{:S(2)}) collective-permute-start(bf16[2,512,128]{2,1,0:T(8,128)(2,1)} %get-tuple-element.87), channel_id=1, source_target_pairs={{8,0},{12,4},{0,8},{4,12},{24,16},{28,20},{16,24},{20,28},{40,32},... | collective-permute-start | bytes 786440 | tf_op jit(solution)/shard_map/ppermute | solution.py:41
  37.0 11.2 %collective-permute-start.16 = (bf16[2,512,128]{2,1,0:T(8,128)(2,1)S(1)}, bf16[2,512,128]{2,1,0:T(8,128)(2,1)S(1)}, u32[]{:S(2)}, u32[]{:S(2)}) collective-permute-start(bf16[2,512,128]{2,1,0:T(8,128)(2,1)S(1)} %get-tuple-element.89), channel_id=1, source_target_pairs={{4,0},{8,4},{12,8},{0,12},{20,16},{24,20},{28,24},{16,28},{36,32},... | collective-permute-start | bytes 786440 | tf_op jit(solution)/shard_map/ppermute | solution.py:41
  43.9 0.6 copy-start.5
  44.5 0.6 copy-start.7
  45.2 0.6 copy-start.9
  45.8 3.6 %collective-permute-start.9 = (bf16[2,512,128]{2,1,0:T(8,128)(2,1)S(1)}, bf16[2,512,128]{2,1,0:T(8,128)(2,1)}, u32[]{:S(2)}, u32[]{:S(2)}) collective-permute-start(bf16[2,512,128]{2,1,0:T(8,128)(2,1)S(1)} %get-tuple-element.75), channel_id=1, source_target_pairs={{128,0},{0,128},{129,1},{1,129},{130,2},{2,130},{131,3},{3,131},{1... | collective-permute-start | bytes 786440 | tf_op jit(solution)/shard_map/ppermute | solution.py:31
  48.9 7.9 %collective-permute-start.17 = (bf16[2,512,128]{2,1,0:T(8,128)(2,1)S(1)}, bf16[2,512,128]{2,1,0:T(8,128)(2,1)S(1)}, u32[]{:S(2)}, u32[]{:S(2)}) collective-permute-start(bf16[2,512,128]{2,1,0:T(8,128)(2,1)S(1)} %get-tuple-element.91), channel_id=1, source_target_pairs={{128,0},{0,128},{129,1},{1,129},{130,2},{2,130},{131,3},{3,131},{1... | collective-permute-start | bytes 786440 | tf_op jit(solution)/shard_map/ppermute | solution.py:31
  49.4 7.4 %copy-start.6 = (bf16[64,896]{1,0:T(8,128)(2,1)S(1)}, bf16[64,896]{1,0:T(8,128)(2,1)}, u32[]{:S(2)}) copy-start(bf16[64,896]{1,0:T(8,128)(2,1)} %copy-done.5) | copy-start | bytes 344068
  49.4 7.4 %copy-start.8 = (bf16[64,896]{1,0:T(8,128)(2,1)S(1)}, bf16[64,896]{1,0:T(8,128)(2,1)}, u32[]{:S(2)}) copy-start(bf16[64,896]{1,0:T(8,128)(2,1)} %copy-done.7) | copy-start | bytes 344068
  49.4 7.4 %copy-start.10 = (bf16[64,896]{1,0:T(8,128)(2,1)S(1)}, bf16[64,896]{1,0:T(8,128)(2,1)}, u32[]{:S(2)}) copy-start(bf16[64,896]{1,0:T(8,128)(2,1)} %copy-done.9) | copy-start | bytes 344068
  50.7 13.1 %collective-permute-start.10 = (bf16[2,512,128]{2,1,0:T(8,128)(2,1)S(1)}, bf16[2,512,128]{2,1,0:T(8,128)(2,1)S(1)}, u32[]{:S(2)}, u32[]{:S(2)}) collective-permute-start(bf16[2,512,128]{2,1,0:T(8,128)(2,1)S(1)} %get-tuple-element.77), channel_id=1, source_target_pairs={{4,0},{8,4},{12,8},{0,12},{20,16},{24,20},{28,24},{16,28},{36,32},... | collective-permute-start | bytes 786440 | tf_op jit(solution)/shard_map/ppermute | solution.py:41
  51.7 15.7 %collective-permute-start.11 = (bf16[2,512,128]{2,1,0:T(8,128)(2,1)S(1)}, bf16[2,512,128]{2,1,0:T(8,128)(2,1)S(1)}, u32[]{:S(2)}, u32[]{:S(2)}) collective-permute-start(bf16[2,512,128]{2,1,0:T(8,128)(2,1)S(1)} %get-tuple-element.78), channel_id=1, source_target_pairs={{8,0},{12,4},{0,8},{4,12},{24,16},{28,20},{16,24},{20,28},{40,32},... | collective-permute-start | bytes 786440 | tf_op jit(solution)/shard_map/ppermute | solution.py:41
  55.5 11.9 %collective-permute-start.12 = (bf16[2,512,128]{2,1,0:T(8,128)(2,1)S(1)}, bf16[2,512,128]{2,1,0:T(8,128)(2,1)S(1)}, u32[]{:S(2)}, u32[]{:S(2)}) collective-permute-start(bf16[2,512,128]{2,1,0:T(8,128)(2,1)S(1)} %get-tuple-element.79), channel_id=1, source_target_pairs={{12,0},{0,4},{4,8},{8,12},{28,16},{16,20},{20,24},{24,28},{44,32},... | collective-permute-start | bytes 786440 | tf_op jit(solution)/shard_map/ppermute | solution.py:41
  63.7 3.9 %collective-permute-start.20 = (bf16[2,512,128]{2,1,0:T(8,128)(2,1)S(1)}, bf16[2,512,128]{2,1,0:T(8,128)(2,1)S(1)}, u32[]{:S(2)}, u32[]{:S(2)}) collective-permute-start(bf16[2,512,128]{2,1,0:T(8,128)(2,1)S(1)} %get-tuple-element.96), channel_id=1, source_target_pairs={{128,0},{0,128},{129,1},{1,129},{130,2},{2,130},{131,3},{3,131},{1... | collective-permute-start | bytes 786440 | tf_op jit(solution)/shard_map/ppermute | solution.py:31
  67.9 13.6 %collective-permute-start.23 = (bf16[2,512,128]{2,1,0:T(8,128)(2,1)S(1)}, bf16[2,512,128]{2,1,0:T(8,128)(2,1)S(1)}, u32[]{:S(2)}, u32[]{:S(2)}) collective-permute-start(bf16[2,512,128]{2,1,0:T(8,128)(2,1)S(1)} %get-tuple-element.104), channel_id=1, source_target_pairs={{12,0},{0,4},{4,8},{8,12},{28,16},{16,20},{20,24},{24,28},{44,32},... | collective-permute-start | bytes 786440 | tf_op jit(solution)/shard_map/ppermute | solution.py:41
  70.2 11.4 %collective-permute-start.22 = (bf16[2,512,128]{2,1,0:T(8,128)(2,1)S(1)}, bf16[2,512,128]{2,1,0:T(8,128)(2,1)S(1)}, u32[]{:S(2)}, u32[]{:S(2)}) collective-permute-start(bf16[2,512,128]{2,1,0:T(8,128)(2,1)S(1)} %get-tuple-element.102), channel_id=1, source_target_pairs={{8,0},{12,4},{0,8},{4,12},{24,16},{28,20},{16,24},{20,28},{40,32},... | collective-permute-start | bytes 786440 | tf_op jit(solution)/shard_map/ppermute | solution.py:41
  71.3 13.8 %collective-permute-start.21 = (bf16[2,512,128]{2,1,0:T(8,128)(2,1)S(1)}, bf16[2,512,128]{2,1,0:T(8,128)(2,1)S(1)}, u32[]{:S(2)}, u32[]{:S(2)}) collective-permute-start(bf16[2,512,128]{2,1,0:T(8,128)(2,1)S(1)} %get-tuple-element.100), channel_id=1, source_target_pairs={{4,0},{8,4},{12,8},{0,12},{20,16},{24,20},{28,24},{16,28},{36,32},... | collective-permute-start | bytes 786440 | tf_op jit(solution)/shard_map/ppermute | solution.py:41
  71.9 6.2 %collective-permute-start.18 = (bf16[64,1792]{1,0:T(8,128)(2,1)S(1)}, bf16[64,1792]{1,0:T(8,128)(2,1)S(1)}, u32[]{:S(2)}, u32[]{:S(2)}) collective-permute-start(bf16[64,1792]{1,0:T(8,128)(2,1)S(1)} %get-tuple-element.93), channel_id=1, source_target_pairs={{1,0},{2,1},{3,2},{0,3},{5,4},{6,5},{7,6},{4,7},{9,8},{10,9},{11,1... | collective-permute-start | bytes 688136 | tf_op jit(solution)/shard_map/ppermute | solution.py:31
  73.4 12.0 %collective-permute-start.24 = (bf16[64,1792]{1,0:T(8,128)(2,1)S(1)}, bf16[64,1792]{1,0:T(8,128)(2,1)S(1)}, u32[]{:S(2)}, u32[]{:S(2)}) collective-permute-start(bf16[64,1792]{1,0:T(8,128)(2,1)S(1)} %get-tuple-element.105), channel_id=1, source_target_pairs={{3,0},{0,1},{1,2},{2,3},{7,4},{4,5},{5,6},{6,7},{11,8},{8,9},{9,10... | collective-permute-start | bytes 688136 | tf_op jit(solution)/shard_map/ppermute | solution.py:31
  78.1 10.9 %collective-permute-start.19 = (bf16[2,512,128]{2,1,0:T(8,128)(2,1)S(1)}, bf16[2,512,128]{2,1,0:T(8,128)(2,1)S(1)}, u32[]{:S(2)}, u32[]{:S(2)}) collective-permute-start(bf16[2,512,128]{2,1,0:T(8,128)(2,1)S(1)} %get-tuple-element.94), channel_id=1, source_target_pairs={{16,0},{20,4},{24,8},{28,12},{32,16},{36,20},{40,24},{44,28},{48,3... | collective-permute-start | bytes 786440 | tf_op jit(solution)/shard_map/ppermute | solution.py:31
  85.4 8.2 %collective-permute-start.25 = (bf16[2,512,128]{2,1,0:T(8,128)(2,1)S(1)}, bf16[2,512,128]{2,1,0:T(8,128)(2,1)S(1)}, u32[]{:S(2)}, u32[]{:S(2)}) collective-permute-start(bf16[2,512,128]{2,1,0:T(8,128)(2,1)S(1)} %get-tuple-element.106), channel_id=1, source_target_pairs={{16,0},{20,4},{24,8},{28,12},{32,16},{36,20},{40,24},{44,28},{48,3... | collective-permute-start | bytes 786440 | tf_op jit(solution)/shard_map/ppermute | solution.py:31
  87.4 8.7 %collective-permute-start.26 = (bf16[64,1792]{1,0:T(8,128)(2,1)S(1)}, bf16[64,1792]{1,0:T(8,128)(2,1)S(1)}, u32[]{:S(2)}, u32[]{:S(2)}) collective-permute-start(bf16[64,1792]{1,0:T(8,128)(2,1)S(1)} %get-tuple-element.110), channel_id=1, source_target_pairs={{2,0},{3,1},{0,2},{1,3},{6,4},{7,5},{4,6},{5,7},{10,8},{11,9},{8,1... | collective-permute-start | bytes 688136 | tf_op jit(solution)/shard_map/ppermute | solution.py:31

commit v3 on v2

--- a/solution.py
+++ b/solution.py
@@ -332,21 +332,22 @@
         [jax.ShapeDtypeStruct((rows, pack_cols), bf16)] * tp_count,
         [scalars()] + [whole()] * 4,
     )(meta, resp_queries, resp_dout, resp_keys, resp_values)
-    arrived = {d: shifted(packs[d], "tp", d) for d in range(1, tp_count, 2)}
-    for d in range(2, tp_count, 2):
-        arrived[d] = shifted(after(packs[d], arrived), "tp", d)
+    arrived = {1: shifted(packs[1], "tp", 1)}
+
+    before = [to_row(block, 1) for block in halves]
+    for d in range(2, tp_count):
+        arrived[d] = shifted(after(packs[d], (arrived[1], before[1]) if d > 2 else arrived[1]), "tp", d)
     arrived = [packs[0]] + [arrived[d] for d in range(1, tp_count)]
-
-    before = [to_row(block, 1) for block in halves]
     sends = [
         list(
             small_call(sends_kernel, "sends", [part] * (WIN - 1), [scalars()] + [whole()] * 2)(
-                after(at_row[None], packs), halves[c], before[c]
+                after(at_row[None], packs), halves[0], before[0]
             )
         )
-        for c in range(CHUNKS)
+    ] + [
+        [jnp.where(at_row + offset >= ROW, before[c], halves[c]) for offset in range(1, WIN)]
+        for c in range(1, CHUNKS)
     ]
-
     offers = []
     for c in range(CHUNKS):
         offer = {0: halves[c]}
@@ -365,9 +366,10 @@
         other = after(shifted(wanted, "section", 1), terms)
         backs, own_grad, other_grad = attend(c, meta, arrived, backs, own, other)
         if c == CHUNKS - 1:
-            returned = {d: shifted(backs[d], "tp", -d) for d in range(1, tp_count, 2)}
-            for d in range(2, tp_count, 2):
-                returned[d] = shifted(after(backs[d], returned), "tp", -d)
+            returned = {1: shifted(backs[1], "tp", -1)}
+            for d in range(2, tp_count):
+                first = after(backs[d], returned[1] if d > 2 else shares[1])
+                returned[d] = shifted(first, "tp", -d)
         sibling_grad = after(shifted(other_grad, "section", 1), passing)
         terms = []
         for offset in range(WIN):
@@ -387,12 +389,10 @@
             passed = passed + jnp.where(crossing, term, 0.0)
         passed = passed.astype(bf16)
         if c == CHUNKS - 1:
-            passed = after(passed, (returned[1], returned[tp_count - 1]))
+            passed = after(passed, (returned[1], returned[2]))
         passing.append(passed)
-        shares += [kept, passed]
-
-    shares[1] = to_row(after(shares[1], returned[1]), -1)
-    shares[3] = to_row(shares[3], -1)
+        shares += [kept, to_row(passed, -1)]
+
     prompt_grads = small_call(
         finish_kernel,
         "finish",
@@ -408,7 +408,7 @@
             jax.ShapeDtypeStruct(resp_values.shape, bf16),
         ],
         [scalars()] + [whole()] * tp_count,
-    )(after(tp, prompt_grads), backs[0], *[returned[d] for d in range(1, tp_count)])
+    )(tp, backs[0], *[returned[d] for d in range(1, tp_count)])
     return (grads[0], grads[1], grads[2], prompt_grads)
 
 

time: 97.4 us -> 101 us (1.037)
  waiting for transfers between devices: 32.1 us -> 38.6 us
  local copies, waits for them, and re-layouts: 4.9 us -> 2.96 us
  Pallas kernels: 19.6 us -> 17.8 us
    ppermute x12, waiting for transfers between devices: 11.6 us -> 19.3 us  [along_row(): return lax.ppermute(block, 'group', route)]
    ppermute x15, starting transfers between devices: 18.1 us -> 20.6 us  [shifted(): return lax.ppermute(block, axis, route)]
    ppermute x12, starting transfers between devices: 15.8 us -> 13.7 us  [along_row(): return lax.ppermute(block, 'group', route)]
    unnamed x24 -> x12, local copies, waits for them, and re-layouts: 4.9 us -> 2.96 us
    ppermute x15, waiting for transfers between devices: 20.5 us -> 19.3 us  [shifted(): return lax.ppermute(block, axis, route)]
  transfers between devices with their start and end apart: 27 -> 27, of which waited for: 11 -> 11; matrix products, arithmetic and copies ran while one was open for 2% -> 2% of each run, Pallas kernels for 19% -> 17%
where the time goes in v3:
time: 101 us; the launch traced here: 100 us
  waiting for transfers between devices  38.6 us (38%)
  starting transfers between devices  34.4 us (34%)
  Pallas kernels  17.8 us (18%)
  between operations  4.41 us (4%)
  local copies, waits for them, and re-layouts  2.96 us (3%)
  other arithmetic  2.2 us (2%)
    ppermute x15, starting transfers between devices, shifted(): return lax.ppermute(block, axis, route)  20.6 us
    ppermute x15, waiting for transfers between devices, shifted(): return lax.ppermute(block, axis, route)  19.3 us
    ppermute x12, waiting for transfers between devices, along_row(): return lax.ppermute(block, 'group', route)  19.3 us
    ppermute x12, starting transfers between devices, along_row(): return lax.ppermute(block, 'group', route)  13.7 us
    pallas_call x2, Pallas kernels, attend(): pl.pallas_call(functools.partial(attend_kernel, chunk, tp_count), out_sha...  13.7 us
    unnamed x12, local copies, waits for them, and re-layouts  2.96 us
  transfers between devices with their start and end apart: 27, of which 11 were waited for; matrix products, arithmetic and copies ran while one was open for 2% of the time, Pallas kernels for 17%

profile of v3, /device:TPU:24, one launch (start us, length us, event | category | flops | bytes accessed | tf_op | source)
XLA Modules:
  0.0 100.3 jit_solution(13214272434870729246)
XLA Ops:
  0.6 1.2 %copy-done = bf16[1,2,1024,256]{3,2,1,0:T(8,128)(2,1)S(1)} copy-done((bf16[1,2,1024,256]{3,2,1,0:T(8,128)(2,1)S(1)}, bf16[1,2,1024,256]{3,2,1,0:T(8,128)(2,1)}, u32[]{:S(2)}) %copy-start) | copy-done | bytes 1048600
  2.0 2.0 %collective-permute-start.5 = (bf16[2,512,128]{2,1,0:T(8,128)(2,1)S(1)}, bf16[2,512,128]{2,1,0:T(8,128)(2,1)S(1)}, u32[]{:S(2)}, u32[]{:S(2)}) collective-permute-start(bf16[2,512,128]{2,1,0:T(8,128)(2,1)S(1)} %get-tuple-element.56.own.refs_0_), channel_id=1, source_target_pairs={{112,0},{116,4},{120,8},{124,12},{0,16},{4,20},{8,24},{12,28},{16,... | collective-permute-start | bytes 786440 | tf_op jit(solution)/shard_map/ppermute | solution.py:31
  4.6 0.6 copy-done.5
  5.4 1.1 %copy-done.2 = bf16[64,5120]{1,0:T(8,128)(2,1)S(1)} copy-done((bf16[64,5120]{1,0:T(8,128)(2,1)S(1)}, bf16[64,5120]{1,0:T(8,128)(2,1)}, u32[]{:S(2)}) %copy-start.2) | copy-done | bytes 655384
  6.5 0.7 pack.1
  7.2 1.6 %collective-permute-start.1 = (bf16[64,3072]{1,0:T(8,128)(2,1)S(1)}, bf16[64,3072]{1,0:T(8,128)(2,1)S(1)}, u32[]{:S(2)}, u32[]{:S(2)}) collective-permute-start(bf16[64,3072]{1,0:T(8,128)(2,1)S(1)} %get-tuple-element.61), channel_id=1, source_target_pairs={{3,0},{0,1},{1,2},{2,3},{7,4},{4,5},{5,6},{6,7},{11,8},{8,9},{9,10... | collective-permute-start | bytes 1179656 | tf_op jit(solution)/shard_map/ppermute | solution.py:31
  8.7 1.9 %collective-permute-start.3 = (bf16[2,512,128]{2,1,0:T(8,128)(2,1)S(1)}, bf16[2,512,128]{2,1,0:T(8,128)(2,1)}, u32[]{:S(2)}, u32[]{:S(2)}) collective-permute-start(bf16[2,512,128]{2,1,0:T(8,128)(2,1)S(1)} %get-tuple-element.57.refs_0_), channel_id=1, source_target_pairs={{112,0},{116,4},{120,8},{124,12},{0,16},{4,20},{8,24},{12,28},{16,... | collective-permute-start | bytes 786440 | tf_op jit(solution)/shard_map/ppermute | solution.py:31
  10.7 3.8 %collective-permute-done.5.before = bf16[2,512,128]{2,1,0:T(8,128)(2,1)S(1)} collective-permute-done((bf16[2,512,128]{2,1,0:T(8,128)(2,1)S(1)}, bf16[2,512,128]{2,1,0:T(8,128)(2,1)S(1)}, u32[]{:S(2)}, u32[]{:S(2)}) %collective-permute-start.5) | collective-permute-done | bytes 262176 | tf_op jit(solution)/shard_map/ppermute | solution.py:31
  14.6 0.3 collective-permute-start.6
  14.9 2.6 %collective-permute-start.7 = (bf16[2,512,128]{2,1,0:T(8,128)(2,1)S(1)}, bf16[2,512,128]{2,1,0:T(8,128)(2,1)S(1)}, u32[]{:S(2)}, u32[]{:S(2)}) collective-permute-start(bf16[2,512,128]{2,1,0:T(8,128)(2,1)S(1)} %get-tuple-element.68), channel_id=1, source_target_pairs={{8,0},{12,4},{0,8},{4,12},{24,16},{28,20},{16,24},{20,28},{40,32},... | collective-permute-start | bytes 786440 | tf_op jit(solution)/shard_map/ppermute | solution.py:41
  17.5 2.5 %collective-permute-done.3 = bf16[2,512,128]{2,1,0:T(8,128)(2,1)} collective-permute-done((bf16[2,512,128]{2,1,0:T(8,128)(2,1)S(1)}, bf16[2,512,128]{2,1,0:T(8,128)(2,1)}, u32[]{:S(2)}, u32[]{:S(2)}) %collective-permute-start.3) | collective-permute-done | bytes 262176 | tf_op jit(solution)/shard_map/ppermute | solution.py:31
  20.0 3.0 %collective-permute-start.2 = (bf16[64,3072]{1,0:T(8,128)(2,1)S(1)}, bf16[64,3072]{1,0:T(8,128)(2,1)S(1)}, u32[]{:S(2)}, u32[]{:S(2)}) collective-permute-start(bf16[64,3072]{1,0:T(8,128)(2,1)S(1)} %get-tuple-element.63), channel_id=1, source_target_pairs={{2,0},{3,1},{0,2},{1,3},{6,4},{7,5},{4,6},{5,7},{10,8},{11,9},{8,1... | collective-permute-start | bytes 1179656 | tf_op jit(solution)/shard_map/ppermute | solution.py:31
  23.0 1.1 %collective-permute-start.4 = (bf16[64,3072]{1,0:T(8,128)(2,1)S(1)}, bf16[64,3072]{1,0:T(8,128)(2,1)S(1)}, u32[]{:S(2)}, u32[]{:S(2)}) collective-permute-start(bf16[64,3072]{1,0:T(8,128)(2,1)S(1)} %get-tuple-element.65), channel_id=1, source_target_pairs={{1,0},{2,1},{3,2},{0,3},{5,4},{6,5},{7,6},{4,7},{9,8},{10,9},{11,1... | collective-permute-start | bytes 1179656 | tf_op jit(solution)/shard_map/ppermute | solution.py:31
  24.8 0.9 collective-permute-done.7.refs_2_
  25.6 3.5 %collective-permute-done.8.refs_3_ = bf16[2,512,128]{2,1,0:T(8,128)(2,1)S(1)} collective-permute-done((bf16[2,512,128]{2,1,0:T(8,128)(2,1)S(1)}, bf16[2,512,128]{2,1,0:T(8,128)(2,1)S(1)}, u32[]{:S(2)}, u32[]{:S(2)}) %collective-permute-start.8) | collective-permute-done | bytes 262176 | tf_op jit(solution)/shard_map/ppermute | solution.py:41
  29.1 0.6 pick.2
  29.7 0.1 collective-permute-start.9
  29.8 1.0 %broadcast_select_fusion = (bf16[2,512,128]{2,1,0:T(8,128)(2,1)S(1)}, bf16[2,512,128]{2,1,0:T(8,128)(2,1)S(1)}, bf16[2,512,128]{2,1,0:T(8,128)(2,1)S(1)}) fusion(bf16[2,512,128]{2,1,0:T(8,128)(2,1)} %collective-permute-done.3, bf16[2,512,128]{2,1,0:T(8,128)(2,1)S(1)} %get-tuple-element.57.refs_0_, pred[]{:T(512)S(6)} %ge.8, pred[]{:T(512)S(6)} %ge.7, pred[]{:T(512)S(6)} %ge.6), kind=kLoop, calls=%fused_computation.54 | loop fusion | flops 393216 | bytes 1310723 | tf_op jit(solution)/shard_map/jit(_where)/select_n | solution.py:348
  30.9 1.1 %collective-permute-start.10 = (bf16[2,512,128]{2,1,0:T(8,128)(2,1)S(1)}, bf16[2,512,128]{2,1,0:T(8,128)(2,1)S(1)}, u32[]{:S(2)}, u32[]{:S(2)}) collective-permute-start(bf16[2,512,128]{2,1,0:T(8,128)(2,1)S(1)} %get-tuple-element.76), channel_id=1, source_target_pairs={{12,0},{0,4},{4,8},{8,12},{28,16},{16,20},{20,24},{24,28},{44,32},... | collective-permute-start | bytes 786440 | tf_op jit(solution)/shard_map/ppermute | solution.py:41
  32.0 2.0 %collective-permute-start.11 = (bf16[2,512,128]{2,1,0:T(8,128)(2,1)S(1)}, bf16[2,512,128]{2,1,0:T(8,128)(2,1)S(1)}, u32[]{:S(2)}, u32[]{:S(2)}) collective-permute-start(bf16[2,512,128]{2,1,0:T(8,128)(2,1)S(1)} %get-tuple-element.77), channel_id=1, source_target_pairs={{8,0},{12,4},{0,8},{4,12},{24,16},{28,20},{16,24},{20,28},{40,32},... | collective-permute-start | bytes 786440 | tf_op jit(solution)/shard_map/ppermute | solution.py:41
  34.0 0.1 collective-permute-start.12
  34.1 6.2 %collective-permute-done.4.refs_3_ = bf16[64,3072]{1,0:T(8,128)(2,1)S(1)} collective-permute-done((bf16[64,3072]{1,0:T(8,128)(2,1)S(1)}, bf16[64,3072]{1,0:T(8,128)(2,1)S(1)}, u32[]{:S(2)}, u32[]{:S(2)}) %collective-permute-start.4) | collective-permute-done | bytes 393248 | tf_op jit(solution)/shard_map/ppermute | solution.py:31
  40.3 6.8 %attend.2 = (bf16[64,896]{1,0:T(8,128)(2,1)S(1)}, bf16[64,896]{1,0:T(8,128)(2,1)S(1)}, bf16[64,896]{1,0:T(8,128)(2,1)S(1)}, bf16[64,896]{1,0:T(8,128)(2,1)S(1)},...) custom-call(s32[11]{0:T(128)S(1)} %pad_add_fusion.meta, ...), custom_call_target="tpu_custom_call" | custom-call | flops 16777216000 | bytes 6291456 | tf_op jit(solution)/shard_map/attend/pallas_call | solution.py:274
  47.1 0.1 collective-permute-start.14
  49.5 0.6 pick.3
  50.1 0.6 collective-permute-start.13
  50.7 0.3 fusion.18
  51.0 0.8 collective-permute-start.16
  51.9 0.9 collective-permute-start.17
  52.8 2.2 %collective-permute-start.18 = (bf16[2,512,128]{2,1,0:T(8,128)(2,1)S(1)}, bf16[2,512,128]{2,1,0:T(8,128)(2,1)S(1)}, u32[]{:S(2)}, u32[]{:S(2)}) collective-permute-start(bf16[2,512,128]{2,1,0:T(8,128)(2,1)S(1)} %get-tuple-element.86), channel_id=1, source_target_pairs={{12,0},{0,4},{4,8},{8,12},{28,16},{16,20},{20,24},{24,28},{44,32},... | collective-permute-start | bytes 786440 | tf_op jit(solution)/shard_map/ppermute | solution.py:41
  55.0 6.9 %attend.3 = (bf16[64,1792]{1,0:T(8,128)(2,1)S(1)}, bf16[64,1792]{1,0:T(8,128)(2,1)S(1)}, bf16[64,1792]{1,0:T(8,128)(2,1)S(1)}, bf16[64,1792]{1,0:T(8,128)(2,1)S(...) custom-call(s32[11]{0:T(128)S(1)} %pad_add_fusion.meta, ...), custom_call_target="tpu_custom_call" | custom-call | flops 16777216000 | bytes 6291456 | tf_op jit(solution)/shard_map/attend/pallas_call | solution.py:274
  61.9 4.2 %collective-permute-done.16 = bf16[2,512,128]{2,1,0:T(8,128)(2,1)S(1)} collective-permute-done((bf16[2,512,128]{2,1,0:T(8,128)(2,1)S(1)}, bf16[2,512,128]{2,1,0:T(8,128)(2,1)S(1)}, u32[]{:S(2)}, u32[]{:S(2)}) %collective-permute-start.16) | collective-permute-done | bytes 262176 | tf_op jit(solution)/shard_map/ppermute | solution.py:41
  66.2 0.6 collective-permute-done.18
  66.8 0.3 fusion.5
  67.1 3.4 %collective-permute-start.19 = (bf16[2,512,128]{2,1,0:T(8,128)(2,1)S(1)}, bf16[2,512,128]{2,1,0:T(8,128)(2,1)S(1)}, u32[]{:S(2)}, u32[]{:S(2)}) collective-permute-start(bf16[2,512,128]{2,1,0:T(8,128)(2,1)S(1)} %get-tuple-element.111), channel_id=1, source_target_pairs={{16,0},{20,4},{24,8},{28,12},{32,16},{36,20},{40,24},{44,28},{48,3... | collective-permute-start | bytes 786440 | tf_op jit(solution)/shard_map/ppermute | solution.py:31
  70.5 0.3 fusion.25
  70.8 2.7 %collective-permute-start.25 = (bf16[2,512,128]{2,1,0:T(8,128)(2,1)S(1)}, bf16[2,512,128]{2,1,0:T(8,128)(2,1)S(1)}, u32[]{:S(2)}, u32[]{:S(2)}) collective-permute-start(bf16[2,512,128]{2,1,0:T(8,128)(2,1)S(1)} %get-tuple-element.106), channel_id=1, source_target_pairs={{12,0},{0,4},{4,8},{8,12},{28,16},{16,20},{20,24},{24,28},{44,32},... | collective-permute-start | bytes 786440 | tf_op jit(solution)/shard_map/ppermute | solution.py:41
  73.5 0.9 collective-permute-start.23
  74.4 2.6 %collective-permute-start.15 = (bf16[64,1792]{1,0:T(8,128)(2,1)S(1)}, bf16[64,1792]{1,0:T(8,128)(2,1)S(1)}, u32[]{:S(2)}, u32[]{:S(2)}) collective-permute-start(bf16[64,1792]{1,0:T(8,128)(2,1)S(1)} %get-tuple-element.89), channel_id=1, source_target_pairs={{1,0},{2,1},{3,2},{0,3},{5,4},{6,5},{7,6},{4,7},{9,8},{10,9},{11,1... | collective-permute-start | bytes 688136 | tf_op jit(solution)/shard_map/ppermute | solution.py:31
  77.1 0.8 collective-permute-start.20
  77.9 6.7 %collective-permute-done.25 = bf16[2,512,128]{2,1,0:T(8,128)(2,1)S(1)} collective-permute-done((bf16[2,512,128]{2,1,0:T(8,128)(2,1)S(1)}, bf16[2,512,128]{2,1,0:T(8,128)(2,1)S(1)}, u32[]{:S(2)}, u32[]{:S(2)}) %collective-permute-start.25) | collective-permute-done | bytes 262176 | tf_op jit(solution)/shard_map/ppermute | solution.py:41
  84.6 3.4 %collective-permute-done.23 = bf16[2,512,128]{2,1,0:T(8,128)(2,1)S(1)} collective-permute-done((bf16[2,512,128]{2,1,0:T(8,128)(2,1)S(1)}, bf16[2,512,128]{2,1,0:T(8,128)(2,1)S(1)}, u32[]{:S(2)}, u32[]{:S(2)}) %collective-permute-start.23) | collective-permute-done | bytes 262176 | tf_op jit(solution)/shard_map/ppermute | solution.py:41
  88.0 0.3 fusion.11
  88.3 2.0 %collective-permute-start.26 = (bf16[2,512,128]{2,1,0:T(8,128)(2,1)S(1)}, bf16[2,512,128]{2,1,0:T(8,128)(2,1)S(1)}, u32[]{:S(2)}, u32[]{:S(2)}) collective-permute-start(bf16[2,512,128]{2,1,0:T(8,128)(2,1)S(1)} %get-tuple-element.107), channel_id=1, source_target_pairs={{16,0},{20,4},{24,8},{28,12},{32,16},{36,20},{40,24},{44,28},{48,3... | collective-permute-start | bytes 786440 | tf_op jit(solution)/shard_map/ppermute | solution.py:31
  90.3 1.4 %collective-permute-start.21 = (bf16[64,1792]{1,0:T(8,128)(2,1)S(1)}, bf16[64,1792]{1,0:T(8,128)(2,1)S(1)}, u32[]{:S(2)}, u32[]{:S(2)}) collective-permute-start(bf16[64,1792]{1,0:T(8,128)(2,1)S(1)} %get-tuple-element.93), channel_id=1, source_target_pairs={{3,0},{0,1},{1,2},{2,3},{7,4},{4,5},{5,6},{6,7},{11,8},{8,9},{9,10... | collective-permute-start | bytes 688136 | tf_op jit(solution)/shard_map/ppermute | solution.py:31
  91.6 6.7 %collective-permute-done.21.refs_3_ = bf16[64,1792]{1,0:T(8,128)(2,1)S(1)} collective-permute-done((bf16[64,1792]{1,0:T(8,128)(2,1)S(1)}, bf16[64,1792]{1,0:T(8,128)(2,1)S(1)}, u32[]{:S(2)}, u32[]{:S(2)}) %collective-permute-start.21) | collective-permute-done | bytes 229408 | tf_op jit(solution)/shard_map/ppermute | solution.py:31
  98.4 1.0 %unpack.1 = (bf16[64,5120]{1,0:T(8,128)(2,1)}, bf16[64,1024]{1,0:T(8,128)(2,1)}, bf16[64,1024]{1,0:T(8,128)(2,1)}) custom-call(s32[1]{0:T(128)} %bitcast.tp, bf16[64,1792]{1,0:T(8,128)(2,1)S(1)} %get-tuple-element.88.refs_0_, bf16[64,1792]{1,0:T(8,128)(2,1)S(1)} %collective-permute-done.15.refs_1_, bf16[64,1792]{1,0:T(8,128)(2,1)S(1)} %collective-permute-done.20.refs_2_, ...), custom_call_target="tpu_custom_call" | custom-call | tf_op jit(solution)/shard_map/unpack/pallas_call | solution.py:402
  99.4 0.9 finish.1
  (33 shorter events, 0.5 us)
Async XLA Ops:
  0.6 1.2 %copy-start = (bf16[1,2,1024,256]{3,2,1,0:T(8,128)(2,1)S(1)}, bf16[1,2,1024,256]{3,2,1,0:T(8,128)(2,1)}, u32[]{:S(2)}) copy-start(bf16[1,2,1024,256]{3,2,1,0:T(8,128)(2,1)} %prompt.1) | copy-start | bytes 3145732
  1.9 3.5 %copy-start.1 = (bf16[64,5120]{1,0:T(8,128)(2,1)S(1)}, bf16[64,5120]{1,0:T(8,128)(2,1)}, u32[]{:S(2)}) copy-start(bf16[64,5120]{1,0:T(8,128)(2,1)} %queries.1) | copy-start | bytes 1966084
  1.9 3.5 %copy-start.3 = (bf16[64,1024]{1,0:T(8,128)(2,1)S(1)}, bf16[64,1024]{1,0:T(8,128)(2,1)}, u32[]{:S(2)}) copy-start(bf16[64,1024]{1,0:T(8,128)(2,1)} %keys.1) | copy-start | bytes 393220
  1.9 3.5 %copy-start.4 = (bf16[64,1024]{1,0:T(8,128)(2,1)S(1)}, bf16[64,1024]{1,0:T(8,128)(2,1)}, u32[]{:S(2)}) copy-start(bf16[64,1024]{1,0:T(8,128)(2,1)} %values.1) | copy-start | bytes 393220
  2.0 12.5 %collective-permute-start.5 = (bf16[2,512,128]{2,1,0:T(8,128)(2,1)S(1)}, bf16[2,512,128]{2,1,0:T(8,128)(2,1)S(1)}, u32[]{:S(2)}, u32[]{:S(2)}) collective-permute-start(bf16[2,512,128]{2,1,0:T(8,128)(2,1)S(1)} %get-tuple-element.56.own.refs_0_), channel_id=1, source_target_pairs={{112,0},{116,4},{120,8},{124,12},{0,16},{4,20},{8,24},{12,28},{16,... | collective-permute-start | bytes 786440 | tf_op jit(solution)/shard_map/ppermute | solution.py:31
  4.0 1.4 %collective-permute-start = (s32[1]{0:T(128)}, s32[1]{0:T(128)}, u32[]{:S(2)}, u32[]{:S(2)}) collective-permute-start(s32[1]{0:T(128)} %param.14), channel_id=1, source_target_pairs={{128,0},{0,128},{129,1},{1,129},{130,2},{2,130},{131,3},{3,131},{1... | collective-permute-start | bytes 20 | tf_op jit(solution)/shard_map/ppermute | solution.py:31
  4.6 0.7 copy-start.5
  5.4 1.1 %copy-start.2 = (bf16[64,5120]{1,0:T(8,128)(2,1)S(1)}, bf16[64,5120]{1,0:T(8,128)(2,1)}, u32[]{:S(2)}) copy-start(bf16[64,5120]{1,0:T(8,128)(2,1)} %grad_out.1) | copy-start | bytes 1966084
  7.2 12.8 %collective-permute-start.1 = (bf16[64,3072]{1,0:T(8,128)(2,1)S(1)}, bf16[64,3072]{1,0:T(8,128)(2,1)S(1)}, u32[]{:S(2)}, u32[]{:S(2)}) collective-permute-start(bf16[64,3072]{1,0:T(8,128)(2,1)S(1)} %get-tuple-element.61), channel_id=1, source_target_pairs={{3,0},{0,1},{1,2},{2,3},{7,4},{4,5},{5,6},{6,7},{11,8},{8,9},{9,10... | collective-permute-start | bytes 1179656 | tf_op jit(solution)/shard_map/ppermute | solution.py:31
  8.7 11.2 %collective-permute-start.3 = (bf16[2,512,128]{2,1,0:T(8,128)(2,1)S(1)}, bf16[2,512,128]{2,1,0:T(8,128)(2,1)}, u32[]{:S(2)}, u32[]{:S(2)}) collective-permute-start(bf16[2,512,128]{2,1,0:T(8,128)(2,1)S(1)} %get-tuple-element.57.refs_0_), channel_id=1, source_target_pairs={{112,0},{116,4},{120,8},{124,12},{0,16},{4,20},{8,24},{12,28},{16,... | collective-permute-start | bytes 786440 | tf_op jit(solution)/shard_map/ppermute | solution.py:31
  14.6 10.2 %collective-permute-start.6 = (bf16[2,512,128]{2,1,0:T(8,128)(2,1)S(1)}, bf16[2,512,128]{2,1,0:T(8,128)(2,1)S(1)}, u32[]{:S(2)}, u32[]{:S(2)}) collective-permute-start(bf16[2,512,128]{2,1,0:T(8,128)(2,1)S(1)} %get-tuple-element.67), channel_id=1, source_target_pairs={{12,0},{0,4},{4,8},{8,12},{28,16},{16,20},{20,24},{24,28},{44,32},... | collective-permute-start | bytes 786440 | tf_op jit(solution)/shard_map/ppermute | solution.py:41
  14.9 10.8 %collective-permute-start.7 = (bf16[2,512,128]{2,1,0:T(8,128)(2,1)S(1)}, bf16[2,512,128]{2,1,0:T(8,128)(2,1)S(1)}, u32[]{:S(2)}, u32[]{:S(2)}) collective-permute-start(bf16[2,512,128]{2,1,0:T(8,128)(2,1)S(1)} %get-tuple-element.68), channel_id=1, source_target_pairs={{8,0},{12,4},{0,8},{4,12},{24,16},{28,20},{16,24},{20,28},{40,32},... | collective-permute-start | bytes 786440 | tf_op jit(solution)/shard_map/ppermute | solution.py:41
  17.4 11.6 %collective-permute-start.8 = (bf16[2,512,128]{2,1,0:T(8,128)(2,1)S(1)}, bf16[2,512,128]{2,1,0:T(8,128)(2,1)S(1)}, u32[]{:S(2)}, u32[]{:S(2)}) collective-permute-start(bf16[2,512,128]{2,1,0:T(8,128)(2,1)S(1)} %get-tuple-element.69), channel_id=1, source_target_pairs={{4,0},{8,4},{12,8},{0,12},{20,16},{24,20},{28,24},{16,28},{36,32},... | collective-permute-start | bytes 786440 | tf_op jit(solution)/shard_map/ppermute | solution.py:41
  20.0 14.1 %collective-permute-start.2 = (bf16[64,3072]{1,0:T(8,128)(2,1)S(1)}, bf16[64,3072]{1,0:T(8,128)(2,1)S(1)}, u32[]{:S(2)}, u32[]{:S(2)}) collective-permute-start(bf16[64,3072]{1,0:T(8,128)(2,1)S(1)} %get-tuple-element.63), channel_id=1, source_target_pairs={{2,0},{3,1},{0,2},{1,3},{6,4},{7,5},{4,6},{5,7},{10,8},{11,9},{8,1... | collective-permute-start | bytes 1179656 | tf_op jit(solution)/shard_map/ppermute | solution.py:31
  23.0 17.3 %collective-permute-start.4 = (bf16[64,3072]{1,0:T(8,128)(2,1)S(1)}, bf16[64,3072]{1,0:T(8,128)(2,1)S(1)}, u32[]{:S(2)}, u32[]{:S(2)}) collective-permute-start(bf16[64,3072]{1,0:T(8,128)(2,1)S(1)} %get-tuple-element.65), channel_id=1, source_target_pairs={{1,0},{2,1},{3,2},{0,3},{5,4},{6,5},{7,6},{4,7},{9,8},{10,9},{11,1... | collective-permute-start | bytes 1179656 | tf_op jit(solution)/shard_map/ppermute | solution.py:31
  29.7 4.2 %collective-permute-start.9 = (bf16[2,512,128]{2,1,0:T(8,128)(2,1)S(1)}, bf16[2,512,128]{2,1,0:T(8,128)(2,1)S(1)}, u32[]{:S(2)}, u32[]{:S(2)}) collective-permute-start(bf16[2,512,128]{2,1,0:T(8,128)(2,1)S(1)} %get-tuple-element.71), channel_id=1, source_target_pairs={{128,0},{0,128},{129,1},{1,129},{130,2},{2,130},{131,3},{3,131},{1... | collective-permute-start | bytes 786440 | tf_op jit(solution)/shard_map/ppermute | solution.py:31
  30.9 18.6 %collective-permute-start.10 = (bf16[2,512,128]{2,1,0:T(8,128)(2,1)S(1)}, bf16[2,512,128]{2,1,0:T(8,128)(2,1)S(1)}, u32[]{:S(2)}, u32[]{:S(2)}) collective-permute-start(bf16[2,512,128]{2,1,0:T(8,128)(2,1)S(1)} %get-tuple-element.76), channel_id=1, source_target_pairs={{12,0},{0,4},{4,8},{8,12},{28,16},{16,20},{20,24},{24,28},{44,32},... | collective-permute-start | bytes 786440 | tf_op jit(solution)/shard_map/ppermute | solution.py:41
  32.0 17.5 %collective-permute-start.11 = (bf16[2,512,128]{2,1,0:T(8,128)(2,1)S(1)}, bf16[2,512,128]{2,1,0:T(8,128)(2,1)S(1)}, u32[]{:S(2)}, u32[]{:S(2)}) collective-permute-start(bf16[2,512,128]{2,1,0:T(8,128)(2,1)S(1)} %get-tuple-element.77), channel_id=1, source_target_pairs={{8,0},{12,4},{0,8},{4,12},{24,16},{28,20},{16,24},{20,28},{40,32},... | collective-permute-start | bytes 786440 | tf_op jit(solution)/shard_map/ppermute | solution.py:41
  34.0 15.5 %collective-permute-start.12 = (bf16[2,512,128]{2,1,0:T(8,128)(2,1)S(1)}, bf16[2,512,128]{2,1,0:T(8,128)(2,1)S(1)}, u32[]{:S(2)}, u32[]{:S(2)}) collective-permute-start(bf16[2,512,128]{2,1,0:T(8,128)(2,1)S(1)} %get-tuple-element.78), channel_id=1, source_target_pairs={{4,0},{8,4},{12,8},{0,12},{20,16},{24,20},{28,24},{16,28},{36,32},... | collective-permute-start | bytes 786440 | tf_op jit(solution)/shard_map/ppermute | solution.py:41
  47.1 3.6 %collective-permute-start.14 = (bf16[2,512,128]{2,1,0:T(8,128)(2,1)S(1)}, bf16[2,512,128]{2,1,0:T(8,128)(2,1)S(1)}, u32[]{:S(2)}, u32[]{:S(2)}) collective-permute-start(bf16[2,512,128]{2,1,0:T(8,128)(2,1)S(1)} %get-tuple-element.82), channel_id=1, source_target_pairs={{128,0},{0,128},{129,1},{1,129},{130,2},{2,130},{131,3},{3,131},{1... | collective-permute-start | bytes 786440 | tf_op jit(solution)/shard_map/ppermute | solution.py:31
  50.1 4.8 %collective-permute-start.13 = (bf16[2,512,128]{2,1,0:T(8,128)(2,1)S(1)}, bf16[2,512,128]{2,1,0:T(8,128)(2,1)S(1)}, u32[]{:S(2)}, u32[]{:S(2)}) collective-permute-start(bf16[2,512,128]{2,1,0:T(8,128)(2,1)S(1)} %get-tuple-element.80), channel_id=1, source_target_pairs={{128,0},{0,128},{129,1},{1,129},{130,2},{2,130},{131,3},{3,131},{1... | collective-permute-start | bytes 786440 | tf_op jit(solution)/shard_map/ppermute | solution.py:31
  51.0 15.1 %collective-permute-start.16 = (bf16[2,512,128]{2,1,0:T(8,128)(2,1)S(1)}, bf16[2,512,128]{2,1,0:T(8,128)(2,1)S(1)}, u32[]{:S(2)}, u32[]{:S(2)}) collective-permute-start(bf16[2,512,128]{2,1,0:T(8,128)(2,1)S(1)} %get-tuple-element.84), channel_id=1, source_target_pairs={{4,0},{8,4},{12,8},{0,12},{20,16},{24,20},{28,24},{16,28},{36,32},... | collective-permute-start | bytes 786440 | tf_op jit(solution)/shard_map/ppermute | solution.py:41
  51.9 14.3 %collective-permute-start.17 = (bf16[2,512,128]{2,1,0:T(8,128)(2,1)S(1)}, bf16[2,512,128]{2,1,0:T(8,128)(2,1)S(1)}, u32[]{:S(2)}, u32[]{:S(2)}) collective-permute-start(bf16[2,512,128]{2,1,0:T(8,128)(2,1)S(1)} %get-tuple-element.85), channel_id=1, source_target_pairs={{8,0},{12,4},{0,8},{4,12},{24,16},{28,20},{16,24},{20,28},{40,32},... | collective-permute-start | bytes 786440 | tf_op jit(solution)/shard_map/ppermute | solution.py:41
  52.8 14.0 %collective-permute-start.18 = (bf16[2,512,128]{2,1,0:T(8,128)(2,1)S(1)}, bf16[2,512,128]{2,1,0:T(8,128)(2,1)S(1)}, u32[]{:S(2)}, u32[]{:S(2)}) collective-permute-start(bf16[2,512,128]{2,1,0:T(8,128)(2,1)S(1)} %get-tuple-element.86), channel_id=1, source_target_pairs={{12,0},{0,4},{4,8},{8,12},{28,16},{16,20},{20,24},{24,28},{44,32},... | collective-permute-start | bytes 786440 | tf_op jit(solution)/shard_map/ppermute | solution.py:41
  61.8 8.6 %collective-permute-start.22 = (bf16[2,512,128]{2,1,0:T(8,128)(2,1)S(1)}, bf16[2,512,128]{2,1,0:T(8,128)(2,1)S(1)}, u32[]{:S(2)}, u32[]{:S(2)}) collective-permute-start(bf16[2,512,128]{2,1,0:T(8,128)(2,1)S(1)} %get-tuple-element.98), channel_id=1, source_target_pairs={{128,0},{0,128},{129,1},{1,129},{130,2},{2,130},{131,3},{3,131},{1... | collective-permute-start | bytes 786440 | tf_op jit(solution)/shard_map/ppermute | solution.py:31
  67.1 10.0 %collective-permute-start.19 = (bf16[2,512,128]{2,1,0:T(8,128)(2,1)S(1)}, bf16[2,512,128]{2,1,0:T(8,128)(2,1)S(1)}, u32[]{:S(2)}, u32[]{:S(2)}) collective-permute-start(bf16[2,512,128]{2,1,0:T(8,128)(2,1)S(1)} %get-tuple-element.111), channel_id=1, source_target_pairs={{16,0},{20,4},{24,8},{28,12},{32,16},{36,20},{40,24},{44,28},{48,3... | collective-permute-start | bytes 786440 | tf_op jit(solution)/shard_map/ppermute | solution.py:31
  70.8 13.8 %collective-permute-start.25 = (bf16[2,512,128]{2,1,0:T(8,128)(2,1)S(1)}, bf16[2,512,128]{2,1,0:T(8,128)(2,1)S(1)}, u32[]{:S(2)}, u32[]{:S(2)}) collective-permute-start(bf16[2,512,128]{2,1,0:T(8,128)(2,1)S(1)} %get-tuple-element.106), channel_id=1, source_target_pairs={{12,0},{0,4},{4,8},{8,12},{28,16},{16,20},{20,24},{24,28},{44,32},... | collective-permute-start | bytes 786440 | tf_op jit(solution)/shard_map/ppermute | solution.py:41
  73.5 11.1 %collective-permute-start.24 = (bf16[2,512,128]{2,1,0:T(8,128)(2,1)S(1)}, bf16[2,512,128]{2,1,0:T(8,128)(2,1)S(1)}, u32[]{:S(2)}, u32[]{:S(2)}) collective-permute-start(bf16[2,512,128]{2,1,0:T(8,128)(2,1)S(1)} %get-tuple-element.104), channel_id=1, source_target_pairs={{8,0},{12,4},{0,8},{4,12},{24,16},{28,20},{16,24},{20,28},{40,32},... | collective-permute-start | bytes 786440 | tf_op jit(solution)/shard_map/ppermute | solution.py:41
  73.5 14.5 %collective-permute-start.23 = (bf16[2,512,128]{2,1,0:T(8,128)(2,1)S(1)}, bf16[2,512,128]{2,1,0:T(8,128)(2,1)S(1)}, u32[]{:S(2)}, u32[]{:S(2)}) collective-permute-start(bf16[2,512,128]{2,1,0:T(8,128)(2,1)S(1)} %get-tuple-element.102), channel_id=1, source_target_pairs={{4,0},{8,4},{12,8},{0,12},{20,16},{24,20},{28,24},{16,28},{36,32},... | collective-permute-start | bytes 786440 | tf_op jit(solution)/shard_map/ppermute | solution.py:41
  74.4 13.8 %collective-permute-start.15 = (bf16[64,1792]{1,0:T(8,128)(2,1)S(1)}, bf16[64,1792]{1,0:T(8,128)(2,1)S(1)}, u32[]{:S(2)}, u32[]{:S(2)}) collective-permute-start(bf16[64,1792]{1,0:T(8,128)(2,1)S(1)} %get-tuple-element.89), channel_id=1, source_target_pairs={{1,0},{2,1},{3,2},{0,3},{5,4},{6,5},{7,6},{4,7},{9,8},{10,9},{11,1... | collective-permute-start | bytes 688136 | tf_op jit(solution)/shard_map/ppermute | solution.py:31
  77.1 11.2 %collective-permute-start.20 = (bf16[64,1792]{1,0:T(8,128)(2,1)S(1)}, bf16[64,1792]{1,0:T(8,128)(2,1)S(1)}, u32[]{:S(2)}, u32[]{:S(2)}) collective-permute-start(bf16[64,1792]{1,0:T(8,128)(2,1)S(1)} %get-tuple-element.91), channel_id=1, source_target_pairs={{2,0},{3,1},{0,2},{1,3},{6,4},{7,5},{4,6},{5,7},{10,8},{11,9},{8,1... | collective-permute-start | bytes 688136 | tf_op jit(solution)/shard_map/ppermute | solution.py:31
  88.3 11.1 %collective-permute-start.26 = (bf16[2,512,128]{2,1,0:T(8,128)(2,1)S(1)}, bf16[2,512,128]{2,1,0:T(8,128)(2,1)S(1)}, u32[]{:S(2)}, u32[]{:S(2)}) collective-permute-start(bf16[2,512,128]{2,1,0:T(8,128)(2,1)S(1)} %get-tuple-element.107), channel_id=1, source_target_pairs={{16,0},{20,4},{24,8},{28,12},{32,16},{36,20},{40,24},{44,28},{48,3... | collective-permute-start | bytes 786440 | tf_op jit(solution)/shard_map/ppermute | solution.py:31
  90.3 8.1 %collective-permute-start.21 = (bf16[64,1792]{1,0:T(8,128)(2,1)S(1)}, bf16[64,1792]{1,0:T(8,128)(2,1)S(1)}, u32[]{:S(2)}, u32[]{:S(2)}) collective-permute-start(bf16[64,1792]{1,0:T(8,128)(2,1)S(1)} %get-tuple-element.93), channel_id=1, source_target_pairs={{3,0},{0,1},{1,2},{2,3},{7,4},{4,5},{5,6},{6,7},{11,8},{8,9},{9,10... | collective-permute-start | bytes 688136 | tf_op jit(solution)/shard_map/ppermute | solution.py:31

commit v4 on v3

--- a/solution.py
+++ b/solution.py
@@ -332,22 +332,17 @@
         [jax.ShapeDtypeStruct((rows, pack_cols), bf16)] * tp_count,
         [scalars()] + [whole()] * 4,
     )(meta, resp_queries, resp_dout, resp_keys, resp_values)
-    arrived = {1: shifted(packs[1], "tp", 1)}
+    arrived = {d: shifted(packs[d], "tp", d) for d in range(1, tp_count, 2)}
+    for d in range(2, tp_count, 2):
+        arrived[d] = shifted(after(packs[d], arrived), "tp", d)
+    arrived = [packs[0]] + [arrived[d] for d in range(1, tp_count)]
 
     before = [to_row(block, 1) for block in halves]
-    for d in range(2, tp_count):
-        arrived[d] = shifted(after(packs[d], (arrived[1], before[1]) if d > 2 else arrived[1]), "tp", d)
-    arrived = [packs[0]] + [arrived[d] for d in range(1, tp_count)]
     sends = [
-        list(
-            small_call(sends_kernel, "sends", [part] * (WIN - 1), [scalars()] + [whole()] * 2)(
-                after(at_row[None], packs), halves[0], before[0]
-            )
-        )
-    ] + [
         [jnp.where(at_row + offset >= ROW, before[c], halves[c]) for offset in range(1, WIN)]
-        for c in range(1, CHUNKS)
+        for c in range(CHUNKS)
     ]
+    sends[0] = list(lax.optimization_barrier(after(sends[0], packs)))
     offers = []
     for c in range(CHUNKS):
         offer = {0: halves[c]}

time: 101 us -> 96.1 us (0.951)
  waiting for transfers between devices: 38.6 us -> 36.1 us
  starting transfers between devices: 34.4 us -> 32.7 us
    ppermute x15, waiting for transfers between devices: 19.3 us -> 14.9 us  [shifted(): return lax.ppermute(block, axis, route)]
    ppermute x15, starting transfers between devices: 20.6 us -> 18.7 us  [shifted(): return lax.ppermute(block, axis, route)]
    ppermute x12, waiting for transfers between devices: 19.3 us -> 21.2 us  [along_row(): return lax.ppermute(block, 'group', route)]
  transfers between devices with their start and end apart: 27 -> 27, of which waited for: 11 -> 12; matrix products, arithmetic and copies ran while one was open for 2% -> 1% of each run, Pallas kernels for 17% -> 18%
where the time goes in v4:
time: 96.1 us; the launch traced here: 95.8 us
  waiting for transfers between devices  36.1 us (38%)
  starting transfers between devices  32.7 us (34%)
  Pallas kernels  17.9 us (19%)
  between operations  4.85 us (5%)
  local copies, waits for them, and re-layouts  2.96 us (3%)
  other arithmetic  1.31 us (1%)
    ppermute x12, waiting for transfers between devices, along_row(): return lax.ppermute(block, 'group', route)  21.2 us
    ppermute x15, starting transfers between devices, shifted(): return lax.ppermute(block, axis, route)  18.7 us
    ppermute x15, waiting for transfers between devices, shifted(): return lax.ppermute(block, axis, route)  14.9 us
    ppermute x12, starting transfers between devices, along_row(): return lax.ppermute(block, 'group', route)  14 us
    pallas_call x2, Pallas kernels, attend(): pl.pallas_call(functools.partial(attend_kernel, chunk, tp_count), out_sha...  13.7 us
    unnamed x12, local copies, waits for them, and re-layouts  2.96 us
  transfers between devices with their start and end apart: 27, of which 12 were waited for; matrix products, arithmetic and copies ran while one was open for 1% of the time, Pallas kernels for 18%

profile of v4, /device:TPU:24, one launch (start us, length us, event | category | flops | bytes accessed | tf_op | source)
XLA Modules:
  0.0 95.8 jit_solution(11997864952864096673)
XLA Ops:
  0.6 1.2 %copy-done = bf16[1,2,1024,256]{3,2,1,0:T(8,128)(2,1)S(1)} copy-done((bf16[1,2,1024,256]{3,2,1,0:T(8,128)(2,1)S(1)}, bf16[1,2,1024,256]{3,2,1,0:T(8,128)(2,1)}, u32[]{:S(2)}) %copy-start) | copy-done | bytes 1048600
  2.0 2.0 %collective-permute-start.4 = (bf16[2,512,128]{2,1,0:T(8,128)(2,1)S(1)}, bf16[2,512,128]{2,1,0:T(8,128)(2,1)S(1)}, u32[]{:S(2)}, u32[]{:S(2)}) collective-permute-start(bf16[2,512,128]{2,1,0:T(8,128)(2,1)S(1)} %get-tuple-element.57.refs_0_), channel_id=1, source_target_pairs={{112,0},{116,4},{120,8},{124,12},{0,16},{4,20},{8,24},{12,28},{16,... | collective-permute-start | bytes 786440 | tf_op jit(solution)/shard_map/ppermute | solution.py:31
  4.6 0.6 copy-done.5
  5.4 1.1 %copy-done.2 = bf16[64,5120]{1,0:T(8,128)(2,1)S(1)} copy-done((bf16[64,5120]{1,0:T(8,128)(2,1)S(1)}, bf16[64,5120]{1,0:T(8,128)(2,1)}, u32[]{:S(2)}) %copy-start.2) | copy-done | bytes 655384
  6.5 0.7 pack.1
  7.2 1.6 %collective-permute-start.1 = (bf16[64,3072]{1,0:T(8,128)(2,1)S(1)}, bf16[64,3072]{1,0:T(8,128)(2,1)S(1)}, u32[]{:S(2)}, u32[]{:S(2)}) collective-permute-start(bf16[64,3072]{1,0:T(8,128)(2,1)S(1)} %get-tuple-element.62), channel_id=1, source_target_pairs={{3,0},{0,1},{1,2},{2,3},{7,4},{4,5},{5,6},{6,7},{11,8},{8,9},{9,10... | collective-permute-start | bytes 1179656 | tf_op jit(solution)/shard_map/ppermute | solution.py:31
  8.7 1.7 %collective-permute-start.2 = (bf16[64,3072]{1,0:T(8,128)(2,1)S(1)}, bf16[64,3072]{1,0:T(8,128)(2,1)S(1)}, u32[]{:S(2)}, u32[]{:S(2)}) collective-permute-start(bf16[64,3072]{1,0:T(8,128)(2,1)S(1)} %get-tuple-element.64), channel_id=1, source_target_pairs={{1,0},{2,1},{3,2},{0,3},{5,4},{6,5},{7,6},{4,7},{9,8},{10,9},{11,1... | collective-permute-start | bytes 1179656 | tf_op jit(solution)/shard_map/ppermute | solution.py:31
  10.5 3.7 %collective-permute-done.4 = bf16[2,512,128]{2,1,0:T(8,128)(2,1)S(1)} collective-permute-done((bf16[2,512,128]{2,1,0:T(8,128)(2,1)S(1)}, bf16[2,512,128]{2,1,0:T(8,128)(2,1)S(1)}, u32[]{:S(2)}, u32[]{:S(2)}) %collective-permute-start.4) | collective-permute-done | bytes 262176 | tf_op jit(solution)/shard_map/ppermute | solution.py:31
  14.3 0.3 collective-permute-start.5
  14.6 2.6 %collective-permute-start.6 = (bf16[2,512,128]{2,1,0:T(8,128)(2,1)S(1)}, bf16[2,512,128]{2,1,0:T(8,128)(2,1)S(1)}, u32[]{:S(2)}, u32[]{:S(2)}) collective-permute-start(bf16[2,512,128]{2,1,0:T(8,128)(2,1)S(1)} %get-tuple-element.70), channel_id=1, source_target_pairs={{8,0},{12,4},{0,8},{4,12},{24,16},{28,20},{16,24},{20,28},{40,32},... | collective-permute-start | bytes 786440 | tf_op jit(solution)/shard_map/ppermute | solution.py:41
  17.2 2.8 %collective-permute-done.1.refs_1_ = bf16[64,3072]{1,0:T(8,128)(2,1)S(1)} collective-permute-done((bf16[64,3072]{1,0:T(8,128)(2,1)S(1)}, bf16[64,3072]{1,0:T(8,128)(2,1)S(1)}, u32[]{:S(2)}, u32[]{:S(2)}) %collective-permute-start.1) | collective-permute-done | bytes 393248 | tf_op jit(solution)/shard_map/ppermute | solution.py:31
  20.0 1.9 %collective-permute-start.9 = (bf16[2,512,128]{2,1,0:T(8,128)(2,1)S(1)}, bf16[2,512,128]{2,1,0:T(8,128)(2,1)S(1)}, u32[]{:S(2)}, u32[]{:S(2)}) collective-permute-start(bf16[2,512,128]{2,1,0:T(8,128)(2,1)S(1)} %get-tuple-element.58.refs_0_), channel_id=1, source_target_pairs={{112,0},{116,4},{120,8},{124,12},{0,16},{4,20},{8,24},{12,28},{16,... | collective-permute-start | bytes 786440 | tf_op jit(solution)/shard_map/ppermute | solution.py:31
  21.9 1.8 %collective-permute-start.3 = (bf16[64,3072]{1,0:T(8,128)(2,1)S(1)}, bf16[64,3072]{1,0:T(8,128)(2,1)S(1)}, u32[]{:S(2)}, u32[]{:S(2)}) collective-permute-start(bf16[64,3072]{1,0:T(8,128)(2,1)S(1)} %get-tuple-element.65), channel_id=1, source_target_pairs={{2,0},{3,1},{0,2},{1,3},{6,4},{7,5},{4,6},{5,7},{10,8},{11,9},{8,1... | collective-permute-start | bytes 1179656 | tf_op jit(solution)/shard_map/ppermute | solution.py:31
  24.4 1.0 %collective-permute-done.6.refs_2_ = bf16[2,512,128]{2,1,0:T(8,128)(2,1)S(1)} collective-permute-done((bf16[2,512,128]{2,1,0:T(8,128)(2,1)S(1)}, bf16[2,512,128]{2,1,0:T(8,128)(2,1)S(1)}, u32[]{:S(2)}, u32[]{:S(2)}) %collective-permute-start.6) | collective-permute-done | bytes 262176 | tf_op jit(solution)/shard_map/ppermute | solution.py:41
  25.4 3.7 %collective-permute-done.7.refs_3_ = bf16[2,512,128]{2,1,0:T(8,128)(2,1)S(1)} collective-permute-done((bf16[2,512,128]{2,1,0:T(8,128)(2,1)S(1)}, bf16[2,512,128]{2,1,0:T(8,128)(2,1)S(1)}, u32[]{:S(2)}, u32[]{:S(2)}) %collective-permute-start.7) | collective-permute-done | bytes 262176 | tf_op jit(solution)/shard_map/ppermute | solution.py:41
  29.1 0.8 pick.2
  29.8 0.1 collective-permute-start.8
  29.9 0.3 collective-permute-done.9
  30.3 0.9 collective-permute-start.10
  31.2 2.0 %collective-permute-start.11 = (bf16[2,512,128]{2,1,0:T(8,128)(2,1)S(1)}, bf16[2,512,128]{2,1,0:T(8,128)(2,1)S(1)}, u32[]{:S(2)}, u32[]{:S(2)}) collective-permute-start(bf16[2,512,128]{2,1,0:T(8,128)(2,1)S(1)} %get-tuple-element.79), channel_id=1, source_target_pairs={{8,0},{12,4},{0,8},{4,12},{24,16},{28,20},{16,24},{20,28},{40,32},... | collective-permute-start | bytes 786440 | tf_op jit(solution)/shard_map/ppermute | solution.py:41
  33.3 0.6 collective-permute-done.3.refs_2_
  33.9 6.8 %attend.2 = (bf16[64,896]{1,0:T(8,128)(2,1)S(1)}, bf16[64,896]{1,0:T(8,128)(2,1)S(1)}, bf16[64,896]{1,0:T(8,128)(2,1)S(1)}, bf16[64,896]{1,0:T(8,128)(2,1)S(1)},...) custom-call(s32[11]{0:T(128)S(1)} %pad_add_fusion.meta, ...), custom_call_target="tpu_custom_call" | custom-call | flops 16777216000 | bytes 6291456 | tf_op jit(solution)/shard_map/attend/pallas_call | solution.py:274
  43.5 3.2 %collective-permute-done.12.refs_3_ = bf16[2,512,128]{2,1,0:T(8,128)(2,1)S(1)} collective-permute-done((bf16[2,512,128]{2,1,0:T(8,128)(2,1)S(1)}, bf16[2,512,128]{2,1,0:T(8,128)(2,1)S(1)}, u32[]{:S(2)}, u32[]{:S(2)}) %collective-permute-start.12) | collective-permute-done | bytes 262176 | tf_op jit(solution)/shard_map/ppermute | solution.py:41
  46.7 0.8 pick.3
  47.5 0.1 collective-permute-start.13
  47.6 0.3 fusion.18
  47.9 0.6 collective-permute-start.16
  48.5 1.6 %collective-permute-start.17 = (bf16[2,512,128]{2,1,0:T(8,128)(2,1)S(1)}, bf16[2,512,128]{2,1,0:T(8,128)(2,1)S(1)}, u32[]{:S(2)}, u32[]{:S(2)}) collective-permute-start(bf16[2,512,128]{2,1,0:T(8,128)(2,1)S(1)} %get-tuple-element.87), channel_id=1, source_target_pairs={{8,0},{12,4},{0,8},{4,12},{24,16},{28,20},{16,24},{20,28},{40,32},... | collective-permute-start | bytes 786440 | tf_op jit(solution)/shard_map/ppermute | solution.py:41
  50.0 2.3 %collective-permute-start.18 = (bf16[2,512,128]{2,1,0:T(8,128)(2,1)S(1)}, bf16[2,512,128]{2,1,0:T(8,128)(2,1)S(1)}, u32[]{:S(2)}, u32[]{:S(2)}) collective-permute-start(bf16[2,512,128]{2,1,0:T(8,128)(2,1)S(1)} %get-tuple-element.88), channel_id=1, source_target_pairs={{12,0},{0,4},{4,8},{8,12},{28,16},{16,20},{20,24},{24,28},{44,32},... | collective-permute-start | bytes 786440 | tf_op jit(solution)/shard_map/ppermute | solution.py:41
  52.3 6.9 %attend.3 = (bf16[64,1792]{1,0:T(8,128)(2,1)S(1)}, bf16[64,1792]{1,0:T(8,128)(2,1)S(1)}, bf16[64,1792]{1,0:T(8,128)(2,1)S(1)}, bf16[64,1792]{1,0:T(8,128)(2,1)S(...) custom-call(s32[11]{0:T(128)S(1)} %pad_add_fusion.meta, ...), custom_call_target="tpu_custom_call" | custom-call | flops 16777216000 | bytes 6291456 | tf_op jit(solution)/shard_map/attend/pallas_call | solution.py:274
  59.3 4.2 %collective-permute-done.16 = bf16[2,512,128]{2,1,0:T(8,128)(2,1)S(1)} collective-permute-done((bf16[2,512,128]{2,1,0:T(8,128)(2,1)S(1)}, bf16[2,512,128]{2,1,0:T(8,128)(2,1)S(1)}, u32[]{:S(2)}, u32[]{:S(2)}) %collective-permute-start.16) | collective-permute-done | bytes 262176 | tf_op jit(solution)/shard_map/ppermute | solution.py:41
  63.5 0.6 collective-permute-done.18
  64.1 0.3 fusion.5
  64.4 1.5 %collective-permute-start.19 = (bf16[2,512,128]{2,1,0:T(8,128)(2,1)S(1)}, bf16[2,512,128]{2,1,0:T(8,128)(2,1)S(1)}, u32[]{:S(2)}, u32[]{:S(2)}) collective-permute-start(bf16[2,512,128]{2,1,0:T(8,128)(2,1)S(1)} %get-tuple-element.113), channel_id=1, source_target_pairs={{16,0},{20,4},{24,8},{28,12},{32,16},{36,20},{40,24},{44,28},{48,3... | collective-permute-start | bytes 786440 | tf_op jit(solution)/shard_map/ppermute | solution.py:31
  65.9 0.3 fusion.25
  66.2 2.7 %collective-permute-start.25 = (bf16[2,512,128]{2,1,0:T(8,128)(2,1)S(1)}, bf16[2,512,128]{2,1,0:T(8,128)(2,1)S(1)}, u32[]{:S(2)}, u32[]{:S(2)}) collective-permute-start(bf16[2,512,128]{2,1,0:T(8,128)(2,1)S(1)} %get-tuple-element.108), channel_id=1, source_target_pairs={{12,0},{0,4},{4,8},{8,12},{28,16},{16,20},{20,24},{24,28},{44,32},... | collective-permute-start | bytes 786440 | tf_op jit(solution)/shard_map/ppermute | solution.py:41
  68.9 0.5 collective-permute-start.24
  69.4 0.4 collective-permute-start.23
  69.8 2.8 %collective-permute-start.15 = (bf16[64,1792]{1,0:T(8,128)(2,1)S(1)}, bf16[64,1792]{1,0:T(8,128)(2,1)S(1)}, u32[]{:S(2)}, u32[]{:S(2)}) collective-permute-start(bf16[64,1792]{1,0:T(8,128)(2,1)S(1)} %get-tuple-element.91), channel_id=1, source_target_pairs={{1,0},{2,1},{3,2},{0,3},{5,4},{6,5},{7,6},{4,7},{9,8},{10,9},{11,1... | collective-permute-start | bytes 688136 | tf_op jit(solution)/shard_map/ppermute | solution.py:31
  72.6 2.5 %collective-permute-start.20 = (bf16[64,1792]{1,0:T(8,128)(2,1)S(1)}, bf16[64,1792]{1,0:T(8,128)(2,1)S(1)}, u32[]{:S(2)}, u32[]{:S(2)}) collective-permute-start(bf16[64,1792]{1,0:T(8,128)(2,1)S(1)} %get-tuple-element.93), channel_id=1, source_target_pairs={{2,0},{3,1},{0,2},{1,3},{6,4},{7,5},{4,6},{5,7},{10,8},{11,9},{8,1... | collective-permute-start | bytes 688136 | tf_op jit(solution)/shard_map/ppermute | solution.py:31
  75.1 4.9 %collective-permute-done.25 = bf16[2,512,128]{2,1,0:T(8,128)(2,1)S(1)} collective-permute-done((bf16[2,512,128]{2,1,0:T(8,128)(2,1)S(1)}, bf16[2,512,128]{2,1,0:T(8,128)(2,1)S(1)}, u32[]{:S(2)}, u32[]{:S(2)}) %collective-permute-start.25) | collective-permute-done | bytes 262176 | tf_op jit(solution)/shard_map/ppermute | solution.py:41
  80.0 3.7 %collective-permute-done.23 = bf16[2,512,128]{2,1,0:T(8,128)(2,1)S(1)} collective-permute-done((bf16[2,512,128]{2,1,0:T(8,128)(2,1)S(1)}, bf16[2,512,128]{2,1,0:T(8,128)(2,1)S(1)}, u32[]{:S(2)}, u32[]{:S(2)}) %collective-permute-start.23) | collective-permute-done | bytes 262176 | tf_op jit(solution)/shard_map/ppermute | solution.py:41
  83.6 0.3 fusion.11
  83.9 1.6 %collective-permute-start.26 = (bf16[2,512,128]{2,1,0:T(8,128)(2,1)S(1)}, bf16[2,512,128]{2,1,0:T(8,128)(2,1)S(1)}, u32[]{:S(2)}, u32[]{:S(2)}) collective-permute-start(bf16[2,512,128]{2,1,0:T(8,128)(2,1)S(1)} %get-tuple-element.109), channel_id=1, source_target_pairs={{16,0},{20,4},{24,8},{28,12},{32,16},{36,20},{40,24},{44,28},{48,3... | collective-permute-start | bytes 786440 | tf_op jit(solution)/shard_map/ppermute | solution.py:31
  85.5 1.0 %collective-permute-start.21 = (bf16[64,1792]{1,0:T(8,128)(2,1)S(1)}, bf16[64,1792]{1,0:T(8,128)(2,1)S(1)}, u32[]{:S(2)}, u32[]{:S(2)}) collective-permute-start(bf16[64,1792]{1,0:T(8,128)(2,1)S(1)} %get-tuple-element.95), channel_id=1, source_target_pairs={{3,0},{0,1},{1,2},{2,3},{7,4},{4,5},{5,6},{6,7},{11,8},{8,9},{9,10... | collective-permute-start | bytes 688136 | tf_op jit(solution)/shard_map/ppermute | solution.py:31
  86.5 7.4 %collective-permute-done.21.refs_3_ = bf16[64,1792]{1,0:T(8,128)(2,1)S(1)} collective-permute-done((bf16[64,1792]{1,0:T(8,128)(2,1)S(1)}, bf16[64,1792]{1,0:T(8,128)(2,1)S(1)}, u32[]{:S(2)}, u32[]{:S(2)}) %collective-permute-start.21) | collective-permute-done | bytes 229408 | tf_op jit(solution)/shard_map/ppermute | solution.py:31
  93.9 1.0 %unpack.1 = (bf16[64,5120]{1,0:T(8,128)(2,1)}, bf16[64,1024]{1,0:T(8,128)(2,1)}, bf16[64,1024]{1,0:T(8,128)(2,1)}) custom-call(s32[1]{0:T(128)} %bitcast.tp, bf16[64,1792]{1,0:T(8,128)(2,1)S(1)} %get-tuple-element.90.refs_0_, bf16[64,1792]{1,0:T(8,128)(2,1)S(1)} %collective-permute-done.15.refs_1_, bf16[64,1792]{1,0:T(8,128)(2,1)S(1)} %collective-permute-done.20.refs_2_, ...), custom_call_target="tpu_custom_call" | custom-call | tf_op jit(solution)/shard_map/unpack/pallas_call | solution.py:397
  94.9 0.9 finish.1
  (33 shorter events, 0.6 us)
Async XLA Ops:
  0.6 1.2 %copy-start = (bf16[1,2,1024,256]{3,2,1,0:T(8,128)(2,1)S(1)}, bf16[1,2,1024,256]{3,2,1,0:T(8,128)(2,1)}, u32[]{:S(2)}) copy-start(bf16[1,2,1024,256]{3,2,1,0:T(8,128)(2,1)} %prompt.1) | copy-start | bytes 3145732
  1.9 3.5 %copy-start.1 = (bf16[64,5120]{1,0:T(8,128)(2,1)S(1)}, bf16[64,5120]{1,0:T(8,128)(2,1)}, u32[]{:S(2)}) copy-start(bf16[64,5120]{1,0:T(8,128)(2,1)} %queries.1) | copy-start | bytes 1966084
  1.9 3.5 %copy-start.3 = (bf16[64,1024]{1,0:T(8,128)(2,1)S(1)}, bf16[64,1024]{1,0:T(8,128)(2,1)}, u32[]{:S(2)}) copy-start(bf16[64,1024]{1,0:T(8,128)(2,1)} %keys.1) | copy-start | bytes 393220
  1.9 3.5 %copy-start.4 = (bf16[64,1024]{1,0:T(8,128)(2,1)S(1)}, bf16[64,1024]{1,0:T(8,128)(2,1)}, u32[]{:S(2)}) copy-start(bf16[64,1024]{1,0:T(8,128)(2,1)} %values.1) | copy-start | bytes 393220
  2.0 12.2 %collective-permute-start.4 = (bf16[2,512,128]{2,1,0:T(8,128)(2,1)S(1)}, bf16[2,512,128]{2,1,0:T(8,128)(2,1)S(1)}, u32[]{:S(2)}, u32[]{:S(2)}) collective-permute-start(bf16[2,512,128]{2,1,0:T(8,128)(2,1)S(1)} %get-tuple-element.57.refs_0_), channel_id=1, source_target_pairs={{112,0},{116,4},{120,8},{124,12},{0,16},{4,20},{8,24},{12,28},{16,... | collective-permute-start | bytes 786440 | tf_op jit(solution)/shard_map/ppermute | solution.py:31
  4.0 1.4 %collective-permute-start = (s32[1]{0:T(128)}, s32[1]{0:T(128)}, u32[]{:S(2)}, u32[]{:S(2)}) collective-permute-start(s32[1]{0:T(128)} %param.14), channel_id=1, source_target_pairs={{128,0},{0,128},{129,1},{1,129},{130,2},{2,130},{131,3},{3,131},{1... | collective-permute-start | bytes 20 | tf_op jit(solution)/shard_map/ppermute | solution.py:31
  4.6 0.7 copy-start.5
  5.4 1.1 %copy-start.2 = (bf16[64,5120]{1,0:T(8,128)(2,1)S(1)}, bf16[64,5120]{1,0:T(8,128)(2,1)}, u32[]{:S(2)}) copy-start(bf16[64,5120]{1,0:T(8,128)(2,1)} %grad_out.1) | copy-start | bytes 1966084
  7.2 12.8 %collective-permute-start.1 = (bf16[64,3072]{1,0:T(8,128)(2,1)S(1)}, bf16[64,3072]{1,0:T(8,128)(2,1)S(1)}, u32[]{:S(2)}, u32[]{:S(2)}) collective-permute-start(bf16[64,3072]{1,0:T(8,128)(2,1)S(1)} %get-tuple-element.62), channel_id=1, source_target_pairs={{3,0},{0,1},{1,2},{2,3},{7,4},{4,5},{5,6},{6,7},{11,8},{8,9},{9,10... | collective-permute-start | bytes 1179656 | tf_op jit(solution)/shard_map/ppermute | solution.py:31
  8.7 13.2 %collective-permute-start.2 = (bf16[64,3072]{1,0:T(8,128)(2,1)S(1)}, bf16[64,3072]{1,0:T(8,128)(2,1)S(1)}, u32[]{:S(2)}, u32[]{:S(2)}) collective-permute-start(bf16[64,3072]{1,0:T(8,128)(2,1)S(1)} %get-tuple-element.64), channel_id=1, source_target_pairs={{1,0},{2,1},{3,2},{0,3},{5,4},{6,5},{7,6},{4,7},{9,8},{10,9},{11,1... | collective-permute-start | bytes 1179656 | tf_op jit(solution)/shard_map/ppermute | solution.py:31
  14.3 10.1 %collective-permute-start.5 = (bf16[2,512,128]{2,1,0:T(8,128)(2,1)S(1)}, bf16[2,512,128]{2,1,0:T(8,128)(2,1)S(1)}, u32[]{:S(2)}, u32[]{:S(2)}) collective-permute-start(bf16[2,512,128]{2,1,0:T(8,128)(2,1)S(1)} %get-tuple-element.69), channel_id=1, source_target_pairs={{12,0},{0,4},{4,8},{8,12},{28,16},{16,20},{20,24},{24,28},{44,32},... | collective-permute-start | bytes 786440 | tf_op jit(solution)/shard_map/ppermute | solution.py:41
  14.6 10.8 %collective-permute-start.6 = (bf16[2,512,128]{2,1,0:T(8,128)(2,1)S(1)}, bf16[2,512,128]{2,1,0:T(8,128)(2,1)S(1)}, u32[]{:S(2)}, u32[]{:S(2)}) collective-permute-start(bf16[2,512,128]{2,1,0:T(8,128)(2,1)S(1)} %get-tuple-element.70), channel_id=1, source_target_pairs={{8,0},{12,4},{0,8},{4,12},{24,16},{28,20},{16,24},{20,28},{40,32},... | collective-permute-start | bytes 786440 | tf_op jit(solution)/shard_map/ppermute | solution.py:41
  17.2 11.9 %collective-permute-start.7 = (bf16[2,512,128]{2,1,0:T(8,128)(2,1)S(1)}, bf16[2,512,128]{2,1,0:T(8,128)(2,1)S(1)}, u32[]{:S(2)}, u32[]{:S(2)}) collective-permute-start(bf16[2,512,128]{2,1,0:T(8,128)(2,1)S(1)} %get-tuple-element.71), channel_id=1, source_target_pairs={{4,0},{8,4},{12,8},{0,12},{20,16},{24,20},{28,24},{16,28},{36,32},... | collective-permute-start | bytes 786440 | tf_op jit(solution)/shard_map/ppermute | solution.py:41
  20.0 10.2 %collective-permute-start.9 = (bf16[2,512,128]{2,1,0:T(8,128)(2,1)S(1)}, bf16[2,512,128]{2,1,0:T(8,128)(2,1)S(1)}, u32[]{:S(2)}, u32[]{:S(2)}) collective-permute-start(bf16[2,512,128]{2,1,0:T(8,128)(2,1)S(1)} %get-tuple-element.58.refs_0_), channel_id=1, source_target_pairs={{112,0},{116,4},{120,8},{124,12},{0,16},{4,20},{8,24},{12,28},{16,... | collective-permute-start | bytes 786440 | tf_op jit(solution)/shard_map/ppermute | solution.py:31
  21.9 12.0 %collective-permute-start.3 = (bf16[64,3072]{1,0:T(8,128)(2,1)S(1)}, bf16[64,3072]{1,0:T(8,128)(2,1)S(1)}, u32[]{:S(2)}, u32[]{:S(2)}) collective-permute-start(bf16[64,3072]{1,0:T(8,128)(2,1)S(1)} %get-tuple-element.65), channel_id=1, source_target_pairs={{2,0},{3,1},{0,2},{1,3},{6,4},{7,5},{4,6},{5,7},{10,8},{11,9},{8,1... | collective-permute-start | bytes 1179656 | tf_op jit(solution)/shard_map/ppermute | solution.py:31
  29.8 3.4 %collective-permute-start.8 = (bf16[2,512,128]{2,1,0:T(8,128)(2,1)S(1)}, bf16[2,512,128]{2,1,0:T(8,128)(2,1)S(1)}, u32[]{:S(2)}, u32[]{:S(2)}) collective-permute-start(bf16[2,512,128]{2,1,0:T(8,128)(2,1)S(1)} %get-tuple-element.73), channel_id=1, source_target_pairs={{128,0},{0,128},{129,1},{1,129},{130,2},{2,130},{131,3},{3,131},{1... | collective-permute-start | bytes 786440 | tf_op jit(solution)/shard_map/ppermute | solution.py:31
  30.3 13.2 %collective-permute-start.10 = (bf16[2,512,128]{2,1,0:T(8,128)(2,1)S(1)}, bf16[2,512,128]{2,1,0:T(8,128)(2,1)S(1)}, u32[]{:S(2)}, u32[]{:S(2)}) collective-permute-start(bf16[2,512,128]{2,1,0:T(8,128)(2,1)S(1)} %get-tuple-element.78), channel_id=1, source_target_pairs={{12,0},{0,4},{4,8},{8,12},{28,16},{16,20},{20,24},{24,28},{44,32},... | collective-permute-start | bytes 786440 | tf_op jit(solution)/shard_map/ppermute | solution.py:41
  31.2 12.4 %collective-permute-start.11 = (bf16[2,512,128]{2,1,0:T(8,128)(2,1)S(1)}, bf16[2,512,128]{2,1,0:T(8,128)(2,1)S(1)}, u32[]{:S(2)}, u32[]{:S(2)}) collective-permute-start(bf16[2,512,128]{2,1,0:T(8,128)(2,1)S(1)} %get-tuple-element.79), channel_id=1, source_target_pairs={{8,0},{12,4},{0,8},{4,12},{24,16},{28,20},{16,24},{20,28},{40,32},... | collective-permute-start | bytes 786440 | tf_op jit(solution)/shard_map/ppermute | solution.py:41
  33.2 13.5 %collective-permute-start.12 = (bf16[2,512,128]{2,1,0:T(8,128)(2,1)S(1)}, bf16[2,512,128]{2,1,0:T(8,128)(2,1)S(1)}, u32[]{:S(2)}, u32[]{:S(2)}) collective-permute-start(bf16[2,512,128]{2,1,0:T(8,128)(2,1)S(1)} %get-tuple-element.80), channel_id=1, source_target_pairs={{4,0},{8,4},{12,8},{0,12},{20,16},{24,20},{28,24},{16,28},{36,32},... | collective-permute-start | bytes 786440 | tf_op jit(solution)/shard_map/ppermute | solution.py:41
  40.7 6.9 %collective-permute-start.14 = (bf16[2,512,128]{2,1,0:T(8,128)(2,1)S(1)}, bf16[2,512,128]{2,1,0:T(8,128)(2,1)S(1)}, u32[]{:S(2)}, u32[]{:S(2)}) collective-permute-start(bf16[2,512,128]{2,1,0:T(8,128)(2,1)S(1)} %get-tuple-element.84), channel_id=1, source_target_pairs={{128,0},{0,128},{129,1},{1,129},{130,2},{2,130},{131,3},{3,131},{1... | collective-permute-start | bytes 786440 | tf_op jit(solution)/shard_map/ppermute | solution.py:31
  47.5 4.9 %collective-permute-start.13 = (bf16[2,512,128]{2,1,0:T(8,128)(2,1)S(1)}, bf16[2,512,128]{2,1,0:T(8,128)(2,1)S(1)}, u32[]{:S(2)}, u32[]{:S(2)}) collective-permute-start(bf16[2,512,128]{2,1,0:T(8,128)(2,1)S(1)} %get-tuple-element.82), channel_id=1, source_target_pairs={{128,0},{0,128},{129,1},{1,129},{130,2},{2,130},{131,3},{3,131},{1... | collective-permute-start | bytes 786440 | tf_op jit(solution)/shard_map/ppermute | solution.py:31
  47.9 15.6 %collective-permute-start.16 = (bf16[2,512,128]{2,1,0:T(8,128)(2,1)S(1)}, bf16[2,512,128]{2,1,0:T(8,128)(2,1)S(1)}, u32[]{:S(2)}, u32[]{:S(2)}) collective-permute-start(bf16[2,512,128]{2,1,0:T(8,128)(2,1)S(1)} %get-tuple-element.86), channel_id=1, source_target_pairs={{4,0},{8,4},{12,8},{0,12},{20,16},{24,20},{28,24},{16,28},{36,32},... | collective-permute-start | bytes 786440 | tf_op jit(solution)/shard_map/ppermute | solution.py:41
  48.5 15.0 %collective-permute-start.17 = (bf16[2,512,128]{2,1,0:T(8,128)(2,1)S(1)}, bf16[2,512,128]{2,1,0:T(8,128)(2,1)S(1)}, u32[]{:S(2)}, u32[]{:S(2)}) collective-permute-start(bf16[2,512,128]{2,1,0:T(8,128)(2,1)S(1)} %get-tuple-element.87), channel_id=1, source_target_pairs={{8,0},{12,4},{0,8},{4,12},{24,16},{28,20},{16,24},{20,28},{40,32},... | collective-permute-start | bytes 786440 | tf_op jit(solution)/shard_map/ppermute | solution.py:41
  50.0 14.1 %collective-permute-start.18 = (bf16[2,512,128]{2,1,0:T(8,128)(2,1)S(1)}, bf16[2,512,128]{2,1,0:T(8,128)(2,1)S(1)}, u32[]{:S(2)}, u32[]{:S(2)}) collective-permute-start(bf16[2,512,128]{2,1,0:T(8,128)(2,1)S(1)} %get-tuple-element.88), channel_id=1, source_target_pairs={{12,0},{0,4},{4,8},{8,12},{28,16},{16,20},{20,24},{24,28},{44,32},... | collective-permute-start | bytes 786440 | tf_op jit(solution)/shard_map/ppermute | solution.py:41
  59.2 6.7 %collective-permute-start.22 = (bf16[2,512,128]{2,1,0:T(8,128)(2,1)S(1)}, bf16[2,512,128]{2,1,0:T(8,128)(2,1)S(1)}, u32[]{:S(2)}, u32[]{:S(2)}) collective-permute-start(bf16[2,512,128]{2,1,0:T(8,128)(2,1)S(1)} %get-tuple-element.100), channel_id=1, source_target_pairs={{128,0},{0,128},{129,1},{1,129},{130,2},{2,130},{131,3},{3,131},{1... | collective-permute-start | bytes 786440 | tf_op jit(solution)/shard_map/ppermute | solution.py:31
  64.4 8.2 %collective-permute-start.19 = (bf16[2,512,128]{2,1,0:T(8,128)(2,1)S(1)}, bf16[2,512,128]{2,1,0:T(8,128)(2,1)S(1)}, u32[]{:S(2)}, u32[]{:S(2)}) collective-permute-start(bf16[2,512,128]{2,1,0:T(8,128)(2,1)S(1)} %get-tuple-element.113), channel_id=1, source_target_pairs={{16,0},{20,4},{24,8},{28,12},{32,16},{36,20},{40,24},{44,28},{48,3... | collective-permute-start | bytes 786440 | tf_op jit(solution)/shard_map/ppermute | solution.py:31
  66.2 13.8 %collective-permute-start.25 = (bf16[2,512,128]{2,1,0:T(8,128)(2,1)S(1)}, bf16[2,512,128]{2,1,0:T(8,128)(2,1)S(1)}, u32[]{:S(2)}, u32[]{:S(2)}) collective-permute-start(bf16[2,512,128]{2,1,0:T(8,128)(2,1)S(1)} %get-tuple-element.108), channel_id=1, source_target_pairs={{12,0},{0,4},{4,8},{8,12},{28,16},{16,20},{20,24},{24,28},{44,32},... | collective-permute-start | bytes 786440 | tf_op jit(solution)/shard_map/ppermute | solution.py:41
  68.9 11.1 %collective-permute-start.24 = (bf16[2,512,128]{2,1,0:T(8,128)(2,1)S(1)}, bf16[2,512,128]{2,1,0:T(8,128)(2,1)S(1)}, u32[]{:S(2)}, u32[]{:S(2)}) collective-permute-start(bf16[2,512,128]{2,1,0:T(8,128)(2,1)S(1)} %get-tuple-element.106), channel_id=1, source_target_pairs={{8,0},{12,4},{0,8},{4,12},{24,16},{28,20},{16,24},{20,28},{40,32},... | collective-permute-start | bytes 786440 | tf_op jit(solution)/shard_map/ppermute | solution.py:41
  69.4 14.2 %collective-permute-start.23 = (bf16[2,512,128]{2,1,0:T(8,128)(2,1)S(1)}, bf16[2,512,128]{2,1,0:T(8,128)(2,1)S(1)}, u32[]{:S(2)}, u32[]{:S(2)}) collective-permute-start(bf16[2,512,128]{2,1,0:T(8,128)(2,1)S(1)} %get-tuple-element.104), channel_id=1, source_target_pairs={{4,0},{8,4},{12,8},{0,12},{20,16},{24,20},{28,24},{16,28},{36,32},... | collective-permute-start | bytes 786440 | tf_op jit(solution)/shard_map/ppermute | solution.py:41
  69.8 14.1 %collective-permute-start.15 = (bf16[64,1792]{1,0:T(8,128)(2,1)S(1)}, bf16[64,1792]{1,0:T(8,128)(2,1)S(1)}, u32[]{:S(2)}, u32[]{:S(2)}) collective-permute-start(bf16[64,1792]{1,0:T(8,128)(2,1)S(1)} %get-tuple-element.91), channel_id=1, source_target_pairs={{1,0},{2,1},{3,2},{0,3},{5,4},{6,5},{7,6},{4,7},{9,8},{10,9},{11,1... | collective-permute-start | bytes 688136 | tf_op jit(solution)/shard_map/ppermute | solution.py:31
  72.6 11.3 %collective-permute-start.20 = (bf16[64,1792]{1,0:T(8,128)(2,1)S(1)}, bf16[64,1792]{1,0:T(8,128)(2,1)S(1)}, u32[]{:S(2)}, u32[]{:S(2)}) collective-permute-start(bf16[64,1792]{1,0:T(8,128)(2,1)S(1)} %get-tuple-element.93), channel_id=1, source_target_pairs={{2,0},{3,1},{0,2},{1,3},{6,4},{7,5},{4,6},{5,7},{10,8},{11,9},{8,1... | collective-permute-start | bytes 688136 | tf_op jit(solution)/shard_map/ppermute | solution.py:31
  83.9 11.0 %collective-permute-start.26 = (bf16[2,512,128]{2,1,0:T(8,128)(2,1)S(1)}, bf16[2,512,128]{2,1,0:T(8,128)(2,1)S(1)}, u32[]{:S(2)}, u32[]{:S(2)}) collective-permute-start(bf16[2,512,128]{2,1,0:T(8,128)(2,1)S(1)} %get-tuple-element.109), channel_id=1, source_target_pairs={{16,0},{20,4},{24,8},{28,12},{32,16},{36,20},{40,24},{44,28},{48,3... | collective-permute-start | bytes 786440 | tf_op jit(solution)/shard_map/ppermute | solution.py:31
  85.5 8.4 %collective-permute-start.21 = (bf16[64,1792]{1,0:T(8,128)(2,1)S(1)}, bf16[64,1792]{1,0:T(8,128)(2,1)S(1)}, u32[]{:S(2)}, u32[]{:S(2)}) collective-permute-start(bf16[64,1792]{1,0:T(8,128)(2,1)S(1)} %get-tuple-element.95), channel_id=1, source_target_pairs={{3,0},{0,1},{1,2},{2,3},{7,4},{4,5},{5,6},{6,7},{11,8},{8,9},{9,10... | collective-permute-start | bytes 688136 | tf_op jit(solution)/shard_map/ppermute | solution.py:31

commit v5 on v4

--- a/solution.py
+++ b/solution.py
@@ -403,7 +403,7 @@
             jax.ShapeDtypeStruct(resp_values.shape, bf16),
         ],
         [scalars()] + [whole()] * tp_count,
-    )(tp, backs[0], *[returned[d] for d in range(1, tp_count)])
+    )(after(tp, prompt_grads), backs[0], *[returned[d] for d in range(1, tp_count)])
     return (grads[0], grads[1], grads[2], prompt_grads)
 
 

time: 96.1 us -> 94.9 us (0.988)
  transfers between devices with their start and end apart: 27 -> 27, of which waited for: 12 -> 13; matrix products, arithmetic and copies ran while one was open for 1% -> 1% of each run, Pallas kernels for 18% -> 17%
where the time goes in v5:
time: 94.9 us; the launch traced here: 94.7 us
  waiting for transfers between devices  35.8 us (38%)
  starting transfers between devices  32.6 us (34%)
  Pallas kernels  17.6 us (19%)
  between operations  4.34 us (5%)
  local copies, waits for them, and re-layouts  2.96 us (3%)
  other arithmetic  1.31 us (1%)
    ppermute x12, waiting for transfers between devices, along_row(): return lax.ppermute(block, 'group', route)  21.6 us
    ppermute x15, starting transfers between devices, shifted(): return lax.ppermute(block, axis, route)  18.7 us
    ppermute x15, waiting for transfers between devices, shifted(): return lax.ppermute(block, axis, route)  14.2 us
    ppermute x12, starting transfers between devices, along_row(): return lax.ppermute(block, 'group', route)  13.9 us
    pallas_call x2, Pallas kernels, attend(): pl.pallas_call(functools.partial(attend_kernel, chunk, tp_count), out_sha...  13.7 us
    unnamed x12, local copies, waits for them, and re-layouts  2.96 us
  transfers between devices with their start and end apart: 27, of which 13 were waited for; matrix products, arithmetic and copies ran while one was open for 1% of the time, Pallas kernels for 17%

profile of v5, /device:TPU:24, one launch (start us, length us, event | category | flops | bytes accessed | tf_op | source)
XLA Modules:
  0.0 94.7 jit_solution(9449248900878028070)
XLA Ops:
  0.6 1.2 %copy-done = bf16[1,2,1024,256]{3,2,1,0:T(8,128)(2,1)S(1)} copy-done((bf16[1,2,1024,256]{3,2,1,0:T(8,128)(2,1)S(1)}, bf16[1,2,1024,256]{3,2,1,0:T(8,128)(2,1)}, u32[]{:S(2)}) %copy-start) | copy-done | bytes 1048600
  2.0 2.0 %collective-permute-start.4 = (bf16[2,512,128]{2,1,0:T(8,128)(2,1)S(1)}, bf16[2,512,128]{2,1,0:T(8,128)(2,1)S(1)}, u32[]{:S(2)}, u32[]{:S(2)}) collective-permute-start(bf16[2,512,128]{2,1,0:T(8,128)(2,1)S(1)} %get-tuple-element.58.refs_0_), channel_id=1, source_target_pairs={{112,0},{116,4},{120,8},{124,12},{0,16},{4,20},{8,24},{12,28},{16,... | collective-permute-start | bytes 786440 | tf_op jit(solution)/shard_map/ppermute | solution.py:31
  4.6 0.6 copy-done.5
  5.4 1.1 %copy-done.2 = bf16[64,5120]{1,0:T(8,128)(2,1)S(1)} copy-done((bf16[64,5120]{1,0:T(8,128)(2,1)S(1)}, bf16[64,5120]{1,0:T(8,128)(2,1)}, u32[]{:S(2)}) %copy-start.2) | copy-done | bytes 655384
  6.5 0.7 pack.1
  7.2 1.6 %collective-permute-start.1 = (bf16[64,3072]{1,0:T(8,128)(2,1)S(1)}, bf16[64,3072]{1,0:T(8,128)(2,1)S(1)}, u32[]{:S(2)}, u32[]{:S(2)}) collective-permute-start(bf16[64,3072]{1,0:T(8,128)(2,1)S(1)} %get-tuple-element.63), channel_id=1, source_target_pairs={{3,0},{0,1},{1,2},{2,3},{7,4},{4,5},{5,6},{6,7},{11,8},{8,9},{9,10... | collective-permute-start | bytes 1179656 | tf_op jit(solution)/shard_map/ppermute | solution.py:31
  8.7 1.7 %collective-permute-start.2 = (bf16[64,3072]{1,0:T(8,128)(2,1)S(1)}, bf16[64,3072]{1,0:T(8,128)(2,1)S(1)}, u32[]{:S(2)}, u32[]{:S(2)}) collective-permute-start(bf16[64,3072]{1,0:T(8,128)(2,1)S(1)} %get-tuple-element.65), channel_id=1, source_target_pairs={{1,0},{2,1},{3,2},{0,3},{5,4},{6,5},{7,6},{4,7},{9,8},{10,9},{11,1... | collective-permute-start | bytes 1179656 | tf_op jit(solution)/shard_map/ppermute | solution.py:31
  10.5 3.7 %collective-permute-done.4 = bf16[2,512,128]{2,1,0:T(8,128)(2,1)S(1)} collective-permute-done((bf16[2,512,128]{2,1,0:T(8,128)(2,1)S(1)}, bf16[2,512,128]{2,1,0:T(8,128)(2,1)S(1)}, u32[]{:S(2)}, u32[]{:S(2)}) %collective-permute-start.4) | collective-permute-done | bytes 262176 | tf_op jit(solution)/shard_map/ppermute | solution.py:31
  14.3 0.3 collective-permute-start.5
  14.6 2.6 %collective-permute-start.6 = (bf16[2,512,128]{2,1,0:T(8,128)(2,1)S(1)}, bf16[2,512,128]{2,1,0:T(8,128)(2,1)S(1)}, u32[]{:S(2)}, u32[]{:S(2)}) collective-permute-start(bf16[2,512,128]{2,1,0:T(8,128)(2,1)S(1)} %get-tuple-element.71), channel_id=1, source_target_pairs={{8,0},{12,4},{0,8},{4,12},{24,16},{28,20},{16,24},{20,28},{40,32},... | collective-permute-start | bytes 786440 | tf_op jit(solution)/shard_map/ppermute | solution.py:41
  17.2 2.8 %collective-permute-done.1.refs_1_ = bf16[64,3072]{1,0:T(8,128)(2,1)S(1)} collective-permute-done((bf16[64,3072]{1,0:T(8,128)(2,1)S(1)}, bf16[64,3072]{1,0:T(8,128)(2,1)S(1)}, u32[]{:S(2)}, u32[]{:S(2)}) %collective-permute-start.1) | collective-permute-done | bytes 393248 | tf_op jit(solution)/shard_map/ppermute | solution.py:31
  20.0 1.9 %collective-permute-start.14 = (bf16[2,512,128]{2,1,0:T(8,128)(2,1)S(1)}, bf16[2,512,128]{2,1,0:T(8,128)(2,1)S(1)}, u32[]{:S(2)}, u32[]{:S(2)}) collective-permute-start(bf16[2,512,128]{2,1,0:T(8,128)(2,1)S(1)} %get-tuple-element.59.refs_0_), channel_id=1, source_target_pairs={{112,0},{116,4},{120,8},{124,12},{0,16},{4,20},{8,24},{12,28},{16,... | collective-permute-start | bytes 786440 | tf_op jit(solution)/shard_map/ppermute | solution.py:31
  21.9 1.8 %collective-permute-start.3 = (bf16[64,3072]{1,0:T(8,128)(2,1)S(1)}, bf16[64,3072]{1,0:T(8,128)(2,1)S(1)}, u32[]{:S(2)}, u32[]{:S(2)}) collective-permute-start(bf16[64,3072]{1,0:T(8,128)(2,1)S(1)} %get-tuple-element.66), channel_id=1, source_target_pairs={{2,0},{3,1},{0,2},{1,3},{6,4},{7,5},{4,6},{5,7},{10,8},{11,9},{8,1... | collective-permute-start | bytes 1179656 | tf_op jit(solution)/shard_map/ppermute | solution.py:31
  24.4 1.0 %collective-permute-done.6.refs_2_ = bf16[2,512,128]{2,1,0:T(8,128)(2,1)S(1)} collective-permute-done((bf16[2,512,128]{2,1,0:T(8,128)(2,1)S(1)}, bf16[2,512,128]{2,1,0:T(8,128)(2,1)S(1)}, u32[]{:S(2)}, u32[]{:S(2)}) %collective-permute-start.6) | collective-permute-done | bytes 262176 | tf_op jit(solution)/shard_map/ppermute | solution.py:41
  25.4 3.7 %collective-permute-done.7.refs_3_ = bf16[2,512,128]{2,1,0:T(8,128)(2,1)S(1)} collective-permute-done((bf16[2,512,128]{2,1,0:T(8,128)(2,1)S(1)}, bf16[2,512,128]{2,1,0:T(8,128)(2,1)S(1)}, u32[]{:S(2)}, u32[]{:S(2)}) %collective-permute-start.7) | collective-permute-done | bytes 262176 | tf_op jit(solution)/shard_map/ppermute | solution.py:41
  29.1 0.6 pick.2
  29.8 0.4 collective-permute-done.14
  30.3 0.8 collective-permute-start.15
  31.0 2.1 %collective-permute-start.16 = (bf16[2,512,128]{2,1,0:T(8,128)(2,1)S(1)}, bf16[2,512,128]{2,1,0:T(8,128)(2,1)S(1)}, u32[]{:S(2)}, u32[]{:S(2)}) collective-permute-start(bf16[2,512,128]{2,1,0:T(8,128)(2,1)S(1)} %get-tuple-element.86), channel_id=1, source_target_pairs={{8,0},{12,4},{0,8},{4,12},{24,16},{28,20},{16,24},{20,28},{40,32},... | collective-permute-start | bytes 786440 | tf_op jit(solution)/shard_map/ppermute | solution.py:41
  33.2 0.7 collective-permute-done.3.refs_2_
  33.9 6.8 %attend.2 = (bf16[64,896]{1,0:T(8,128)(2,1)S(1)}, bf16[64,896]{1,0:T(8,128)(2,1)S(1)}, bf16[64,896]{1,0:T(8,128)(2,1)S(1)}, bf16[64,896]{1,0:T(8,128)(2,1)S(1)},...) custom-call(s32[11]{0:T(128)S(1)} %pad_add_fusion.meta, ...), custom_call_target="tpu_custom_call" | custom-call | flops 16777216000 | bytes 6291456 | tf_op jit(solution)/shard_map/attend/pallas_call | solution.py:274
  43.0 3.5 %collective-permute-done.17.refs_3_ = bf16[2,512,128]{2,1,0:T(8,128)(2,1)S(1)} collective-permute-done((bf16[2,512,128]{2,1,0:T(8,128)(2,1)S(1)}, bf16[2,512,128]{2,1,0:T(8,128)(2,1)S(1)}, u32[]{:S(2)}, u32[]{:S(2)}) %collective-permute-start.17) | collective-permute-done | bytes 262176 | tf_op jit(solution)/shard_map/ppermute | solution.py:41
  46.6 0.6 pick.3
  47.2 0.1 collective-permute-start.18
  47.3 0.3 fusion.18
  47.6 0.6 collective-permute-start.10
  48.2 1.6 %collective-permute-start.11 = (bf16[2,512,128]{2,1,0:T(8,128)(2,1)S(1)}, bf16[2,512,128]{2,1,0:T(8,128)(2,1)S(1)}, u32[]{:S(2)}, u32[]{:S(2)}) collective-permute-start(bf16[2,512,128]{2,1,0:T(8,128)(2,1)S(1)} %get-tuple-element.79), channel_id=1, source_target_pairs={{8,0},{12,4},{0,8},{4,12},{24,16},{28,20},{16,24},{20,28},{40,32},... | collective-permute-start | bytes 786440 | tf_op jit(solution)/shard_map/ppermute | solution.py:41
  49.8 2.3 %collective-permute-start.12 = (bf16[2,512,128]{2,1,0:T(8,128)(2,1)S(1)}, bf16[2,512,128]{2,1,0:T(8,128)(2,1)S(1)}, u32[]{:S(2)}, u32[]{:S(2)}) collective-permute-start(bf16[2,512,128]{2,1,0:T(8,128)(2,1)S(1)} %get-tuple-element.80), channel_id=1, source_target_pairs={{12,0},{0,4},{4,8},{8,12},{28,16},{16,20},{20,24},{24,28},{44,32},... | collective-permute-start | bytes 786440 | tf_op jit(solution)/shard_map/ppermute | solution.py:41
  52.1 6.9 %attend.3 = (bf16[64,1792]{1,0:T(8,128)(2,1)S(1)}, bf16[64,1792]{1,0:T(8,128)(2,1)S(1)}, bf16[64,1792]{1,0:T(8,128)(2,1)S(1)}, bf16[64,1792]{1,0:T(8,128)(2,1)S(...) custom-call(s32[11]{0:T(128)S(1)} %pad_add_fusion.meta, ...), custom_call_target="tpu_custom_call" | custom-call | flops 16777216000 | bytes 6291456 | tf_op jit(solution)/shard_map/attend/pallas_call | solution.py:274
  59.0 4.2 %collective-permute-done.10 = bf16[2,512,128]{2,1,0:T(8,128)(2,1)S(1)} collective-permute-done((bf16[2,512,128]{2,1,0:T(8,128)(2,1)S(1)}, bf16[2,512,128]{2,1,0:T(8,128)(2,1)S(1)}, u32[]{:S(2)}, u32[]{:S(2)}) %collective-permute-start.10) | collective-permute-done | bytes 262176 | tf_op jit(solution)/shard_map/ppermute | solution.py:41
  63.2 0.6 collective-permute-done.12
  63.8 0.3 fusion.5
  64.1 1.5 %collective-permute-start.13 = (bf16[2,512,128]{2,1,0:T(8,128)(2,1)S(1)}, bf16[2,512,128]{2,1,0:T(8,128)(2,1)S(1)}, u32[]{:S(2)}, u32[]{:S(2)}) collective-permute-start(bf16[2,512,128]{2,1,0:T(8,128)(2,1)S(1)} %get-tuple-element.114), channel_id=1, source_target_pairs={{16,0},{20,4},{24,8},{28,12},{32,16},{36,20},{40,24},{44,28},{48,3... | collective-permute-start | bytes 786440 | tf_op jit(solution)/shard_map/ppermute | solution.py:31
  65.6 0.3 fusion.25
  65.9 2.7 %collective-permute-start.22 = (bf16[2,512,128]{2,1,0:T(8,128)(2,1)S(1)}, bf16[2,512,128]{2,1,0:T(8,128)(2,1)S(1)}, u32[]{:S(2)}, u32[]{:S(2)}) collective-permute-start(bf16[2,512,128]{2,1,0:T(8,128)(2,1)S(1)} %get-tuple-element.100), channel_id=1, source_target_pairs={{12,0},{0,4},{4,8},{8,12},{28,16},{16,20},{20,24},{24,28},{44,32},... | collective-permute-start | bytes 786440 | tf_op jit(solution)/shard_map/ppermute | solution.py:41
  68.6 0.5 collective-permute-start.21
  69.2 0.4 collective-permute-start.20
  69.6 2.7 %collective-permute-start.23 = (bf16[64,1792]{1,0:T(8,128)(2,1)S(1)}, bf16[64,1792]{1,0:T(8,128)(2,1)S(1)}, u32[]{:S(2)}, u32[]{:S(2)}) collective-permute-start(bf16[64,1792]{1,0:T(8,128)(2,1)S(1)} %get-tuple-element.101), channel_id=1, source_target_pairs={{1,0},{2,1},{3,2},{0,3},{5,4},{6,5},{7,6},{4,7},{9,8},{10,9},{11,1... | collective-permute-start | bytes 688136 | tf_op jit(solution)/shard_map/ppermute | solution.py:31
  72.3 2.5 %collective-permute-start.24 = (bf16[64,1792]{1,0:T(8,128)(2,1)S(1)}, bf16[64,1792]{1,0:T(8,128)(2,1)S(1)}, u32[]{:S(2)}, u32[]{:S(2)}) collective-permute-start(bf16[64,1792]{1,0:T(8,128)(2,1)S(1)} %get-tuple-element.103), channel_id=1, source_target_pairs={{2,0},{3,1},{0,2},{1,3},{6,4},{7,5},{4,6},{5,7},{10,8},{11,9},{8,1... | collective-permute-start | bytes 688136 | tf_op jit(solution)/shard_map/ppermute | solution.py:31
  74.8 4.9 %collective-permute-done.22 = bf16[2,512,128]{2,1,0:T(8,128)(2,1)S(1)} collective-permute-done((bf16[2,512,128]{2,1,0:T(8,128)(2,1)S(1)}, bf16[2,512,128]{2,1,0:T(8,128)(2,1)S(1)}, u32[]{:S(2)}, u32[]{:S(2)}) %collective-permute-start.22) | collective-permute-done | bytes 262176 | tf_op jit(solution)/shard_map/ppermute | solution.py:41
  79.7 3.7 %collective-permute-done.20 = bf16[2,512,128]{2,1,0:T(8,128)(2,1)S(1)} collective-permute-done((bf16[2,512,128]{2,1,0:T(8,128)(2,1)S(1)}, bf16[2,512,128]{2,1,0:T(8,128)(2,1)S(1)}, u32[]{:S(2)}, u32[]{:S(2)}) %collective-permute-start.20) | collective-permute-done | bytes 262176 | tf_op jit(solution)/shard_map/ppermute | solution.py:41
  83.4 0.3 fusion.11
  83.7 1.6 %collective-permute-start.25 = (bf16[2,512,128]{2,1,0:T(8,128)(2,1)S(1)}, bf16[2,512,128]{2,1,0:T(8,128)(2,1)S(1)}, u32[]{:S(2)}, u32[]{:S(2)}) collective-permute-start(bf16[2,512,128]{2,1,0:T(8,128)(2,1)S(1)} %get-tuple-element.104), channel_id=1, source_target_pairs={{16,0},{20,4},{24,8},{28,12},{32,16},{36,20},{40,24},{44,28},{48,3... | collective-permute-start | bytes 786440 | tf_op jit(solution)/shard_map/ppermute | solution.py:31
  85.2 1.0 %collective-permute-start.26 = (bf16[64,1792]{1,0:T(8,128)(2,1)S(1)}, bf16[64,1792]{1,0:T(8,128)(2,1)S(1)}, u32[]{:S(2)}, u32[]{:S(2)}) collective-permute-start(bf16[64,1792]{1,0:T(8,128)(2,1)S(1)} %get-tuple-element.108), channel_id=1, source_target_pairs={{3,0},{0,1},{1,2},{2,3},{7,4},{4,5},{5,6},{6,7},{11,8},{8,9},{9,10... | collective-permute-start | bytes 688136 | tf_op jit(solution)/shard_map/ppermute | solution.py:31
  86.2 5.7 %collective-permute-done.25.refs_3_ = bf16[2,512,128]{2,1,0:T(8,128)(2,1)S(1)} collective-permute-done((bf16[2,512,128]{2,1,0:T(8,128)(2,1)S(1)}, bf16[2,512,128]{2,1,0:T(8,128)(2,1)S(1)}, u32[]{:S(2)}, u32[]{:S(2)}) %collective-permute-start.25) | collective-permute-done | bytes 262176 | tf_op jit(solution)/shard_map/ppermute | solution.py:31
  91.9 0.9 finish.1
  92.8 0.8 collective-permute-done.26.refs_3_
  93.7 1.0 %unpack.1 = (bf16[64,5120]{1,0:T(8,128)(2,1)}, bf16[64,1024]{1,0:T(8,128)(2,1)}, bf16[64,1024]{1,0:T(8,128)(2,1)}) custom-call(s32[1]{0:T(128)} %bitcast.tp, bf16[64,1792]{1,0:T(8,128)(2,1)S(1)} %get-tuple-element.106.refs_0_, bf16[64,1792]{1,0:T(8,128)(2,1)S(1)} %collective-permute-done.23.refs_1_, bf16[64,1792]{1,0:T(8,128)(2,1)S(1)} %collective-permute-done.24.refs_2_, ...), custom_call_target="tpu_custom_call" | custom-call | tf_op jit(solution)/shard_map/unpack/pallas_call | solution.py:397
  (33 shorter events, 0.6 us)
Async XLA Ops:
  0.6 1.2 %copy-start = (bf16[1,2,1024,256]{3,2,1,0:T(8,128)(2,1)S(1)}, bf16[1,2,1024,256]{3,2,1,0:T(8,128)(2,1)}, u32[]{:S(2)}) copy-start(bf16[1,2,1024,256]{3,2,1,0:T(8,128)(2,1)} %prompt.1) | copy-start | bytes 3145732
  1.9 3.5 %copy-start.1 = (bf16[64,5120]{1,0:T(8,128)(2,1)S(1)}, bf16[64,5120]{1,0:T(8,128)(2,1)}, u32[]{:S(2)}) copy-start(bf16[64,5120]{1,0:T(8,128)(2,1)} %queries.1) | copy-start | bytes 1966084
  1.9 3.5 %copy-start.3 = (bf16[64,1024]{1,0:T(8,128)(2,1)S(1)}, bf16[64,1024]{1,0:T(8,128)(2,1)}, u32[]{:S(2)}) copy-start(bf16[64,1024]{1,0:T(8,128)(2,1)} %keys.1) | copy-start | bytes 393220
  1.9 3.5 %copy-start.4 = (bf16[64,1024]{1,0:T(8,128)(2,1)S(1)}, bf16[64,1024]{1,0:T(8,128)(2,1)}, u32[]{:S(2)}) copy-start(bf16[64,1024]{1,0:T(8,128)(2,1)} %values.1) | copy-start | bytes 393220
  2.0 12.2 %collective-permute-start.4 = (bf16[2,512,128]{2,1,0:T(8,128)(2,1)S(1)}, bf16[2,512,128]{2,1,0:T(8,128)(2,1)S(1)}, u32[]{:S(2)}, u32[]{:S(2)}) collective-permute-start(bf16[2,512,128]{2,1,0:T(8,128)(2,1)S(1)} %get-tuple-element.58.refs_0_), channel_id=1, source_target_pairs={{112,0},{116,4},{120,8},{124,12},{0,16},{4,20},{8,24},{12,28},{16,... | collective-permute-start | bytes 786440 | tf_op jit(solution)/shard_map/ppermute | solution.py:31
  4.0 1.4 %collective-permute-start = (s32[1]{0:T(128)}, s32[1]{0:T(128)}, u32[]{:S(2)}, u32[]{:S(2)}) collective-permute-start(s32[1]{0:T(128)} %param.14), channel_id=1, source_target_pairs={{128,0},{0,128},{129,1},{1,129},{130,2},{2,130},{131,3},{3,131},{1... | collective-permute-start | bytes 20 | tf_op jit(solution)/shard_map/ppermute | solution.py:31
  4.6 0.7 copy-start.5
  5.4 1.1 %copy-start.2 = (bf16[64,5120]{1,0:T(8,128)(2,1)S(1)}, bf16[64,5120]{1,0:T(8,128)(2,1)}, u32[]{:S(2)}) copy-start(bf16[64,5120]{1,0:T(8,128)(2,1)} %grad_out.1) | copy-start | bytes 1966084
  7.2 12.8 %collective-permute-start.1 = (bf16[64,3072]{1,0:T(8,128)(2,1)S(1)}, bf16[64,3072]{1,0:T(8,128)(2,1)S(1)}, u32[]{:S(2)}, u32[]{:S(2)}) collective-permute-start(bf16[64,3072]{1,0:T(8,128)(2,1)S(1)} %get-tuple-element.63), channel_id=1, source_target_pairs={{3,0},{0,1},{1,2},{2,3},{7,4},{4,5},{5,6},{6,7},{11,8},{8,9},{9,10... | collective-permute-start | bytes 1179656 | tf_op jit(solution)/shard_map/ppermute | solution.py:31
  8.7 13.2 %collective-permute-start.2 = (bf16[64,3072]{1,0:T(8,128)(2,1)S(1)}, bf16[64,3072]{1,0:T(8,128)(2,1)S(1)}, u32[]{:S(2)}, u32[]{:S(2)}) collective-permute-start(bf16[64,3072]{1,0:T(8,128)(2,1)S(1)} %get-tuple-element.65), channel_id=1, source_target_pairs={{1,0},{2,1},{3,2},{0,3},{5,4},{6,5},{7,6},{4,7},{9,8},{10,9},{11,1... | collective-permute-start | bytes 1179656 | tf_op jit(solution)/shard_map/ppermute | solution.py:31
  14.3 10.1 %collective-permute-start.5 = (bf16[2,512,128]{2,1,0:T(8,128)(2,1)S(1)}, bf16[2,512,128]{2,1,0:T(8,128)(2,1)S(1)}, u32[]{:S(2)}, u32[]{:S(2)}) collective-permute-start(bf16[2,512,128]{2,1,0:T(8,128)(2,1)S(1)} %get-tuple-element.70), channel_id=1, source_target_pairs={{12,0},{0,4},{4,8},{8,12},{28,16},{16,20},{20,24},{24,28},{44,32},... | collective-permute-start | bytes 786440 | tf_op jit(solution)/shard_map/ppermute | solution.py:41
  14.6 10.8 %collective-permute-start.6 = (bf16[2,512,128]{2,1,0:T(8,128)(2,1)S(1)}, bf16[2,512,128]{2,1,0:T(8,128)(2,1)S(1)}, u32[]{:S(2)}, u32[]{:S(2)}) collective-permute-start(bf16[2,512,128]{2,1,0:T(8,128)(2,1)S(1)} %get-tuple-element.71), channel_id=1, source_target_pairs={{8,0},{12,4},{0,8},{4,12},{24,16},{28,20},{16,24},{20,28},{40,32},... | collective-permute-start | bytes 786440 | tf_op jit(solution)/shard_map/ppermute | solution.py:41
  17.2 11.9 %collective-permute-start.7 = (bf16[2,512,128]{2,1,0:T(8,128)(2,1)S(1)}, bf16[2,512,128]{2,1,0:T(8,128)(2,1)S(1)}, u32[]{:S(2)}, u32[]{:S(2)}) collective-permute-start(bf16[2,512,128]{2,1,0:T(8,128)(2,1)S(1)} %get-tuple-element.72), channel_id=1, source_target_pairs={{4,0},{8,4},{12,8},{0,12},{20,16},{24,20},{28,24},{16,28},{36,32},... | collective-permute-start | bytes 786440 | tf_op jit(solution)/shard_map/ppermute | solution.py:41
  20.0 10.2 %collective-permute-start.14 = (bf16[2,512,128]{2,1,0:T(8,128)(2,1)S(1)}, bf16[2,512,128]{2,1,0:T(8,128)(2,1)S(1)}, u32[]{:S(2)}, u32[]{:S(2)}) collective-permute-start(bf16[2,512,128]{2,1,0:T(8,128)(2,1)S(1)} %get-tuple-element.59.refs_0_), channel_id=1, source_target_pairs={{112,0},{116,4},{120,8},{124,12},{0,16},{4,20},{8,24},{12,28},{16,... | collective-permute-start | bytes 786440 | tf_op jit(solution)/shard_map/ppermute | solution.py:31
  21.9 12.0 %collective-permute-start.3 = (bf16[64,3072]{1,0:T(8,128)(2,1)S(1)}, bf16[64,3072]{1,0:T(8,128)(2,1)S(1)}, u32[]{:S(2)}, u32[]{:S(2)}) collective-permute-start(bf16[64,3072]{1,0:T(8,128)(2,1)S(1)} %get-tuple-element.66), channel_id=1, source_target_pairs={{2,0},{3,1},{0,2},{1,3},{6,4},{7,5},{4,6},{5,7},{10,8},{11,9},{8,1... | collective-permute-start | bytes 1179656 | tf_op jit(solution)/shard_map/ppermute | solution.py:31
  29.7 3.5 %collective-permute-start.8 = (bf16[2,512,128]{2,1,0:T(8,128)(2,1)S(1)}, bf16[2,512,128]{2,1,0:T(8,128)(2,1)S(1)}, u32[]{:S(2)}, u32[]{:S(2)}) collective-permute-start(bf16[2,512,128]{2,1,0:T(8,128)(2,1)S(1)} %get-tuple-element.74), channel_id=1, source_target_pairs={{128,0},{0,128},{129,1},{1,129},{130,2},{2,130},{131,3},{3,131},{1... | collective-permute-start | bytes 786440 | tf_op jit(solution)/shard_map/ppermute | solution.py:31
  30.3 12.7 %collective-permute-start.15 = (bf16[2,512,128]{2,1,0:T(8,128)(2,1)S(1)}, bf16[2,512,128]{2,1,0:T(8,128)(2,1)S(1)}, u32[]{:S(2)}, u32[]{:S(2)}) collective-permute-start(bf16[2,512,128]{2,1,0:T(8,128)(2,1)S(1)} %get-tuple-element.85), channel_id=1, source_target_pairs={{12,0},{0,4},{4,8},{8,12},{28,16},{16,20},{20,24},{24,28},{44,32},... | collective-permute-start | bytes 786440 | tf_op jit(solution)/shard_map/ppermute | solution.py:41
  31.0 12.0 %collective-permute-start.16 = (bf16[2,512,128]{2,1,0:T(8,128)(2,1)S(1)}, bf16[2,512,128]{2,1,0:T(8,128)(2,1)S(1)}, u32[]{:S(2)}, u32[]{:S(2)}) collective-permute-start(bf16[2,512,128]{2,1,0:T(8,128)(2,1)S(1)} %get-tuple-element.86), channel_id=1, source_target_pairs={{8,0},{12,4},{0,8},{4,12},{24,16},{28,20},{16,24},{20,28},{40,32},... | collective-permute-start | bytes 786440 | tf_op jit(solution)/shard_map/ppermute | solution.py:41
  33.2 13.4 %collective-permute-start.17 = (bf16[2,512,128]{2,1,0:T(8,128)(2,1)S(1)}, bf16[2,512,128]{2,1,0:T(8,128)(2,1)S(1)}, u32[]{:S(2)}, u32[]{:S(2)}) collective-permute-start(bf16[2,512,128]{2,1,0:T(8,128)(2,1)S(1)} %get-tuple-element.87), channel_id=1, source_target_pairs={{4,0},{8,4},{12,8},{0,12},{20,16},{24,20},{28,24},{16,28},{36,32},... | collective-permute-start | bytes 786440 | tf_op jit(solution)/shard_map/ppermute | solution.py:41
  40.7 6.6 %collective-permute-start.9 = (bf16[2,512,128]{2,1,0:T(8,128)(2,1)S(1)}, bf16[2,512,128]{2,1,0:T(8,128)(2,1)S(1)}, u32[]{:S(2)}, u32[]{:S(2)}) collective-permute-start(bf16[2,512,128]{2,1,0:T(8,128)(2,1)S(1)} %get-tuple-element.76), channel_id=1, source_target_pairs={{128,0},{0,128},{129,1},{1,129},{130,2},{2,130},{131,3},{3,131},{1... | collective-permute-start | bytes 786440 | tf_op jit(solution)/shard_map/ppermute | solution.py:31
  47.2 4.9 %collective-permute-start.18 = (bf16[2,512,128]{2,1,0:T(8,128)(2,1)S(1)}, bf16[2,512,128]{2,1,0:T(8,128)(2,1)S(1)}, u32[]{:S(2)}, u32[]{:S(2)}) collective-permute-start(bf16[2,512,128]{2,1,0:T(8,128)(2,1)S(1)} %get-tuple-element.89), channel_id=1, source_target_pairs={{128,0},{0,128},{129,1},{1,129},{130,2},{2,130},{131,3},{3,131},{1... | collective-permute-start | bytes 786440 | tf_op jit(solution)/shard_map/ppermute | solution.py:31
  47.6 15.6 %collective-permute-start.10 = (bf16[2,512,128]{2,1,0:T(8,128)(2,1)S(1)}, bf16[2,512,128]{2,1,0:T(8,128)(2,1)S(1)}, u32[]{:S(2)}, u32[]{:S(2)}) collective-permute-start(bf16[2,512,128]{2,1,0:T(8,128)(2,1)S(1)} %get-tuple-element.78), channel_id=1, source_target_pairs={{4,0},{8,4},{12,8},{0,12},{20,16},{24,20},{28,24},{16,28},{36,32},... | collective-permute-start | bytes 786440 | tf_op jit(solution)/shard_map/ppermute | solution.py:41
  48.2 15.0 %collective-permute-start.11 = (bf16[2,512,128]{2,1,0:T(8,128)(2,1)S(1)}, bf16[2,512,128]{2,1,0:T(8,128)(2,1)S(1)}, u32[]{:S(2)}, u32[]{:S(2)}) collective-permute-start(bf16[2,512,128]{2,1,0:T(8,128)(2,1)S(1)} %get-tuple-element.79), channel_id=1, source_target_pairs={{8,0},{12,4},{0,8},{4,12},{24,16},{28,20},{16,24},{20,28},{40,32},... | collective-permute-start | bytes 786440 | tf_op jit(solution)/shard_map/ppermute | solution.py:41
  49.8 14.1 %collective-permute-start.12 = (bf16[2,512,128]{2,1,0:T(8,128)(2,1)S(1)}, bf16[2,512,128]{2,1,0:T(8,128)(2,1)S(1)}, u32[]{:S(2)}, u32[]{:S(2)}) collective-permute-start(bf16[2,512,128]{2,1,0:T(8,128)(2,1)S(1)} %get-tuple-element.80), channel_id=1, source_target_pairs={{12,0},{0,4},{4,8},{8,12},{28,16},{16,20},{20,24},{24,28},{44,32},... | collective-permute-start | bytes 786440 | tf_op jit(solution)/shard_map/ppermute | solution.py:41
  58.9 6.7 %collective-permute-start.19 = (bf16[2,512,128]{2,1,0:T(8,128)(2,1)S(1)}, bf16[2,512,128]{2,1,0:T(8,128)(2,1)S(1)}, u32[]{:S(2)}, u32[]{:S(2)}) collective-permute-start(bf16[2,512,128]{2,1,0:T(8,128)(2,1)S(1)} %get-tuple-element.92), channel_id=1, source_target_pairs={{128,0},{0,128},{129,1},{1,129},{130,2},{2,130},{131,3},{3,131},{1... | collective-permute-start | bytes 786440 | tf_op jit(solution)/shard_map/ppermute | solution.py:31
  64.1 8.2 %collective-permute-start.13 = (bf16[2,512,128]{2,1,0:T(8,128)(2,1)S(1)}, bf16[2,512,128]{2,1,0:T(8,128)(2,1)S(1)}, u32[]{:S(2)}, u32[]{:S(2)}) collective-permute-start(bf16[2,512,128]{2,1,0:T(8,128)(2,1)S(1)} %get-tuple-element.114), channel_id=1, source_target_pairs={{16,0},{20,4},{24,8},{28,12},{32,16},{36,20},{40,24},{44,28},{48,3... | collective-permute-start | bytes 786440 | tf_op jit(solution)/shard_map/ppermute | solution.py:31
  65.9 13.8 %collective-permute-start.22 = (bf16[2,512,128]{2,1,0:T(8,128)(2,1)S(1)}, bf16[2,512,128]{2,1,0:T(8,128)(2,1)S(1)}, u32[]{:S(2)}, u32[]{:S(2)}) collective-permute-start(bf16[2,512,128]{2,1,0:T(8,128)(2,1)S(1)} %get-tuple-element.100), channel_id=1, source_target_pairs={{12,0},{0,4},{4,8},{8,12},{28,16},{16,20},{20,24},{24,28},{44,32},... | collective-permute-start | bytes 786440 | tf_op jit(solution)/shard_map/ppermute | solution.py:41
  68.6 11.1 %collective-permute-start.21 = (bf16[2,512,128]{2,1,0:T(8,128)(2,1)S(1)}, bf16[2,512,128]{2,1,0:T(8,128)(2,1)S(1)}, u32[]{:S(2)}, u32[]{:S(2)}) collective-permute-start(bf16[2,512,128]{2,1,0:T(8,128)(2,1)S(1)} %get-tuple-element.98), channel_id=1, source_target_pairs={{8,0},{12,4},{0,8},{4,12},{24,16},{28,20},{16,24},{20,28},{40,32},... | collective-permute-start | bytes 786440 | tf_op jit(solution)/shard_map/ppermute | solution.py:41
  69.2 14.2 %collective-permute-start.20 = (bf16[2,512,128]{2,1,0:T(8,128)(2,1)S(1)}, bf16[2,512,128]{2,1,0:T(8,128)(2,1)S(1)}, u32[]{:S(2)}, u32[]{:S(2)}) collective-permute-start(bf16[2,512,128]{2,1,0:T(8,128)(2,1)S(1)} %get-tuple-element.96), channel_id=1, source_target_pairs={{4,0},{8,4},{12,8},{0,12},{20,16},{24,20},{28,24},{16,28},{36,32},... | collective-permute-start | bytes 786440 | tf_op jit(solution)/shard_map/ppermute | solution.py:41
  69.6 14.1 %collective-permute-start.23 = (bf16[64,1792]{1,0:T(8,128)(2,1)S(1)}, bf16[64,1792]{1,0:T(8,128)(2,1)S(1)}, u32[]{:S(2)}, u32[]{:S(2)}) collective-permute-start(bf16[64,1792]{1,0:T(8,128)(2,1)S(1)} %get-tuple-element.101), channel_id=1, source_target_pairs={{1,0},{2,1},{3,2},{0,3},{5,4},{6,5},{7,6},{4,7},{9,8},{10,9},{11,1... | collective-permute-start | bytes 688136 | tf_op jit(solution)/shard_map/ppermute | solution.py:31
  72.3 11.3 %collective-permute-start.24 = (bf16[64,1792]{1,0:T(8,128)(2,1)S(1)}, bf16[64,1792]{1,0:T(8,128)(2,1)S(1)}, u32[]{:S(2)}, u32[]{:S(2)}) collective-permute-start(bf16[64,1792]{1,0:T(8,128)(2,1)S(1)} %get-tuple-element.103), channel_id=1, source_target_pairs={{2,0},{3,1},{0,2},{1,3},{6,4},{7,5},{4,6},{5,7},{10,8},{11,9},{8,1... | collective-permute-start | bytes 688136 | tf_op jit(solution)/shard_map/ppermute | solution.py:31
  83.7 8.3 %collective-permute-start.25 = (bf16[2,512,128]{2,1,0:T(8,128)(2,1)S(1)}, bf16[2,512,128]{2,1,0:T(8,128)(2,1)S(1)}, u32[]{:S(2)}, u32[]{:S(2)}) collective-permute-start(bf16[2,512,128]{2,1,0:T(8,128)(2,1)S(1)} %get-tuple-element.104), channel_id=1, source_target_pairs={{16,0},{20,4},{24,8},{28,12},{32,16},{36,20},{40,24},{44,28},{48,3... | collective-permute-start | bytes 786440 | tf_op jit(solution)/shard_map/ppermute | solution.py:31
  85.2 8.4 %collective-permute-start.26 = (bf16[64,1792]{1,0:T(8,128)(2,1)S(1)}, bf16[64,1792]{1,0:T(8,128)(2,1)S(1)}, u32[]{:S(2)}, u32[]{:S(2)}) collective-permute-start(bf16[64,1792]{1,0:T(8,128)(2,1)S(1)} %get-tuple-element.108), channel_id=1, source_target_pairs={{3,0},{0,1},{1,2},{2,3},{7,4},{4,5},{5,6},{6,7},{11,8},{8,9},{9,10... | collective-permute-start | bytes 688136 | tf_op jit(solution)/shard_map/ppermute | solution.py:31

commit v6 on v5

--- a/solution.py
+++ b/solution.py
@@ -361,10 +361,10 @@
         other = after(shifted(wanted, "section", 1), terms)
         backs, own_grad, other_grad = attend(c, meta, arrived, backs, own, other)
         if c == CHUNKS - 1:
-            returned = {1: shifted(backs[1], "tp", -1)}
-            for d in range(2, tp_count):
-                first = after(backs[d], returned[1] if d > 2 else shares[1])
-                returned[d] = shifted(first, "tp", -d)
+            returned = {d: shifted(backs[d], "tp", -d) for d in (1, 2)}
+            shares[1] = to_row(after(shares[1], returned[1]), -1)
+            for d in range(3, tp_count):
+                returned[d] = shifted(after(backs[d], returned), "tp", -d)
         sibling_grad = after(shifted(other_grad, "section", 1), passing)
         terms = []
         for offset in range(WIN):
@@ -386,7 +386,7 @@
         if c == CHUNKS - 1:
             passed = after(passed, (returned[1], returned[2]))
         passing.append(passed)
-        shares += [kept, to_row(passed, -1)]
+        shares += [kept, passed if c < CHUNKS - 1 else to_row(passed, -1)]
 
     prompt_grads = small_call(
         finish_kernel,

time: 94.9 us -> 95.3 us (level)
  starting transfers between devices: 32.6 us -> 31.3 us
    ppermute x15, waiting for transfers between devices: 14.2 us -> 23.2 us  [shifted(): return lax.ppermute(block, axis, route)]
    ppermute x12, waiting for transfers between devices: 21.6 us -> 13.5 us  [along_row(): return lax.ppermute(block, 'group', route)]
    ppermute x15, starting transfers between devices: 18.7 us -> 17.4 us  [shifted(): return lax.ppermute(block, axis, route)]
  transfers between devices with their start and end apart: 27 -> 27, of which waited for: 13 -> 13; matrix products, arithmetic and copies ran while one was open for 1% -> 1% of each run, Pallas kernels for 17% -> 18%
where the time goes in v6:
time: 95.3 us; the launch traced here: 94.2 us
  waiting for transfers between devices  36.6 us (38%)
  starting transfers between devices  31.3 us (33%)
  Pallas kernels  17.7 us (19%)
  between operations  4.35 us (5%)
  local copies, waits for them, and re-layouts  2.96 us (3%)
  other arithmetic  1.31 us (1%)
    ppermute x15, waiting for transfers between devices, shifted(): return lax.ppermute(block, axis, route)  23.2 us
    ppermute x15, starting transfers between devices, shifted(): return lax.ppermute(block, axis, route)  17.4 us
    ppermute x12, starting transfers between devices, along_row(): return lax.ppermute(block, 'group', route)  13.9 us
    pallas_call x2, Pallas kernels, attend(): pl.pallas_call(functools.partial(attend_kernel, chunk, tp_count), out_sha...  13.7 us
    ppermute x12, waiting for transfers between devices, along_row(): return lax.ppermute(block, 'group', route)  13.5 us
    unnamed x12, local copies, waits for them, and re-layouts  2.96 us
  transfers between devices with their start and end apart: 27, of which 13 were waited for; matrix products, arithmetic and copies ran while one was open for 1% of the time, Pallas kernels for 18%

profile of v6, /device:TPU:24, one launch (start us, length us, event | category | flops | bytes accessed | tf_op | source)
XLA Modules:
  0.0 94.2 jit_solution(6303788528410996740)
XLA Ops:
  0.6 1.2 %copy-done = bf16[1,2,1024,256]{3,2,1,0:T(8,128)(2,1)S(1)} copy-done((bf16[1,2,1024,256]{3,2,1,0:T(8,128)(2,1)S(1)}, bf16[1,2,1024,256]{3,2,1,0:T(8,128)(2,1)}, u32[]{:S(2)}) %copy-start) | copy-done | bytes 1048600
  2.0 2.0 %collective-permute-start.4 = (bf16[2,512,128]{2,1,0:T(8,128)(2,1)S(1)}, bf16[2,512,128]{2,1,0:T(8,128)(2,1)S(1)}, u32[]{:S(2)}, u32[]{:S(2)}) collective-permute-start(bf16[2,512,128]{2,1,0:T(8,128)(2,1)S(1)} %get-tuple-element.58.refs_0_), channel_id=1, source_target_pairs={{112,0},{116,4},{120,8},{124,12},{0,16},{4,20},{8,24},{12,28},{16,... | collective-permute-start | bytes 786440 | tf_op jit(solution)/shard_map/ppermute | solution.py:31
  4.6 0.6 copy-done.5
  5.4 1.1 %copy-done.2 = bf16[64,5120]{1,0:T(8,128)(2,1)S(1)} copy-done((bf16[64,5120]{1,0:T(8,128)(2,1)S(1)}, bf16[64,5120]{1,0:T(8,128)(2,1)}, u32[]{:S(2)}) %copy-start.2) | copy-done | bytes 655384
  6.5 0.7 pack.1
  7.2 1.6 %collective-permute-start.1 = (bf16[64,3072]{1,0:T(8,128)(2,1)S(1)}, bf16[64,3072]{1,0:T(8,128)(2,1)S(1)}, u32[]{:S(2)}, u32[]{:S(2)}) collective-permute-start(bf16[64,3072]{1,0:T(8,128)(2,1)S(1)} %get-tuple-element.63), channel_id=1, source_target_pairs={{3,0},{0,1},{1,2},{2,3},{7,4},{4,5},{5,6},{6,7},{11,8},{8,9},{9,10... | collective-permute-start | bytes 1179656 | tf_op jit(solution)/shard_map/ppermute | solution.py:31
  8.7 1.7 %collective-permute-start.2 = (bf16[64,3072]{1,0:T(8,128)(2,1)S(1)}, bf16[64,3072]{1,0:T(8,128)(2,1)S(1)}, u32[]{:S(2)}, u32[]{:S(2)}) collective-permute-start(bf16[64,3072]{1,0:T(8,128)(2,1)S(1)} %get-tuple-element.65), channel_id=1, source_target_pairs={{1,0},{2,1},{3,2},{0,3},{5,4},{6,5},{7,6},{4,7},{9,8},{10,9},{11,1... | collective-permute-start | bytes 1179656 | tf_op jit(solution)/shard_map/ppermute | solution.py:31
  10.5 3.7 %collective-permute-done.4 = bf16[2,512,128]{2,1,0:T(8,128)(2,1)S(1)} collective-permute-done((bf16[2,512,128]{2,1,0:T(8,128)(2,1)S(1)}, bf16[2,512,128]{2,1,0:T(8,128)(2,1)S(1)}, u32[]{:S(2)}, u32[]{:S(2)}) %collective-permute-start.4) | collective-permute-done | bytes 262176 | tf_op jit(solution)/shard_map/ppermute | solution.py:31
  14.3 0.3 collective-permute-start.5
  14.6 2.6 %collective-permute-start.6 = (bf16[2,512,128]{2,1,0:T(8,128)(2,1)S(1)}, bf16[2,512,128]{2,1,0:T(8,128)(2,1)S(1)}, u32[]{:S(2)}, u32[]{:S(2)}) collective-permute-start(bf16[2,512,128]{2,1,0:T(8,128)(2,1)S(1)} %get-tuple-element.71), channel_id=1, source_target_pairs={{8,0},{12,4},{0,8},{4,12},{24,16},{28,20},{16,24},{20,28},{40,32},... | collective-permute-start | bytes 786440 | tf_op jit(solution)/shard_map/ppermute | solution.py:41
  17.2 2.8 %collective-permute-done.1.refs_1_ = bf16[64,3072]{1,0:T(8,128)(2,1)S(1)} collective-permute-done((bf16[64,3072]{1,0:T(8,128)(2,1)S(1)}, bf16[64,3072]{1,0:T(8,128)(2,1)S(1)}, u32[]{:S(2)}, u32[]{:S(2)}) %collective-permute-start.1) | collective-permute-done | bytes 393248 | tf_op jit(solution)/shard_map/ppermute | solution.py:31
  20.0 1.9 %collective-permute-start.13 = (bf16[2,512,128]{2,1,0:T(8,128)(2,1)S(1)}, bf16[2,512,128]{2,1,0:T(8,128)(2,1)S(1)}, u32[]{:S(2)}, u32[]{:S(2)}) collective-permute-start(bf16[2,512,128]{2,1,0:T(8,128)(2,1)S(1)} %get-tuple-element.59.refs_0_), channel_id=1, source_target_pairs={{112,0},{116,4},{120,8},{124,12},{0,16},{4,20},{8,24},{12,28},{16,... | collective-permute-start | bytes 786440 | tf_op jit(solution)/shard_map/ppermute | solution.py:31
  21.9 1.8 %collective-permute-start.3 = (bf16[64,3072]{1,0:T(8,128)(2,1)S(1)}, bf16[64,3072]{1,0:T(8,128)(2,1)S(1)}, u32[]{:S(2)}, u32[]{:S(2)}) collective-permute-start(bf16[64,3072]{1,0:T(8,128)(2,1)S(1)} %get-tuple-element.66), channel_id=1, source_target_pairs={{2,0},{3,1},{0,2},{1,3},{6,4},{7,5},{4,6},{5,7},{10,8},{11,9},{8,1... | collective-permute-start | bytes 1179656 | tf_op jit(solution)/shard_map/ppermute | solution.py:31
  24.4 1.0 %collective-permute-done.6.refs_2_ = bf16[2,512,128]{2,1,0:T(8,128)(2,1)S(1)} collective-permute-done((bf16[2,512,128]{2,1,0:T(8,128)(2,1)S(1)}, bf16[2,512,128]{2,1,0:T(8,128)(2,1)S(1)}, u32[]{:S(2)}, u32[]{:S(2)}) %collective-permute-start.6) | collective-permute-done | bytes 262176 | tf_op jit(solution)/shard_map/ppermute | solution.py:41
  25.4 3.7 %collective-permute-done.7.refs_3_ = bf16[2,512,128]{2,1,0:T(8,128)(2,1)S(1)} collective-permute-done((bf16[2,512,128]{2,1,0:T(8,128)(2,1)S(1)}, bf16[2,512,128]{2,1,0:T(8,128)(2,1)S(1)}, u32[]{:S(2)}, u32[]{:S(2)}) %collective-permute-start.7) | collective-permute-done | bytes 262176 | tf_op jit(solution)/shard_map/ppermute | solution.py:41
  29.1 0.6 pick.2
  29.8 0.4 collective-permute-done.13
  30.3 0.8 collective-permute-start.14
  31.0 2.1 %collective-permute-start.15 = (bf16[2,512,128]{2,1,0:T(8,128)(2,1)S(1)}, bf16[2,512,128]{2,1,0:T(8,128)(2,1)S(1)}, u32[]{:S(2)}, u32[]{:S(2)}) collective-permute-start(bf16[2,512,128]{2,1,0:T(8,128)(2,1)S(1)} %get-tuple-element.86), channel_id=1, source_target_pairs={{8,0},{12,4},{0,8},{4,12},{24,16},{28,20},{16,24},{20,28},{40,32},... | collective-permute-start | bytes 786440 | tf_op jit(solution)/shard_map/ppermute | solution.py:41
  33.2 0.7 collective-permute-done.3.refs_2_
  33.9 6.8 %attend.2 = (bf16[64,896]{1,0:T(8,128)(2,1)S(1)}, bf16[64,896]{1,0:T(8,128)(2,1)S(1)}, bf16[64,896]{1,0:T(8,128)(2,1)S(1)}, bf16[64,896]{1,0:T(8,128)(2,1)S(1)},...) custom-call(s32[11]{0:T(128)S(1)} %pad_add_fusion.meta, ...), custom_call_target="tpu_custom_call" | custom-call | flops 16777216000 | bytes 6291456 | tf_op jit(solution)/shard_map/attend/pallas_call | solution.py:274
  43.0 3.5 %collective-permute-done.16.refs_3_ = bf16[2,512,128]{2,1,0:T(8,128)(2,1)S(1)} collective-permute-done((bf16[2,512,128]{2,1,0:T(8,128)(2,1)S(1)}, bf16[2,512,128]{2,1,0:T(8,128)(2,1)S(1)}, u32[]{:S(2)}, u32[]{:S(2)}) %collective-permute-start.16) | collective-permute-done | bytes 262176 | tf_op jit(solution)/shard_map/ppermute | solution.py:41
  46.6 0.6 pick.3
  47.2 0.1 collective-permute-start.17
  47.3 0.3 fusion.18
  47.6 0.6 collective-permute-start.10
  48.2 1.6 %collective-permute-start.11 = (bf16[2,512,128]{2,1,0:T(8,128)(2,1)S(1)}, bf16[2,512,128]{2,1,0:T(8,128)(2,1)S(1)}, u32[]{:S(2)}, u32[]{:S(2)}) collective-permute-start(bf16[2,512,128]{2,1,0:T(8,128)(2,1)S(1)} %get-tuple-element.79), channel_id=1, source_target_pairs={{8,0},{12,4},{0,8},{4,12},{24,16},{28,20},{16,24},{20,28},{40,32},... | collective-permute-start | bytes 786440 | tf_op jit(solution)/shard_map/ppermute | solution.py:41
  49.8 2.3 %collective-permute-start.12 = (bf16[2,512,128]{2,1,0:T(8,128)(2,1)S(1)}, bf16[2,512,128]{2,1,0:T(8,128)(2,1)S(1)}, u32[]{:S(2)}, u32[]{:S(2)}) collective-permute-start(bf16[2,512,128]{2,1,0:T(8,128)(2,1)S(1)} %get-tuple-element.80), channel_id=1, source_target_pairs={{12,0},{0,4},{4,8},{8,12},{28,16},{16,20},{20,24},{24,28},{44,32},... | collective-permute-start | bytes 786440 | tf_op jit(solution)/shard_map/ppermute | solution.py:41
  52.1 6.9 %attend.3 = (bf16[64,1792]{1,0:T(8,128)(2,1)S(1)}, bf16[64,1792]{1,0:T(8,128)(2,1)S(1)}, bf16[64,1792]{1,0:T(8,128)(2,1)S(1)}, bf16[64,1792]{1,0:T(8,128)(2,1)S(...) custom-call(s32[11]{0:T(128)S(1)} %pad_add_fusion.meta, ...), custom_call_target="tpu_custom_call" | custom-call | flops 16777216000 | bytes 6291456 | tf_op jit(solution)/shard_map/attend/pallas_call | solution.py:274
  59.0 4.2 %collective-permute-done.10 = bf16[2,512,128]{2,1,0:T(8,128)(2,1)S(1)} collective-permute-done((bf16[2,512,128]{2,1,0:T(8,128)(2,1)S(1)}, bf16[2,512,128]{2,1,0:T(8,128)(2,1)S(1)}, u32[]{:S(2)}, u32[]{:S(2)}) %collective-permute-start.10) | collective-permute-done | bytes 262176 | tf_op jit(solution)/shard_map/ppermute | solution.py:41
  63.2 0.6 collective-permute-done.12
  63.8 0.3 fusion.5
  64.1 0.3 fusion.25
  64.4 2.7 %collective-permute-start.23 = (bf16[2,512,128]{2,1,0:T(8,128)(2,1)S(1)}, bf16[2,512,128]{2,1,0:T(8,128)(2,1)S(1)}, u32[]{:S(2)}, u32[]{:S(2)}) collective-permute-start(bf16[2,512,128]{2,1,0:T(8,128)(2,1)S(1)} %get-tuple-element.102), channel_id=1, source_target_pairs={{12,0},{0,4},{4,8},{8,12},{28,16},{16,20},{20,24},{24,28},{44,32},... | collective-permute-start | bytes 786440 | tf_op jit(solution)/shard_map/ppermute | solution.py:41
  67.1 0.5 collective-permute-start.22
  67.7 0.4 collective-permute-start.21
  68.1 2.8 %collective-permute-start.18 = (bf16[64,1792]{1,0:T(8,128)(2,1)S(1)}, bf16[64,1792]{1,0:T(8,128)(2,1)S(1)}, u32[]{:S(2)}, u32[]{:S(2)}) collective-permute-start(bf16[64,1792]{1,0:T(8,128)(2,1)S(1)} %get-tuple-element.91), channel_id=1, source_target_pairs={{1,0},{2,1},{3,2},{0,3},{5,4},{6,5},{7,6},{4,7},{9,8},{10,9},{11,1... | collective-permute-start | bytes 688136 | tf_op jit(solution)/shard_map/ppermute | solution.py:31
  70.9 0.8 collective-permute-start.24
  71.7 8.6 %collective-permute-done.18.refs_1_ = bf16[64,1792]{1,0:T(8,128)(2,1)S(1)} collective-permute-done((bf16[64,1792]{1,0:T(8,128)(2,1)S(1)}, bf16[64,1792]{1,0:T(8,128)(2,1)S(1)}, u32[]{:S(2)}, u32[]{:S(2)}) %collective-permute-start.18) | collective-permute-done | bytes 229408 | tf_op jit(solution)/shard_map/ppermute | solution.py:31
  80.3 1.4 %collective-permute-start.19 = (bf16[2,512,128]{2,1,0:T(8,128)(2,1)S(1)}, bf16[2,512,128]{2,1,0:T(8,128)(2,1)S(1)}, u32[]{:S(2)}, u32[]{:S(2)}) collective-permute-start(bf16[2,512,128]{2,1,0:T(8,128)(2,1)S(1)} %get-tuple-element.92), channel_id=1, source_target_pairs={{16,0},{20,4},{24,8},{28,12},{32,16},{36,20},{40,24},{44,28},{48,3... | collective-permute-start | bytes 786440 | tf_op jit(solution)/shard_map/ppermute | solution.py:31
  81.7 0.5 collective-permute-done.21
  82.2 0.3 fusion.11
  82.4 1.5 %collective-permute-start.25 = (bf16[2,512,128]{2,1,0:T(8,128)(2,1)S(1)}, bf16[2,512,128]{2,1,0:T(8,128)(2,1)S(1)}, u32[]{:S(2)}, u32[]{:S(2)}) collective-permute-start(bf16[2,512,128]{2,1,0:T(8,128)(2,1)S(1)} %get-tuple-element.104), channel_id=1, source_target_pairs={{16,0},{20,4},{24,8},{28,12},{32,16},{36,20},{40,24},{44,28},{48,3... | collective-permute-start | bytes 786440 | tf_op jit(solution)/shard_map/ppermute | solution.py:31
  83.9 1.5 %collective-permute-start.26 = (bf16[64,1792]{1,0:T(8,128)(2,1)S(1)}, bf16[64,1792]{1,0:T(8,128)(2,1)S(1)}, u32[]{:S(2)}, u32[]{:S(2)}) collective-permute-start(bf16[64,1792]{1,0:T(8,128)(2,1)S(1)} %get-tuple-element.108), channel_id=1, source_target_pairs={{3,0},{0,1},{1,2},{2,3},{7,4},{4,5},{5,6},{6,7},{11,8},{8,9},{9,10... | collective-permute-start | bytes 688136 | tf_op jit(solution)/shard_map/ppermute | solution.py:31
  85.4 2.8 %collective-permute-done.19.refs_1_ = bf16[2,512,128]{2,1,0:T(8,128)(2,1)S(1)} collective-permute-done((bf16[2,512,128]{2,1,0:T(8,128)(2,1)S(1)}, bf16[2,512,128]{2,1,0:T(8,128)(2,1)S(1)}, u32[]{:S(2)}, u32[]{:S(2)}) %collective-permute-start.19) | collective-permute-done | bytes 262176 | tf_op jit(solution)/shard_map/ppermute | solution.py:31
  88.2 4.1 %collective-permute-done.25.refs_3_ = bf16[2,512,128]{2,1,0:T(8,128)(2,1)S(1)} collective-permute-done((bf16[2,512,128]{2,1,0:T(8,128)(2,1)S(1)}, bf16[2,512,128]{2,1,0:T(8,128)(2,1)S(1)}, u32[]{:S(2)}, u32[]{:S(2)}) %collective-permute-start.25) | collective-permute-done | bytes 262176 | tf_op jit(solution)/shard_map/ppermute | solution.py:31
  92.3 0.9 finish.1
  93.2 1.0 %unpack.1 = (bf16[64,5120]{1,0:T(8,128)(2,1)}, bf16[64,1024]{1,0:T(8,128)(2,1)}, bf16[64,1024]{1,0:T(8,128)(2,1)}) custom-call(s32[1]{0:T(128)} %bitcast.tp, bf16[64,1792]{1,0:T(8,128)(2,1)S(1)} %get-tuple-element.106.refs_0_, bf16[64,1792]{1,0:T(8,128)(2,1)S(1)} %collective-permute-done.18.refs_1_, bf16[64,1792]{1,0:T(8,128)(2,1)S(1)} %collective-permute-done.24.refs_2_, ...), custom_call_target="tpu_custom_call" | custom-call | tf_op jit(solution)/shard_map/unpack/pallas_call | solution.py:397
  (33 shorter events, 0.6 us)
Async XLA Ops:
  0.6 1.2 %copy-start = (bf16[1,2,1024,256]{3,2,1,0:T(8,128)(2,1)S(1)}, bf16[1,2,1024,256]{3,2,1,0:T(8,128)(2,1)}, u32[]{:S(2)}) copy-start(bf16[1,2,1024,256]{3,2,1,0:T(8,128)(2,1)} %prompt.1) | copy-start | bytes 3145732
  1.9 3.5 %copy-start.1 = (bf16[64,5120]{1,0:T(8,128)(2,1)S(1)}, bf16[64,5120]{1,0:T(8,128)(2,1)}, u32[]{:S(2)}) copy-start(bf16[64,5120]{1,0:T(8,128)(2,1)} %queries.1) | copy-start | bytes 1966084
  1.9 3.5 %copy-start.3 = (bf16[64,1024]{1,0:T(8,128)(2,1)S(1)}, bf16[64,1024]{1,0:T(8,128)(2,1)}, u32[]{:S(2)}) copy-start(bf16[64,1024]{1,0:T(8,128)(2,1)} %keys.1) | copy-start | bytes 393220
  1.9 3.5 %copy-start.4 = (bf16[64,1024]{1,0:T(8,128)(2,1)S(1)}, bf16[64,1024]{1,0:T(8,128)(2,1)}, u32[]{:S(2)}) copy-start(bf16[64,1024]{1,0:T(8,128)(2,1)} %values.1) | copy-start | bytes 393220
  2.0 12.2 %collective-permute-start.4 = (bf16[2,512,128]{2,1,0:T(8,128)(2,1)S(1)}, bf16[2,512,128]{2,1,0:T(8,128)(2,1)S(1)}, u32[]{:S(2)}, u32[]{:S(2)}) collective-permute-start(bf16[2,512,128]{2,1,0:T(8,128)(2,1)S(1)} %get-tuple-element.58.refs_0_), channel_id=1, source_target_pairs={{112,0},{116,4},{120,8},{124,12},{0,16},{4,20},{8,24},{12,28},{16,... | collective-permute-start | bytes 786440 | tf_op jit(solution)/shard_map/ppermute | solution.py:31
  4.0 1.4 %collective-permute-start = (s32[1]{0:T(128)}, s32[1]{0:T(128)}, u32[]{:S(2)}, u32[]{:S(2)}) collective-permute-start(s32[1]{0:T(128)} %param.14), channel_id=1, source_target_pairs={{128,0},{0,128},{129,1},{1,129},{130,2},{2,130},{131,3},{3,131},{1... | collective-permute-start | bytes 20 | tf_op jit(solution)/shard_map/ppermute | solution.py:31
  4.6 0.7 copy-start.5
  5.4 1.1 %copy-start.2 = (bf16[64,5120]{1,0:T(8,128)(2,1)S(1)}, bf16[64,5120]{1,0:T(8,128)(2,1)}, u32[]{:S(2)}) copy-start(bf16[64,5120]{1,0:T(8,128)(2,1)} %grad_out.1) | copy-start | bytes 1966084
  7.2 12.8 %collective-permute-start.1 = (bf16[64,3072]{1,0:T(8,128)(2,1)S(1)}, bf16[64,3072]{1,0:T(8,128)(2,1)S(1)}, u32[]{:S(2)}, u32[]{:S(2)}) collective-permute-start(bf16[64,3072]{1,0:T(8,128)(2,1)S(1)} %get-tuple-element.63), channel_id=1, source_target_pairs={{3,0},{0,1},{1,2},{2,3},{7,4},{4,5},{5,6},{6,7},{11,8},{8,9},{9,10... | collective-permute-start | bytes 1179656 | tf_op jit(solution)/shard_map/ppermute | solution.py:31
  8.7 13.2 %collective-permute-start.2 = (bf16[64,3072]{1,0:T(8,128)(2,1)S(1)}, bf16[64,3072]{1,0:T(8,128)(2,1)S(1)}, u32[]{:S(2)}, u32[]{:S(2)}) collective-permute-start(bf16[64,3072]{1,0:T(8,128)(2,1)S(1)} %get-tuple-element.65), channel_id=1, source_target_pairs={{1,0},{2,1},{3,2},{0,3},{5,4},{6,5},{7,6},{4,7},{9,8},{10,9},{11,1... | collective-permute-start | bytes 1179656 | tf_op jit(solution)/shard_map/ppermute | solution.py:31
  14.3 10.1 %collective-permute-start.5 = (bf16[2,512,128]{2,1,0:T(8,128)(2,1)S(1)}, bf16[2,512,128]{2,1,0:T(8,128)(2,1)S(1)}, u32[]{:S(2)}, u32[]{:S(2)}) collective-permute-start(bf16[2,512,128]{2,1,0:T(8,128)(2,1)S(1)} %get-tuple-element.70), channel_id=1, source_target_pairs={{12,0},{0,4},{4,8},{8,12},{28,16},{16,20},{20,24},{24,28},{44,32},... | collective-permute-start | bytes 786440 | tf_op jit(solution)/shard_map/ppermute | solution.py:41
  14.6 10.8 %collective-permute-start.6 = (bf16[2,512,128]{2,1,0:T(8,128)(2,1)S(1)}, bf16[2,512,128]{2,1,0:T(8,128)(2,1)S(1)}, u32[]{:S(2)}, u32[]{:S(2)}) collective-permute-start(bf16[2,512,128]{2,1,0:T(8,128)(2,1)S(1)} %get-tuple-element.71), channel_id=1, source_target_pairs={{8,0},{12,4},{0,8},{4,12},{24,16},{28,20},{16,24},{20,28},{40,32},... | collective-permute-start | bytes 786440 | tf_op jit(solution)/shard_map/ppermute | solution.py:41
  17.2 11.9 %collective-permute-start.7 = (bf16[2,512,128]{2,1,0:T(8,128)(2,1)S(1)}, bf16[2,512,128]{2,1,0:T(8,128)(2,1)S(1)}, u32[]{:S(2)}, u32[]{:S(2)}) collective-permute-start(bf16[2,512,128]{2,1,0:T(8,128)(2,1)S(1)} %get-tuple-element.72), channel_id=1, source_target_pairs={{4,0},{8,4},{12,8},{0,12},{20,16},{24,20},{28,24},{16,28},{36,32},... | collective-permute-start | bytes 786440 | tf_op jit(solution)/shard_map/ppermute | solution.py:41
  20.0 10.2 %collective-permute-start.13 = (bf16[2,512,128]{2,1,0:T(8,128)(2,1)S(1)}, bf16[2,512,128]{2,1,0:T(8,128)(2,1)S(1)}, u32[]{:S(2)}, u32[]{:S(2)}) collective-permute-start(bf16[2,512,128]{2,1,0:T(8,128)(2,1)S(1)} %get-tuple-element.59.refs_0_), channel_id=1, source_target_pairs={{112,0},{116,4},{120,8},{124,12},{0,16},{4,20},{8,24},{12,28},{16,... | collective-permute-start | bytes 786440 | tf_op jit(solution)/shard_map/ppermute | solution.py:31
  21.9 12.0 %collective-permute-start.3 = (bf16[64,3072]{1,0:T(8,128)(2,1)S(1)}, bf16[64,3072]{1,0:T(8,128)(2,1)S(1)}, u32[]{:S(2)}, u32[]{:S(2)}) collective-permute-start(bf16[64,3072]{1,0:T(8,128)(2,1)S(1)} %get-tuple-element.66), channel_id=1, source_target_pairs={{2,0},{3,1},{0,2},{1,3},{6,4},{7,5},{4,6},{5,7},{10,8},{11,9},{8,1... | collective-permute-start | bytes 1179656 | tf_op jit(solution)/shard_map/ppermute | solution.py:31
  29.7 3.5 %collective-permute-start.8 = (bf16[2,512,128]{2,1,0:T(8,128)(2,1)S(1)}, bf16[2,512,128]{2,1,0:T(8,128)(2,1)S(1)}, u32[]{:S(2)}, u32[]{:S(2)}) collective-permute-start(bf16[2,512,128]{2,1,0:T(8,128)(2,1)S(1)} %get-tuple-element.74), channel_id=1, source_target_pairs={{128,0},{0,128},{129,1},{1,129},{130,2},{2,130},{131,3},{3,131},{1... | collective-permute-start | bytes 786440 | tf_op jit(solution)/shard_map/ppermute | solution.py:31
  30.3 12.7 %collective-permute-start.14 = (bf16[2,512,128]{2,1,0:T(8,128)(2,1)S(1)}, bf16[2,512,128]{2,1,0:T(8,128)(2,1)S(1)}, u32[]{:S(2)}, u32[]{:S(2)}) collective-permute-start(bf16[2,512,128]{2,1,0:T(8,128)(2,1)S(1)} %get-tuple-element.85), channel_id=1, source_target_pairs={{12,0},{0,4},{4,8},{8,12},{28,16},{16,20},{20,24},{24,28},{44,32},... | collective-permute-start | bytes 786440 | tf_op jit(solution)/shard_map/ppermute | solution.py:41
  31.0 12.0 %collective-permute-start.15 = (bf16[2,512,128]{2,1,0:T(8,128)(2,1)S(1)}, bf16[2,512,128]{2,1,0:T(8,128)(2,1)S(1)}, u32[]{:S(2)}, u32[]{:S(2)}) collective-permute-start(bf16[2,512,128]{2,1,0:T(8,128)(2,1)S(1)} %get-tuple-element.86), channel_id=1, source_target_pairs={{8,0},{12,4},{0,8},{4,12},{24,16},{28,20},{16,24},{20,28},{40,32},... | collective-permute-start | bytes 786440 | tf_op jit(solution)/shard_map/ppermute | solution.py:41
  33.2 13.4 %collective-permute-start.16 = (bf16[2,512,128]{2,1,0:T(8,128)(2,1)S(1)}, bf16[2,512,128]{2,1,0:T(8,128)(2,1)S(1)}, u32[]{:S(2)}, u32[]{:S(2)}) collective-permute-start(bf16[2,512,128]{2,1,0:T(8,128)(2,1)S(1)} %get-tuple-element.87), channel_id=1, source_target_pairs={{4,0},{8,4},{12,8},{0,12},{20,16},{24,20},{28,24},{16,28},{36,32},... | collective-permute-start | bytes 786440 | tf_op jit(solution)/shard_map/ppermute | solution.py:41
  40.7 6.6 %collective-permute-start.9 = (bf16[2,512,128]{2,1,0:T(8,128)(2,1)S(1)}, bf16[2,512,128]{2,1,0:T(8,128)(2,1)S(1)}, u32[]{:S(2)}, u32[]{:S(2)}) collective-permute-start(bf16[2,512,128]{2,1,0:T(8,128)(2,1)S(1)} %get-tuple-element.76), channel_id=1, source_target_pairs={{128,0},{0,128},{129,1},{1,129},{130,2},{2,130},{131,3},{3,131},{1... | collective-permute-start | bytes 786440 | tf_op jit(solution)/shard_map/ppermute | solution.py:31
  47.2 4.9 %collective-permute-start.17 = (bf16[2,512,128]{2,1,0:T(8,128)(2,1)S(1)}, bf16[2,512,128]{2,1,0:T(8,128)(2,1)S(1)}, u32[]{:S(2)}, u32[]{:S(2)}) collective-permute-start(bf16[2,512,128]{2,1,0:T(8,128)(2,1)S(1)} %get-tuple-element.89), channel_id=1, source_target_pairs={{128,0},{0,128},{129,1},{1,129},{130,2},{2,130},{131,3},{3,131},{1... | collective-permute-start | bytes 786440 | tf_op jit(solution)/shard_map/ppermute | solution.py:31
  47.6 15.6 %collective-permute-start.10 = (bf16[2,512,128]{2,1,0:T(8,128)(2,1)S(1)}, bf16[2,512,128]{2,1,0:T(8,128)(2,1)S(1)}, u32[]{:S(2)}, u32[]{:S(2)}) collective-permute-start(bf16[2,512,128]{2,1,0:T(8,128)(2,1)S(1)} %get-tuple-element.78), channel_id=1, source_target_pairs={{4,0},{8,4},{12,8},{0,12},{20,16},{24,20},{28,24},{16,28},{36,32},... | collective-permute-start | bytes 786440 | tf_op jit(solution)/shard_map/ppermute | solution.py:41
  48.2 15.0 %collective-permute-start.11 = (bf16[2,512,128]{2,1,0:T(8,128)(2,1)S(1)}, bf16[2,512,128]{2,1,0:T(8,128)(2,1)S(1)}, u32[]{:S(2)}, u32[]{:S(2)}) collective-permute-start(bf16[2,512,128]{2,1,0:T(8,128)(2,1)S(1)} %get-tuple-element.79), channel_id=1, source_target_pairs={{8,0},{12,4},{0,8},{4,12},{24,16},{28,20},{16,24},{20,28},{40,32},... | collective-permute-start | bytes 786440 | tf_op jit(solution)/shard_map/ppermute | solution.py:41
  49.8 14.1 %collective-permute-start.12 = (bf16[2,512,128]{2,1,0:T(8,128)(2,1)S(1)}, bf16[2,512,128]{2,1,0:T(8,128)(2,1)S(1)}, u32[]{:S(2)}, u32[]{:S(2)}) collective-permute-start(bf16[2,512,128]{2,1,0:T(8,128)(2,1)S(1)} %get-tuple-element.80), channel_id=1, source_target_pairs={{12,0},{0,4},{4,8},{8,12},{28,16},{16,20},{20,24},{24,28},{44,32},... | collective-permute-start | bytes 786440 | tf_op jit(solution)/shard_map/ppermute | solution.py:41
  58.9 5.2 %collective-permute-start.20 = (bf16[2,512,128]{2,1,0:T(8,128)(2,1)S(1)}, bf16[2,512,128]{2,1,0:T(8,128)(2,1)S(1)}, u32[]{:S(2)}, u32[]{:S(2)}) collective-permute-start(bf16[2,512,128]{2,1,0:T(8,128)(2,1)S(1)} %get-tuple-element.94), channel_id=1, source_target_pairs={{128,0},{0,128},{129,1},{1,129},{130,2},{2,130},{131,3},{3,131},{1... | collective-permute-start | bytes 786440 | tf_op jit(solution)/shard_map/ppermute | solution.py:31
  64.4 17.3 %collective-permute-start.23 = (bf16[2,512,128]{2,1,0:T(8,128)(2,1)S(1)}, bf16[2,512,128]{2,1,0:T(8,128)(2,1)S(1)}, u32[]{:S(2)}, u32[]{:S(2)}) collective-permute-start(bf16[2,512,128]{2,1,0:T(8,128)(2,1)S(1)} %get-tuple-element.102), channel_id=1, source_target_pairs={{12,0},{0,4},{4,8},{8,12},{28,16},{16,20},{20,24},{24,28},{44,32},... | collective-permute-start | bytes 786440 | tf_op jit(solution)/shard_map/ppermute | solution.py:41
  67.1 14.6 %collective-permute-start.22 = (bf16[2,512,128]{2,1,0:T(8,128)(2,1)S(1)}, bf16[2,512,128]{2,1,0:T(8,128)(2,1)S(1)}, u32[]{:S(2)}, u32[]{:S(2)}) collective-permute-start(bf16[2,512,128]{2,1,0:T(8,128)(2,1)S(1)} %get-tuple-element.100), channel_id=1, source_target_pairs={{8,0},{12,4},{0,8},{4,12},{24,16},{28,20},{16,24},{20,28},{40,32},... | collective-permute-start | bytes 786440 | tf_op jit(solution)/shard_map/ppermute | solution.py:41
  67.7 14.5 %collective-permute-start.21 = (bf16[2,512,128]{2,1,0:T(8,128)(2,1)S(1)}, bf16[2,512,128]{2,1,0:T(8,128)(2,1)S(1)}, u32[]{:S(2)}, u32[]{:S(2)}) collective-permute-start(bf16[2,512,128]{2,1,0:T(8,128)(2,1)S(1)} %get-tuple-element.98), channel_id=1, source_target_pairs={{4,0},{8,4},{12,8},{0,12},{20,16},{24,20},{28,24},{16,28},{36,32},... | collective-permute-start | bytes 786440 | tf_op jit(solution)/shard_map/ppermute | solution.py:41
  68.1 12.2 %collective-permute-start.18 = (bf16[64,1792]{1,0:T(8,128)(2,1)S(1)}, bf16[64,1792]{1,0:T(8,128)(2,1)S(1)}, u32[]{:S(2)}, u32[]{:S(2)}) collective-permute-start(bf16[64,1792]{1,0:T(8,128)(2,1)S(1)} %get-tuple-element.91), channel_id=1, source_target_pairs={{1,0},{2,1},{3,2},{0,3},{5,4},{6,5},{7,6},{4,7},{9,8},{10,9},{11,1... | collective-permute-start | bytes 688136 | tf_op jit(solution)/shard_map/ppermute | solution.py:31
  70.9 11.6 %collective-permute-start.24 = (bf16[64,1792]{1,0:T(8,128)(2,1)S(1)}, bf16[64,1792]{1,0:T(8,128)(2,1)S(1)}, u32[]{:S(2)}, u32[]{:S(2)}) collective-permute-start(bf16[64,1792]{1,0:T(8,128)(2,1)S(1)} %get-tuple-element.103), channel_id=1, source_target_pairs={{2,0},{3,1},{0,2},{1,3},{6,4},{7,5},{4,6},{5,7},{10,8},{11,9},{8,1... | collective-permute-start | bytes 688136 | tf_op jit(solution)/shard_map/ppermute | solution.py:31
  80.3 7.9 %collective-permute-start.19 = (bf16[2,512,128]{2,1,0:T(8,128)(2,1)S(1)}, bf16[2,512,128]{2,1,0:T(8,128)(2,1)S(1)}, u32[]{:S(2)}, u32[]{:S(2)}) collective-permute-start(bf16[2,512,128]{2,1,0:T(8,128)(2,1)S(1)} %get-tuple-element.92), channel_id=1, source_target_pairs={{16,0},{20,4},{24,8},{28,12},{32,16},{36,20},{40,24},{44,28},{48,3... | collective-permute-start | bytes 786440 | tf_op jit(solution)/shard_map/ppermute | solution.py:31
  82.4 9.8 %collective-permute-start.25 = (bf16[2,512,128]{2,1,0:T(8,128)(2,1)S(1)}, bf16[2,512,128]{2,1,0:T(8,128)(2,1)S(1)}, u32[]{:S(2)}, u32[]{:S(2)}) collective-permute-start(bf16[2,512,128]{2,1,0:T(8,128)(2,1)S(1)} %get-tuple-element.104), channel_id=1, source_target_pairs={{16,0},{20,4},{24,8},{28,12},{32,16},{36,20},{40,24},{44,28},{48,3... | collective-permute-start | bytes 786440 | tf_op jit(solution)/shard_map/ppermute | solution.py:31
  83.9 9.2 %collective-permute-start.26 = (bf16[64,1792]{1,0:T(8,128)(2,1)S(1)}, bf16[64,1792]{1,0:T(8,128)(2,1)S(1)}, u32[]{:S(2)}, u32[]{:S(2)}) collective-permute-start(bf16[64,1792]{1,0:T(8,128)(2,1)S(1)} %get-tuple-element.108), channel_id=1, source_target_pairs={{3,0},{0,1},{1,2},{2,3},{7,4},{4,5},{5,6},{6,7},{11,8},{8,9},{9,10... | collective-permute-start | bytes 688136 | tf_op jit(solution)/shard_map/ppermute | solution.py:31

commit v7 on v5

--- a/solution.py
+++ b/solution.py
@@ -346,7 +346,7 @@
     offers = []
     for c in range(CHUNKS):
         offer = {0: halves[c]}
-        for offset in (1, 3, 2):
+        for offset in (2, 1, 3):
             send = sends[c][offset - 1]
             if c:
                 send = after(send, offers[c - 1][offset])
@@ -373,7 +373,7 @@
             )
             terms.append(term if offset == 0 else term.astype(bf16))
         terms = lax.optimization_barrier(terms)
-        for offset in (1, 3, 2):
+        for offset in (2, 1, 3):
             term = after(terms[offset], ringed[offset]) if c else terms[offset]
             ringed[offset] = along_row(term, -offset)
         kept, passed = terms[0], jnp.zeros(part.shape, f32)

time: 94.9 us -> 94.9 us (level)
  no operation moved by 1% of the time
where the time goes in v7:
time: 94.9 us; the launch traced here: 94.7 us
  waiting for transfers between devices  35.8 us (38%)
  starting transfers between devices  32.6 us (34%)
  Pallas kernels  17.6 us (19%)
  between operations  4.34 us (5%)
  local copies, waits for them, and re-layouts  2.96 us (3%)
  other arithmetic  1.31 us (1%)
    ppermute x12, waiting for transfers between devices, along_row(): return lax.ppermute(block, 'group', route)  21.6 us
    ppermute x15, starting transfers between devices, shifted(): return lax.ppermute(block, axis, route)  18.7 us
    ppermute x15, waiting for transfers between devices, shifted(): return lax.ppermute(block, axis, route)  14.2 us
    ppermute x12, starting transfers between devices, along_row(): return lax.ppermute(block, 'group', route)  13.9 us
    pallas_call x2, Pallas kernels, attend(): pl.pallas_call(functools.partial(attend_kernel, chunk, tp_count), out_sha...  13.7 us
    unnamed x12, local copies, waits for them, and re-layouts  2.96 us
  transfers between devices with their start and end apart: 27, of which 13 were waited for; matrix products, arithmetic and copies ran while one was open for 1% of the time, Pallas kernels for 17%

profile of v7, /device:TPU:24, one launch (start us, length us, event | category | flops | bytes accessed | tf_op | source)
XLA Modules:
  0.0 94.7 jit_solution(9449248900878028070)
XLA Ops:
  0.6 1.2 %copy-done = bf16[1,2,1024,256]{3,2,1,0:T(8,128)(2,1)S(1)} copy-done((bf16[1,2,1024,256]{3,2,1,0:T(8,128)(2,1)S(1)}, bf16[1,2,1024,256]{3,2,1,0:T(8,128)(2,1)}, u32[]{:S(2)}) %copy-start) | copy-done | bytes 1048600
  2.0 2.0 %collective-permute-start.4 = (bf16[2,512,128]{2,1,0:T(8,128)(2,1)S(1)}, bf16[2,512,128]{2,1,0:T(8,128)(2,1)S(1)}, u32[]{:S(2)}, u32[]{:S(2)}) collective-permute-start(bf16[2,512,128]{2,1,0:T(8,128)(2,1)S(1)} %get-tuple-element.58.refs_0_), channel_id=1, source_target_pairs={{112,0},{116,4},{120,8},{124,12},{0,16},{4,20},{8,24},{12,28},{16,... | collective-permute-start | bytes 786440 | tf_op jit(solution)/shard_map/ppermute | solution.py:31
  4.6 0.6 copy-done.5
  5.4 1.1 %copy-done.2 = bf16[64,5120]{1,0:T(8,128)(2,1)S(1)} copy-done((bf16[64,5120]{1,0:T(8,128)(2,1)S(1)}, bf16[64,5120]{1,0:T(8,128)(2,1)}, u32[]{:S(2)}) %copy-start.2) | copy-done | bytes 655384
  6.5 0.7 pack.1
  7.2 1.6 %collective-permute-start.1 = (bf16[64,3072]{1,0:T(8,128)(2,1)S(1)}, bf16[64,3072]{1,0:T(8,128)(2,1)S(1)}, u32[]{:S(2)}, u32[]{:S(2)}) collective-permute-start(bf16[64,3072]{1,0:T(8,128)(2,1)S(1)} %get-tuple-element.63), channel_id=1, source_target_pairs={{3,0},{0,1},{1,2},{2,3},{7,4},{4,5},{5,6},{6,7},{11,8},{8,9},{9,10... | collective-permute-start | bytes 1179656 | tf_op jit(solution)/shard_map/ppermute | solution.py:31
  8.7 1.7 %collective-permute-start.2 = (bf16[64,3072]{1,0:T(8,128)(2,1)S(1)}, bf16[64,3072]{1,0:T(8,128)(2,1)S(1)}, u32[]{:S(2)}, u32[]{:S(2)}) collective-permute-start(bf16[64,3072]{1,0:T(8,128)(2,1)S(1)} %get-tuple-element.65), channel_id=1, source_target_pairs={{1,0},{2,1},{3,2},{0,3},{5,4},{6,5},{7,6},{4,7},{9,8},{10,9},{11,1... | collective-permute-start | bytes 1179656 | tf_op jit(solution)/shard_map/ppermute | solution.py:31
  10.5 3.7 %collective-permute-done.4 = bf16[2,512,128]{2,1,0:T(8,128)(2,1)S(1)} collective-permute-done((bf16[2,512,128]{2,1,0:T(8,128)(2,1)S(1)}, bf16[2,512,128]{2,1,0:T(8,128)(2,1)S(1)}, u32[]{:S(2)}, u32[]{:S(2)}) %collective-permute-start.4) | collective-permute-done | bytes 262176 | tf_op jit(solution)/shard_map/ppermute | solution.py:31
  14.3 0.3 collective-permute-start.5
  14.6 2.6 %collective-permute-start.6 = (bf16[2,512,128]{2,1,0:T(8,128)(2,1)S(1)}, bf16[2,512,128]{2,1,0:T(8,128)(2,1)S(1)}, u32[]{:S(2)}, u32[]{:S(2)}) collective-permute-start(bf16[2,512,128]{2,1,0:T(8,128)(2,1)S(1)} %get-tuple-element.71), channel_id=1, source_target_pairs={{8,0},{12,4},{0,8},{4,12},{24,16},{28,20},{16,24},{20,28},{40,32},... | collective-permute-start | bytes 786440 | tf_op jit(solution)/shard_map/ppermute | solution.py:41
  17.2 2.8 %collective-permute-done.1.refs_1_ = bf16[64,3072]{1,0:T(8,128)(2,1)S(1)} collective-permute-done((bf16[64,3072]{1,0:T(8,128)(2,1)S(1)}, bf16[64,3072]{1,0:T(8,128)(2,1)S(1)}, u32[]{:S(2)}, u32[]{:S(2)}) %collective-permute-start.1) | collective-permute-done | bytes 393248 | tf_op jit(solution)/shard_map/ppermute | solution.py:31
  20.0 1.9 %collective-permute-start.14 = (bf16[2,512,128]{2,1,0:T(8,128)(2,1)S(1)}, bf16[2,512,128]{2,1,0:T(8,128)(2,1)S(1)}, u32[]{:S(2)}, u32[]{:S(2)}) collective-permute-start(bf16[2,512,128]{2,1,0:T(8,128)(2,1)S(1)} %get-tuple-element.59.refs_0_), channel_id=1, source_target_pairs={{112,0},{116,4},{120,8},{124,12},{0,16},{4,20},{8,24},{12,28},{16,... | collective-permute-start | bytes 786440 | tf_op jit(solution)/shard_map/ppermute | solution.py:31
  21.9 1.8 %collective-permute-start.3 = (bf16[64,3072]{1,0:T(8,128)(2,1)S(1)}, bf16[64,3072]{1,0:T(8,128)(2,1)S(1)}, u32[]{:S(2)}, u32[]{:S(2)}) collective-permute-start(bf16[64,3072]{1,0:T(8,128)(2,1)S(1)} %get-tuple-element.66), channel_id=1, source_target_pairs={{2,0},{3,1},{0,2},{1,3},{6,4},{7,5},{4,6},{5,7},{10,8},{11,9},{8,1... | collective-permute-start | bytes 1179656 | tf_op jit(solution)/shard_map/ppermute | solution.py:31
  24.4 1.0 %collective-permute-done.6.refs_2_ = bf16[2,512,128]{2,1,0:T(8,128)(2,1)S(1)} collective-permute-done((bf16[2,512,128]{2,1,0:T(8,128)(2,1)S(1)}, bf16[2,512,128]{2,1,0:T(8,128)(2,1)S(1)}, u32[]{:S(2)}, u32[]{:S(2)}) %collective-permute-start.6) | collective-permute-done | bytes 262176 | tf_op jit(solution)/shard_map/ppermute | solution.py:41
  25.4 3.7 %collective-permute-done.7.refs_3_ = bf16[2,512,128]{2,1,0:T(8,128)(2,1)S(1)} collective-permute-done((bf16[2,512,128]{2,1,0:T(8,128)(2,1)S(1)}, bf16[2,512,128]{2,1,0:T(8,128)(2,1)S(1)}, u32[]{:S(2)}, u32[]{:S(2)}) %collective-permute-start.7) | collective-permute-done | bytes 262176 | tf_op jit(solution)/shard_map/ppermute | solution.py:41
  29.1 0.6 pick.2
  29.8 0.4 collective-permute-done.14
  30.3 0.8 collective-permute-start.15
  31.0 2.1 %collective-permute-start.16 = (bf16[2,512,128]{2,1,0:T(8,128)(2,1)S(1)}, bf16[2,512,128]{2,1,0:T(8,128)(2,1)S(1)}, u32[]{:S(2)}, u32[]{:S(2)}) collective-permute-start(bf16[2,512,128]{2,1,0:T(8,128)(2,1)S(1)} %get-tuple-element.86), channel_id=1, source_target_pairs={{8,0},{12,4},{0,8},{4,12},{24,16},{28,20},{16,24},{20,28},{40,32},... | collective-permute-start | bytes 786440 | tf_op jit(solution)/shard_map/ppermute | solution.py:41
  33.2 0.7 collective-permute-done.3.refs_2_
  33.9 6.8 %attend.2 = (bf16[64,896]{1,0:T(8,128)(2,1)S(1)}, bf16[64,896]{1,0:T(8,128)(2,1)S(1)}, bf16[64,896]{1,0:T(8,128)(2,1)S(1)}, bf16[64,896]{1,0:T(8,128)(2,1)S(1)},...) custom-call(s32[11]{0:T(128)S(1)} %pad_add_fusion.meta, ...), custom_call_target="tpu_custom_call" | custom-call | flops 16777216000 | bytes 6291456 | tf_op jit(solution)/shard_map/attend/pallas_call | solution.py:274
  43.0 3.5 %collective-permute-done.17.refs_3_ = bf16[2,512,128]{2,1,0:T(8,128)(2,1)S(1)} collective-permute-done((bf16[2,512,128]{2,1,0:T(8,128)(2,1)S(1)}, bf16[2,512,128]{2,1,0:T(8,128)(2,1)S(1)}, u32[]{:S(2)}, u32[]{:S(2)}) %collective-permute-start.17) | collective-permute-done | bytes 262176 | tf_op jit(solution)/shard_map/ppermute | solution.py:41
  46.6 0.6 pick.3
  47.2 0.1 collective-permute-start.18
  47.3 0.3 fusion.18
  47.6 0.6 collective-permute-start.10
  48.2 1.6 %collective-permute-start.11 = (bf16[2,512,128]{2,1,0:T(8,128)(2,1)S(1)}, bf16[2,512,128]{2,1,0:T(8,128)(2,1)S(1)}, u32[]{:S(2)}, u32[]{:S(2)}) collective-permute-start(bf16[2,512,128]{2,1,0:T(8,128)(2,1)S(1)} %get-tuple-element.79), channel_id=1, source_target_pairs={{8,0},{12,4},{0,8},{4,12},{24,16},{28,20},{16,24},{20,28},{40,32},... | collective-permute-start | bytes 786440 | tf_op jit(solution)/shard_map/ppermute | solution.py:41
  49.8 2.3 %collective-permute-start.12 = (bf16[2,512,128]{2,1,0:T(8,128)(2,1)S(1)}, bf16[2,512,128]{2,1,0:T(8,128)(2,1)S(1)}, u32[]{:S(2)}, u32[]{:S(2)}) collective-permute-start(bf16[2,512,128]{2,1,0:T(8,128)(2,1)S(1)} %get-tuple-element.80), channel_id=1, source_target_pairs={{12,0},{0,4},{4,8},{8,12},{28,16},{16,20},{20,24},{24,28},{44,32},... | collective-permute-start | bytes 786440 | tf_op jit(solution)/shard_map/ppermute | solution.py:41
  52.1 6.9 %attend.3 = (bf16[64,1792]{1,0:T(8,128)(2,1)S(1)}, bf16[64,1792]{1,0:T(8,128)(2,1)S(1)}, bf16[64,1792]{1,0:T(8,128)(2,1)S(1)}, bf16[64,1792]{1,0:T(8,128)(2,1)S(...) custom-call(s32[11]{0:T(128)S(1)} %pad_add_fusion.meta, ...), custom_call_target="tpu_custom_call" | custom-call | flops 16777216000 | bytes 6291456 | tf_op jit(solution)/shard_map/attend/pallas_call | solution.py:274
  59.0 4.2 %collective-permute-done.10 = bf16[2,512,128]{2,1,0:T(8,128)(2,1)S(1)} collective-permute-done((bf16[2,512,128]{2,1,0:T(8,128)(2,1)S(1)}, bf16[2,512,128]{2,1,0:T(8,128)(2,1)S(1)}, u32[]{:S(2)}, u32[]{:S(2)}) %collective-permute-start.10) | collective-permute-done | bytes 262176 | tf_op jit(solution)/shard_map/ppermute | solution.py:41
  63.2 0.6 collective-permute-done.12
  63.8 0.3 fusion.5
  64.1 1.5 %collective-permute-start.13 = (bf16[2,512,128]{2,1,0:T(8,128)(2,1)S(1)}, bf16[2,512,128]{2,1,0:T(8,128)(2,1)S(1)}, u32[]{:S(2)}, u32[]{:S(2)}) collective-permute-start(bf16[2,512,128]{2,1,0:T(8,128)(2,1)S(1)} %get-tuple-element.114), channel_id=1, source_target_pairs={{16,0},{20,4},{24,8},{28,12},{32,16},{36,20},{40,24},{44,28},{48,3... | collective-permute-start | bytes 786440 | tf_op jit(solution)/shard_map/ppermute | solution.py:31
  65.6 0.3 fusion.25
  65.9 2.7 %collective-permute-start.22 = (bf16[2,512,128]{2,1,0:T(8,128)(2,1)S(1)}, bf16[2,512,128]{2,1,0:T(8,128)(2,1)S(1)}, u32[]{:S(2)}, u32[]{:S(2)}) collective-permute-start(bf16[2,512,128]{2,1,0:T(8,128)(2,1)S(1)} %get-tuple-element.100), channel_id=1, source_target_pairs={{12,0},{0,4},{4,8},{8,12},{28,16},{16,20},{20,24},{24,28},{44,32},... | collective-permute-start | bytes 786440 | tf_op jit(solution)/shard_map/ppermute | solution.py:41
  68.6 0.5 collective-permute-start.21
  69.2 0.4 collective-permute-start.20
  69.6 2.7 %collective-permute-start.23 = (bf16[64,1792]{1,0:T(8,128)(2,1)S(1)}, bf16[64,1792]{1,0:T(8,128)(2,1)S(1)}, u32[]{:S(2)}, u32[]{:S(2)}) collective-permute-start(bf16[64,1792]{1,0:T(8,128)(2,1)S(1)} %get-tuple-element.101), channel_id=1, source_target_pairs={{1,0},{2,1},{3,2},{0,3},{5,4},{6,5},{7,6},{4,7},{9,8},{10,9},{11,1... | collective-permute-start | bytes 688136 | tf_op jit(solution)/shard_map/ppermute | solution.py:31
  72.3 2.5 %collective-permute-start.24 = (bf16[64,1792]{1,0:T(8,128)(2,1)S(1)}, bf16[64,1792]{1,0:T(8,128)(2,1)S(1)}, u32[]{:S(2)}, u32[]{:S(2)}) collective-permute-start(bf16[64,1792]{1,0:T(8,128)(2,1)S(1)} %get-tuple-element.103), channel_id=1, source_target_pairs={{2,0},{3,1},{0,2},{1,3},{6,4},{7,5},{4,6},{5,7},{10,8},{11,9},{8,1... | collective-permute-start | bytes 688136 | tf_op jit(solution)/shard_map/ppermute | solution.py:31
  74.8 4.9 %collective-permute-done.22 = bf16[2,512,128]{2,1,0:T(8,128)(2,1)S(1)} collective-permute-done((bf16[2,512,128]{2,1,0:T(8,128)(2,1)S(1)}, bf16[2,512,128]{2,1,0:T(8,128)(2,1)S(1)}, u32[]{:S(2)}, u32[]{:S(2)}) %collective-permute-start.22) | collective-permute-done | bytes 262176 | tf_op jit(solution)/shard_map/ppermute | solution.py:41
  79.7 3.7 %collective-permute-done.20 = bf16[2,512,128]{2,1,0:T(8,128)(2,1)S(1)} collective-permute-done((bf16[2,512,128]{2,1,0:T(8,128)(2,1)S(1)}, bf16[2,512,128]{2,1,0:T(8,128)(2,1)S(1)}, u32[]{:S(2)}, u32[]{:S(2)}) %collective-permute-start.20) | collective-permute-done | bytes 262176 | tf_op jit(solution)/shard_map/ppermute | solution.py:41
  83.4 0.3 fusion.11
  83.7 1.6 %collective-permute-start.25 = (bf16[2,512,128]{2,1,0:T(8,128)(2,1)S(1)}, bf16[2,512,128]{2,1,0:T(8,128)(2,1)S(1)}, u32[]{:S(2)}, u32[]{:S(2)}) collective-permute-start(bf16[2,512,128]{2,1,0:T(8,128)(2,1)S(1)} %get-tuple-element.104), channel_id=1, source_target_pairs={{16,0},{20,4},{24,8},{28,12},{32,16},{36,20},{40,24},{44,28},{48,3... | collective-permute-start | bytes 786440 | tf_op jit(solution)/shard_map/ppermute | solution.py:31
  85.2 1.0 %collective-permute-start.26 = (bf16[64,1792]{1,0:T(8,128)(2,1)S(1)}, bf16[64,1792]{1,0:T(8,128)(2,1)S(1)}, u32[]{:S(2)}, u32[]{:S(2)}) collective-permute-start(bf16[64,1792]{1,0:T(8,128)(2,1)S(1)} %get-tuple-element.108), channel_id=1, source_target_pairs={{3,0},{0,1},{1,2},{2,3},{7,4},{4,5},{5,6},{6,7},{11,8},{8,9},{9,10... | collective-permute-start | bytes 688136 | tf_op jit(solution)/shard_map/ppermute | solution.py:31
  86.2 5.7 %collective-permute-done.25.refs_3_ = bf16[2,512,128]{2,1,0:T(8,128)(2,1)S(1)} collective-permute-done((bf16[2,512,128]{2,1,0:T(8,128)(2,1)S(1)}, bf16[2,512,128]{2,1,0:T(8,128)(2,1)S(1)}, u32[]{:S(2)}, u32[]{:S(2)}) %collective-permute-start.25) | collective-permute-done | bytes 262176 | tf_op jit(solution)/shard_map/ppermute | solution.py:31
  91.9 0.9 finish.1
  92.8 0.8 collective-permute-done.26.refs_3_
  93.7 1.0 %unpack.1 = (bf16[64,5120]{1,0:T(8,128)(2,1)}, bf16[64,1024]{1,0:T(8,128)(2,1)}, bf16[64,1024]{1,0:T(8,128)(2,1)}) custom-call(s32[1]{0:T(128)} %bitcast.tp, bf16[64,1792]{1,0:T(8,128)(2,1)S(1)} %get-tuple-element.106.refs_0_, bf16[64,1792]{1,0:T(8,128)(2,1)S(1)} %collective-permute-done.23.refs_1_, bf16[64,1792]{1,0:T(8,128)(2,1)S(1)} %collective-permute-done.24.refs_2_, ...), custom_call_target="tpu_custom_call" | custom-call | tf_op jit(solution)/shard_map/unpack/pallas_call | solution.py:397
  (33 shorter events, 0.6 us)
Async XLA Ops:
  0.6 1.2 %copy-start = (bf16[1,2,1024,256]{3,2,1,0:T(8,128)(2,1)S(1)}, bf16[1,2,1024,256]{3,2,1,0:T(8,128)(2,1)}, u32[]{:S(2)}) copy-start(bf16[1,2,1024,256]{3,2,1,0:T(8,128)(2,1)} %prompt.1) | copy-start | bytes 3145732
  1.9 3.5 %copy-start.1 = (bf16[64,5120]{1,0:T(8,128)(2,1)S(1)}, bf16[64,5120]{1,0:T(8,128)(2,1)}, u32[]{:S(2)}) copy-start(bf16[64,5120]{1,0:T(8,128)(2,1)} %queries.1) | copy-start | bytes 1966084
  1.9 3.5 %copy-start.3 = (bf16[64,1024]{1,0:T(8,128)(2,1)S(1)}, bf16[64,1024]{1,0:T(8,128)(2,1)}, u32[]{:S(2)}) copy-start(bf16[64,1024]{1,0:T(8,128)(2,1)} %keys.1) | copy-start | bytes 393220
  1.9 3.5 %copy-start.4 = (bf16[64,1024]{1,0:T(8,128)(2,1)S(1)}, bf16[64,1024]{1,0:T(8,128)(2,1)}, u32[]{:S(2)}) copy-start(bf16[64,1024]{1,0:T(8,128)(2,1)} %values.1) | copy-start | bytes 393220
  2.0 12.2 %collective-permute-start.4 = (bf16[2,512,128]{2,1,0:T(8,128)(2,1)S(1)}, bf16[2,512,128]{2,1,0:T(8,128)(2,1)S(1)}, u32[]{:S(2)}, u32[]{:S(2)}) collective-permute-start(bf16[2,512,128]{2,1,0:T(8,128)(2,1)S(1)} %get-tuple-element.58.refs_0_), channel_id=1, source_target_pairs={{112,0},{116,4},{120,8},{124,12},{0,16},{4,20},{8,24},{12,28},{16,... | collective-permute-start | bytes 786440 | tf_op jit(solution)/shard_map/ppermute | solution.py:31
  4.0 1.4 %collective-permute-start = (s32[1]{0:T(128)}, s32[1]{0:T(128)}, u32[]{:S(2)}, u32[]{:S(2)}) collective-permute-start(s32[1]{0:T(128)} %param.14), channel_id=1, source_target_pairs={{128,0},{0,128},{129,1},{1,129},{130,2},{2,130},{131,3},{3,131},{1... | collective-permute-start | bytes 20 | tf_op jit(solution)/shard_map/ppermute | solution.py:31
  4.6 0.7 copy-start.5
  5.4 1.1 %copy-start.2 = (bf16[64,5120]{1,0:T(8,128)(2,1)S(1)}, bf16[64,5120]{1,0:T(8,128)(2,1)}, u32[]{:S(2)}) copy-start(bf16[64,5120]{1,0:T(8,128)(2,1)} %grad_out.1) | copy-start | bytes 1966084
  7.2 12.8 %collective-permute-start.1 = (bf16[64,3072]{1,0:T(8,128)(2,1)S(1)}, bf16[64,3072]{1,0:T(8,128)(2,1)S(1)}, u32[]{:S(2)}, u32[]{:S(2)}) collective-permute-start(bf16[64,3072]{1,0:T(8,128)(2,1)S(1)} %get-tuple-element.63), channel_id=1, source_target_pairs={{3,0},{0,1},{1,2},{2,3},{7,4},{4,5},{5,6},{6,7},{11,8},{8,9},{9,10... | collective-permute-start | bytes 1179656 | tf_op jit(solution)/shard_map/ppermute | solution.py:31
  8.7 13.2 %collective-permute-start.2 = (bf16[64,3072]{1,0:T(8,128)(2,1)S(1)}, bf16[64,3072]{1,0:T(8,128)(2,1)S(1)}, u32[]{:S(2)}, u32[]{:S(2)}) collective-permute-start(bf16[64,3072]{1,0:T(8,128)(2,1)S(1)} %get-tuple-element.65), channel_id=1, source_target_pairs={{1,0},{2,1},{3,2},{0,3},{5,4},{6,5},{7,6},{4,7},{9,8},{10,9},{11,1... | collective-permute-start | bytes 1179656 | tf_op jit(solution)/shard_map/ppermute | solution.py:31
  14.3 10.1 %collective-permute-start.5 = (bf16[2,512,128]{2,1,0:T(8,128)(2,1)S(1)}, bf16[2,512,128]{2,1,0:T(8,128)(2,1)S(1)}, u32[]{:S(2)}, u32[]{:S(2)}) collective-permute-start(bf16[2,512,128]{2,1,0:T(8,128)(2,1)S(1)} %get-tuple-element.70), channel_id=1, source_target_pairs={{12,0},{0,4},{4,8},{8,12},{28,16},{16,20},{20,24},{24,28},{44,32},... | collective-permute-start | bytes 786440 | tf_op jit(solution)/shard_map/ppermute | solution.py:41
  14.6 10.8 %collective-permute-start.6 = (bf16[2,512,128]{2,1,0:T(8,128)(2,1)S(1)}, bf16[2,512,128]{2,1,0:T(8,128)(2,1)S(1)}, u32[]{:S(2)}, u32[]{:S(2)}) collective-permute-start(bf16[2,512,128]{2,1,0:T(8,128)(2,1)S(1)} %get-tuple-element.71), channel_id=1, source_target_pairs={{8,0},{12,4},{0,8},{4,12},{24,16},{28,20},{16,24},{20,28},{40,32},... | collective-permute-start | bytes 786440 | tf_op jit(solution)/shard_map/ppermute | solution.py:41
  17.2 11.9 %collective-permute-start.7 = (bf16[2,512,128]{2,1,0:T(8,128)(2,1)S(1)}, bf16[2,512,128]{2,1,0:T(8,128)(2,1)S(1)}, u32[]{:S(2)}, u32[]{:S(2)}) collective-permute-start(bf16[2,512,128]{2,1,0:T(8,128)(2,1)S(1)} %get-tuple-element.72), channel_id=1, source_target_pairs={{4,0},{8,4},{12,8},{0,12},{20,16},{24,20},{28,24},{16,28},{36,32},... | collective-permute-start | bytes 786440 | tf_op jit(solution)/shard_map/ppermute | solution.py:41
  20.0 10.2 %collective-permute-start.14 = (bf16[2,512,128]{2,1,0:T(8,128)(2,1)S(1)}, bf16[2,512,128]{2,1,0:T(8,128)(2,1)S(1)}, u32[]{:S(2)}, u32[]{:S(2)}) collective-permute-start(bf16[2,512,128]{2,1,0:T(8,128)(2,1)S(1)} %get-tuple-element.59.refs_0_), channel_id=1, source_target_pairs={{112,0},{116,4},{120,8},{124,12},{0,16},{4,20},{8,24},{12,28},{16,... | collective-permute-start | bytes 786440 | tf_op jit(solution)/shard_map/ppermute | solution.py:31
  21.9 12.0 %collective-permute-start.3 = (bf16[64,3072]{1,0:T(8,128)(2,1)S(1)}, bf16[64,3072]{1,0:T(8,128)(2,1)S(1)}, u32[]{:S(2)}, u32[]{:S(2)}) collective-permute-start(bf16[64,3072]{1,0:T(8,128)(2,1)S(1)} %get-tuple-element.66), channel_id=1, source_target_pairs={{2,0},{3,1},{0,2},{1,3},{6,4},{7,5},{4,6},{5,7},{10,8},{11,9},{8,1... | collective-permute-start | bytes 1179656 | tf_op jit(solution)/shard_map/ppermute | solution.py:31
  29.7 3.5 %collective-permute-start.8 = (bf16[2,512,128]{2,1,0:T(8,128)(2,1)S(1)}, bf16[2,512,128]{2,1,0:T(8,128)(2,1)S(1)}, u32[]{:S(2)}, u32[]{:S(2)}) collective-permute-start(bf16[2,512,128]{2,1,0:T(8,128)(2,1)S(1)} %get-tuple-element.74), channel_id=1, source_target_pairs={{128,0},{0,128},{129,1},{1,129},{130,2},{2,130},{131,3},{3,131},{1... | collective-permute-start | bytes 786440 | tf_op jit(solution)/shard_map/ppermute | solution.py:31
  30.3 12.7 %collective-permute-start.15 = (bf16[2,512,128]{2,1,0:T(8,128)(2,1)S(1)}, bf16[2,512,128]{2,1,0:T(8,128)(2,1)S(1)}, u32[]{:S(2)}, u32[]{:S(2)}) collective-permute-start(bf16[2,512,128]{2,1,0:T(8,128)(2,1)S(1)} %get-tuple-element.85), channel_id=1, source_target_pairs={{12,0},{0,4},{4,8},{8,12},{28,16},{16,20},{20,24},{24,28},{44,32},... | collective-permute-start | bytes 786440 | tf_op jit(solution)/shard_map/ppermute | solution.py:41
  31.0 12.0 %collective-permute-start.16 = (bf16[2,512,128]{2,1,0:T(8,128)(2,1)S(1)}, bf16[2,512,128]{2,1,0:T(8,128)(2,1)S(1)}, u32[]{:S(2)}, u32[]{:S(2)}) collective-permute-start(bf16[2,512,128]{2,1,0:T(8,128)(2,1)S(1)} %get-tuple-element.86), channel_id=1, source_target_pairs={{8,0},{12,4},{0,8},{4,12},{24,16},{28,20},{16,24},{20,28},{40,32},... | collective-permute-start | bytes 786440 | tf_op jit(solution)/shard_map/ppermute | solution.py:41
  33.2 13.4 %collective-permute-start.17 = (bf16[2,512,128]{2,1,0:T(8,128)(2,1)S(1)}, bf16[2,512,128]{2,1,0:T(8,128)(2,1)S(1)}, u32[]{:S(2)}, u32[]{:S(2)}) collective-permute-start(bf16[2,512,128]{2,1,0:T(8,128)(2,1)S(1)} %get-tuple-element.87), channel_id=1, source_target_pairs={{4,0},{8,4},{12,8},{0,12},{20,16},{24,20},{28,24},{16,28},{36,32},... | collective-permute-start | bytes 786440 | tf_op jit(solution)/shard_map/ppermute | solution.py:41
  40.7 6.6 %collective-permute-start.9 = (bf16[2,512,128]{2,1,0:T(8,128)(2,1)S(1)}, bf16[2,512,128]{2,1,0:T(8,128)(2,1)S(1)}, u32[]{:S(2)}, u32[]{:S(2)}) collective-permute-start(bf16[2,512,128]{2,1,0:T(8,128)(2,1)S(1)} %get-tuple-element.76), channel_id=1, source_target_pairs={{128,0},{0,128},{129,1},{1,129},{130,2},{2,130},{131,3},{3,131},{1... | collective-permute-start | bytes 786440 | tf_op jit(solution)/shard_map/ppermute | solution.py:31
  47.2 4.9 %collective-permute-start.18 = (bf16[2,512,128]{2,1,0:T(8,128)(2,1)S(1)}, bf16[2,512,128]{2,1,0:T(8,128)(2,1)S(1)}, u32[]{:S(2)}, u32[]{:S(2)}) collective-permute-start(bf16[2,512,128]{2,1,0:T(8,128)(2,1)S(1)} %get-tuple-element.89), channel_id=1, source_target_pairs={{128,0},{0,128},{129,1},{1,129},{130,2},{2,130},{131,3},{3,131},{1... | collective-permute-start | bytes 786440 | tf_op jit(solution)/shard_map/ppermute | solution.py:31
  47.6 15.6 %collective-permute-start.10 = (bf16[2,512,128]{2,1,0:T(8,128)(2,1)S(1)}, bf16[2,512,128]{2,1,0:T(8,128)(2,1)S(1)}, u32[]{:S(2)}, u32[]{:S(2)}) collective-permute-start(bf16[2,512,128]{2,1,0:T(8,128)(2,1)S(1)} %get-tuple-element.78), channel_id=1, source_target_pairs={{4,0},{8,4},{12,8},{0,12},{20,16},{24,20},{28,24},{16,28},{36,32},... | collective-permute-start | bytes 786440 | tf_op jit(solution)/shard_map/ppermute | solution.py:41
  48.2 15.0 %collective-permute-start.11 = (bf16[2,512,128]{2,1,0:T(8,128)(2,1)S(1)}, bf16[2,512,128]{2,1,0:T(8,128)(2,1)S(1)}, u32[]{:S(2)}, u32[]{:S(2)}) collective-permute-start(bf16[2,512,128]{2,1,0:T(8,128)(2,1)S(1)} %get-tuple-element.79), channel_id=1, source_target_pairs={{8,0},{12,4},{0,8},{4,12},{24,16},{28,20},{16,24},{20,28},{40,32},... | collective-permute-start | bytes 786440 | tf_op jit(solution)/shard_map/ppermute | solution.py:41
  49.8 14.1 %collective-permute-start.12 = (bf16[2,512,128]{2,1,0:T(8,128)(2,1)S(1)}, bf16[2,512,128]{2,1,0:T(8,128)(2,1)S(1)}, u32[]{:S(2)}, u32[]{:S(2)}) collective-permute-start(bf16[2,512,128]{2,1,0:T(8,128)(2,1)S(1)} %get-tuple-element.80), channel_id=1, source_target_pairs={{12,0},{0,4},{4,8},{8,12},{28,16},{16,20},{20,24},{24,28},{44,32},... | collective-permute-start | bytes 786440 | tf_op jit(solution)/shard_map/ppermute | solution.py:41
  58.9 6.7 %collective-permute-start.19 = (bf16[2,512,128]{2,1,0:T(8,128)(2,1)S(1)}, bf16[2,512,128]{2,1,0:T(8,128)(2,1)S(1)}, u32[]{:S(2)}, u32[]{:S(2)}) collective-permute-start(bf16[2,512,128]{2,1,0:T(8,128)(2,1)S(1)} %get-tuple-element.92), channel_id=1, source_target_pairs={{128,0},{0,128},{129,1},{1,129},{130,2},{2,130},{131,3},{3,131},{1... | collective-permute-start | bytes 786440 | tf_op jit(solution)/shard_map/ppermute | solution.py:31
  64.1 8.2 %collective-permute-start.13 = (bf16[2,512,128]{2,1,0:T(8,128)(2,1)S(1)}, bf16[2,512,128]{2,1,0:T(8,128)(2,1)S(1)}, u32[]{:S(2)}, u32[]{:S(2)}) collective-permute-start(bf16[2,512,128]{2,1,0:T(8,128)(2,1)S(1)} %get-tuple-element.114), channel_id=1, source_target_pairs={{16,0},{20,4},{24,8},{28,12},{32,16},{36,20},{40,24},{44,28},{48,3... | collective-permute-start | bytes 786440 | tf_op jit(solution)/shard_map/ppermute | solution.py:31
  65.9 13.8 %collective-permute-start.22 = (bf16[2,512,128]{2,1,0:T(8,128)(2,1)S(1)}, bf16[2,512,128]{2,1,0:T(8,128)(2,1)S(1)}, u32[]{:S(2)}, u32[]{:S(2)}) collective-permute-start(bf16[2,512,128]{2,1,0:T(8,128)(2,1)S(1)} %get-tuple-element.100), channel_id=1, source_target_pairs={{12,0},{0,4},{4,8},{8,12},{28,16},{16,20},{20,24},{24,28},{44,32},... | collective-permute-start | bytes 786440 | tf_op jit(solution)/shard_map/ppermute | solution.py:41
  68.6 11.1 %collective-permute-start.21 = (bf16[2,512,128]{2,1,0:T(8,128)(2,1)S(1)}, bf16[2,512,128]{2,1,0:T(8,128)(2,1)S(1)}, u32[]{:S(2)}, u32[]{:S(2)}) collective-permute-start(bf16[2,512,128]{2,1,0:T(8,128)(2,1)S(1)} %get-tuple-element.98), channel_id=1, source_target_pairs={{8,0},{12,4},{0,8},{4,12},{24,16},{28,20},{16,24},{20,28},{40,32},... | collective-permute-start | bytes 786440 | tf_op jit(solution)/shard_map/ppermute | solution.py:41
  69.2 14.2 %collective-permute-start.20 = (bf16[2,512,128]{2,1,0:T(8,128)(2,1)S(1)}, bf16[2,512,128]{2,1,0:T(8,128)(2,1)S(1)}, u32[]{:S(2)}, u32[]{:S(2)}) collective-permute-start(bf16[2,512,128]{2,1,0:T(8,128)(2,1)S(1)} %get-tuple-element.96), channel_id=1, source_target_pairs={{4,0},{8,4},{12,8},{0,12},{20,16},{24,20},{28,24},{16,28},{36,32},... | collective-permute-start | bytes 786440 | tf_op jit(solution)/shard_map/ppermute | solution.py:41
  69.6 14.1 %collective-permute-start.23 = (bf16[64,1792]{1,0:T(8,128)(2,1)S(1)}, bf16[64,1792]{1,0:T(8,128)(2,1)S(1)}, u32[]{:S(2)}, u32[]{:S(2)}) collective-permute-start(bf16[64,1792]{1,0:T(8,128)(2,1)S(1)} %get-tuple-element.101), channel_id=1, source_target_pairs={{1,0},{2,1},{3,2},{0,3},{5,4},{6,5},{7,6},{4,7},{9,8},{10,9},{11,1... | collective-permute-start | bytes 688136 | tf_op jit(solution)/shard_map/ppermute | solution.py:31
  72.3 11.3 %collective-permute-start.24 = (bf16[64,1792]{1,0:T(8,128)(2,1)S(1)}, bf16[64,1792]{1,0:T(8,128)(2,1)S(1)}, u32[]{:S(2)}, u32[]{:S(2)}) collective-permute-start(bf16[64,1792]{1,0:T(8,128)(2,1)S(1)} %get-tuple-element.103), channel_id=1, source_target_pairs={{2,0},{3,1},{0,2},{1,3},{6,4},{7,5},{4,6},{5,7},{10,8},{11,9},{8,1... | collective-permute-start | bytes 688136 | tf_op jit(solution)/shard_map/ppermute | solution.py:31
  83.7 8.3 %collective-permute-start.25 = (bf16[2,512,128]{2,1,0:T(8,128)(2,1)S(1)}, bf16[2,512,128]{2,1,0:T(8,128)(2,1)S(1)}, u32[]{:S(2)}, u32[]{:S(2)}) collective-permute-start(bf16[2,512,128]{2,1,0:T(8,128)(2,1)S(1)} %get-tuple-element.104), channel_id=1, source_target_pairs={{16,0},{20,4},{24,8},{28,12},{32,16},{36,20},{40,24},{44,28},{48,3... | collective-permute-start | bytes 786440 | tf_op jit(solution)/shard_map/ppermute | solution.py:31
  85.2 8.4 %collective-permute-start.26 = (bf16[64,1792]{1,0:T(8,128)(2,1)S(1)}, bf16[64,1792]{1,0:T(8,128)(2,1)S(1)}, u32[]{:S(2)}, u32[]{:S(2)}) collective-permute-start(bf16[64,1792]{1,0:T(8,128)(2,1)S(1)} %get-tuple-element.108), channel_id=1, source_target_pairs={{3,0},{0,1},{1,2},{2,3},{7,4},{4,5},{5,6},{6,7},{11,8},{8,9},{9,10... | collective-permute-start | bytes 688136 | tf_op jit(solution)/shard_map/ppermute | solution.py:31
